TPU v7x, 32 devices: a whole 2x2x4 slice. The times are simulated.
32 devices in a mesh: wide: 8 (over z, x), narrow: 4 (over y, core).
Axes of the slice: x: 2, y: 2, z: 4, core: 2. Of those that a mesh axis runs over, the one named last changes fastest.
Arguments:
- tokens: bfloat16 [2, 8, 1024, 1280], P(None, 'wide', 'narrow'), may hold values from -6 to 6
- cotangent: bfloat16 [2, 8, 1024, 1280], P(None, 'wide', 'narrow'), may hold values from -6 to 6
- cell_of: int32 [16], replicated, may hold values from 0 to 15, each once
- query_count: int32 [16], replicated, may hold values from 50 to 2000
- attn_norm_gain: bfloat16 [1280], replicated, may hold values from 0.25 to 1.75
- attn_norm_bias: bfloat16 [1280], replicated, may hold values from -1.5 to 1.5
- input_weight: bfloat16 [1280, 3, 1280], P(None, None, 'narrow'), may hold values from -0.15625 to 0.15625
- query_bias: bfloat16 [1280], P('narrow'), may hold values from -1.5 to 1.5
- value_bias: bfloat16 [1280], P('narrow'), may hold values from -0.25 to 0.25
- out_weight: bfloat16 [1280, 1280], P('narrow'), may hold values from -3.5 to 3.5
- out_bias: bfloat16 [1280], replicated, may hold values from -1 to 1
- ffn_norm_gain: bfloat16 [1280], replicated, may hold values from 0.25 to 1.75
- ffn_norm_bias: bfloat16 [1280], replicated, may hold values from -1.5 to 1.5
- up_weight: bfloat16 [1280, 5120], P(None, 'narrow'), may hold values from -0.15625 to 0.15625
- up_bias: bfloat16 [5120], P('narrow'), may hold values from -1.5 to 1.5
- down_weight: bfloat16 [5120, 1280], P('narrow'), may hold values from -0.078125 to 0.078125
- down_bias: bfloat16 [1280], replicated, may hold values from -1 to 1
Outputs:
- block_out: bfloat16 [2, 8, 1024, 1280], P(None, 'wide', 'narrow')
- tokens_grad: float32 [2, 8, 1024, 1280], P(None, 'wide', 'narrow')
- attn_norm_gain_grad: float32 [1280], replicated
- attn_norm_bias_grad: float32 [1280], replicated
- input_weight_grad: float32 [1280, 3, 1280], P(None, None, 'narrow')
- query_bias_grad: float32 [1280], P('narrow')
- value_bias_grad: float32 [1280], P('narrow')
- out_weight_grad: float32 [1280, 1280], P('narrow')
- out_bias_grad: float32 [1280], replicated
- ffn_norm_gain_grad: float32 [1280], replicated
- ffn_norm_bias_grad: float32 [1280], replicated
- up_weight_grad: float32 [1280, 5120], P(None, 'narrow')
- up_bias_grad: float32 [5120], P('narrow')
- down_weight_grad: float32 [5120, 1280], P('narrow')
- down_bias_grad: float32 [1280], replicated
Inputs may be any that keep to these rules, and one draw needn't show every extreme that they name: `cell_of`: each cell id stands in exactly one slot.
All inputs are finite; a program needn't handle non-finite values.
Results may differ from a plain program's by a relative error of at most 0.019.
Values may be sent and summed in bfloat16 or wider, within the bound.
No kernel may reach another device: no remote copies, remote signals or barrier semaphores. Data moves between devices by JAX's collectives and lax.ppermute only.
A program may use at most 192 MiB of HBM per device.

v0:
```python
import jax
import jax.numpy as jnp
from jax import lax
from jax.sharding import PartitionSpec as P

HEAD = 64


norm_eps = 1e-05
score_scale = 0.125


def layer_norm(values, gain_vec, bias_vec):
    average = jnp.mean(values, axis=-1, keepdims=True)
    centred = values - average
    variance = jnp.mean(centred * centred, axis=-1, keepdims=True)
    return centred * lax.rsqrt(variance + norm_eps) * gain_vec + bias_vec


def tree_add(first_tree, second_tree):
    return jax.tree.map(jnp.add, first_tree, second_tree)


def gelu_slope(values):
    cumul = 0.5 * (1.0 + lax.erf(values * 0.7071067811865476))
    density = jnp.exp(-0.5 * values * values) * 0.3989422804014327
    return cumul + values * density


def attend_forward(queries, key_rows, value_rows, block_rows):
    whole_rows, heads_here, head_dim = queries.shape
    blocks = whole_rows // block_rows
    query_blocks = queries.reshape(blocks, block_rows, heads_here, head_dim)

    def one_block(query_block):
        scores = (
            jnp.einsum("qhe,khe->hqk", query_block, key_rows, preferred_element_type=jnp.float32)
            * score_scale
        )
        top_val = jnp.max(scores, axis=-1, keepdims=True)
        exp_scores = jnp.exp(scores - top_val)
        totals = jnp.sum(exp_scores, axis=-1, keepdims=True)
        weights_bf = (exp_scores / totals).astype(jnp.bfloat16)
        mixed_rows = jnp.einsum(
            "hqk,khe->qhe", weights_bf, value_rows, preferred_element_type=jnp.float32
        )
        return (mixed_rows, top_val, totals)

    mixed_rows, top_vals, totals = lax.map(one_block, query_blocks)
    return (mixed_rows.reshape(whole_rows, heads_here * head_dim), top_vals, totals)


def attend_backward(queries, key_rows, value_rows, grad_out, top_vals, totals, block_rows):
    whole_rows, heads_here, head_dim = queries.shape
    blocks = whole_rows // block_rows
    query_blocks = queries.reshape(blocks, block_rows, heads_here, head_dim)
    grad_blocks = grad_out.reshape(blocks, block_rows, heads_here, head_dim)

    def one_block(carried, inputs):
        key_grad, value_grad = carried
        query_block, grad_block, top_block, total_block = inputs
        scores = (
            jnp.einsum("qhe,khe->hqk", query_block, key_rows, preferred_element_type=jnp.float32)
            * score_scale
        )
        weights_f = jnp.exp(scores - top_block) / total_block
        grad_weights = jnp.einsum(
            "qhe,khe->hqk", grad_block, value_rows, preferred_element_type=jnp.float32
        )
        inner_sum = jnp.sum(weights_f * grad_weights, axis=-1, keepdims=True)
        grad_scores = (weights_f * (grad_weights - inner_sum)).astype(jnp.bfloat16)
        query_grad = (
            jnp.einsum("hqk,khe->qhe", grad_scores, key_rows, preferred_element_type=jnp.float32)
            * score_scale
        )
        key_grad = (
            key_grad
            + jnp.einsum(
                "hqk,qhe->khe", grad_scores, query_block, preferred_element_type=jnp.float32
            )
            * score_scale
        )
        value_grad = value_grad + jnp.einsum(
            "hqk,qhe->khe",
            weights_f.astype(jnp.bfloat16),
            grad_block,
            preferred_element_type=jnp.float32,
        )
        return ((key_grad, value_grad), query_grad)

    zero_rows = jnp.zeros((whole_rows, heads_here, head_dim), jnp.float32)
    (key_grad, value_grad), query_grad = lax.scan(
        one_block, (zero_rows, zero_rows), (query_blocks, grad_blocks, top_vals, totals)
    )
    return (
        query_grad.reshape(whole_rows, heads_here * head_dim),
        key_grad.reshape(whole_rows, heads_here * head_dim),
        value_grad.reshape(whole_rows, heads_here * head_dim),
    )


def local(
    tokens,
    cotangent,
    cell_of,
    query_count,
    attn_norm_gain,
    attn_norm_bias,
    input_weight,
    query_bias,
    value_bias,
    out_weight,
    out_bias,
    ffn_norm_gain,
    ffn_norm_bias,
    up_weight,
    up_bias,
    down_weight,
    down_bias,
):
    micro_count = tokens.shape[0]
    local_rows = tokens.shape[2]
    head_local = input_weight.shape[2]
    heads_here = head_local // HEAD
    group_count = lax.axis_size("wide")
    group_index = lax.axis_index("wide")
    whole_rows = local_rows * lax.axis_size("narrow")
    block_rows = min(512, whole_rows)
    cell_slots = jnp.arange(cell_of.shape[0], dtype=jnp.int32)
    gain_one = attn_norm_gain.astype(jnp.float32)
    bias_one = attn_norm_bias.astype(jnp.float32)
    gain_two = ffn_norm_gain.astype(jnp.float32)
    bias_two = ffn_norm_bias.astype(jnp.float32)
    query_bias_f = query_bias.astype(jnp.float32)
    value_bias_f = value_bias.astype(jnp.float32)
    out_bias_f = out_bias.astype(jnp.float32)
    up_bias_f = up_bias.astype(jnp.float32)
    down_bias_f = down_bias.astype(jnp.float32)
    out_rows = []
    grad_rows = []
    totals_acc = None
    vector_acc = None
    for index_mb in range(micro_count):
        slot_index = index_mb * group_count + group_index
        cell_id = jnp.sum(jnp.where(cell_slots == slot_index, cell_of, 0))
        count_val = jnp.sum(jnp.where(cell_slots == cell_id, query_count, 0))
        loss_scale = jnp.sqrt(count_val.astype(jnp.float32) / 500.0)
        rows_in = tokens[index_mb, 0].astype(jnp.float32)
        normed_one = layer_norm(rows_in, gain_one, bias_one).astype(jnp.bfloat16)
        normed_all = lax.all_gather(normed_one, "narrow", axis=0, tiled=True)
        project = jnp.einsum(
            "sd,dje->sje", normed_all, input_weight, preferred_element_type=jnp.float32
        )
        head_shape = (whole_rows, heads_here, HEAD)
        queries = (project[:, 0] + query_bias_f).astype(jnp.bfloat16).reshape(head_shape)
        key_rows = project[:, 1].astype(jnp.bfloat16).reshape(head_shape)
        value_rows = (project[:, 2] + value_bias_f).astype(jnp.bfloat16).reshape(head_shape)
        attended, top_vals, totals = attend_forward(queries, key_rows, value_rows, block_rows)
        attended = attended.astype(jnp.bfloat16)
        attn_sum = lax.psum_scatter(
            jnp.dot(attended, out_weight, preferred_element_type=jnp.float32).astype(jnp.bfloat16),
            "narrow",
            scatter_dimension=0,
            tiled=True,
        ).astype(jnp.float32)
        resid = rows_in + attn_sum + out_bias_f
        normed_two = layer_norm(resid, gain_two, bias_two).astype(jnp.bfloat16)
        normed_two_all = lax.all_gather(normed_two, "narrow", axis=0, tiled=True)
        pre_act = jnp.dot(normed_two_all, up_weight, preferred_element_type=jnp.float32) + up_bias_f
        activ = jax.nn.gelu(pre_act, approximate=False).astype(jnp.bfloat16)
        ffn_sum = lax.psum_scatter(
            jnp.dot(activ, down_weight, preferred_element_type=jnp.float32).astype(jnp.bfloat16),
            "narrow",
            scatter_dimension=0,
            tiled=True,
        ).astype(jnp.float32)
        out_rows.append((resid + ffn_sum + down_bias_f).astype(jnp.bfloat16))
        top_grad = cotangent[index_mb, 0].astype(jnp.float32) * loss_scale
        top_grad_all = lax.all_gather(top_grad.astype(jnp.bfloat16), "narrow", axis=0, tiled=True)
        down_grad = jnp.einsum("sf,sd->fd", activ, top_grad_all, preferred_element_type=jnp.float32)
        act_grad = jnp.einsum(
            "sd,fd->sf", top_grad_all, down_weight, preferred_element_type=jnp.float32
        )
        pre_grad = (act_grad * gelu_slope(pre_act)).astype(jnp.bfloat16)
        up_grad = jnp.einsum(
            "sd,sf->df", normed_two_all, pre_grad, preferred_element_type=jnp.float32
        )
        up_bias_grad = jnp.sum(pre_grad.astype(jnp.float32), axis=0)
        normed_two_grad = lax.psum_scatter(
            jnp.einsum("sf,df->sd", pre_grad, up_weight, preferred_element_type=jnp.float32).astype(
                jnp.bfloat16
            ),
            "narrow",
            scatter_dimension=0,
            tiled=True,
        ).astype(jnp.float32)
        norm_value, norm_pull = jax.vjp(layer_norm, resid, gain_two, bias_two)
        resid_norm_grad, gain_two_grad, bias_two_grad = norm_pull(normed_two_grad)
        resid_grad = top_grad + resid_norm_grad
        attn_grad_all = lax.all_gather(
            resid_grad.astype(jnp.bfloat16), "narrow", axis=0, tiled=True
        )
        out_grad = jnp.einsum(
            "se,sd->ed", attended, attn_grad_all, preferred_element_type=jnp.float32
        )
        attended_grad = jnp.einsum(
            "sd,ed->se", attn_grad_all, out_weight, preferred_element_type=jnp.float32
        )
        attended_grad = attended_grad.astype(jnp.bfloat16).reshape(head_shape)
        query_grad, key_grad, value_grad = attend_backward(
            queries, key_rows, value_rows, attended_grad, top_vals, totals, block_rows
        )
        stacked_grad = jnp.stack([query_grad, key_grad, value_grad], axis=1).astype(jnp.bfloat16)
        input_grad = jnp.einsum(
            "sd,sje->dje", normed_all, stacked_grad, preferred_element_type=jnp.float32
        )
        query_bias_grad = jnp.sum(stacked_grad[:, 0].astype(jnp.float32), axis=0)
        value_bias_grad = jnp.sum(stacked_grad[:, 2].astype(jnp.float32), axis=0)
        normed_one_grad = lax.psum_scatter(
            jnp.einsum(
                "sje,dje->sd", stacked_grad, input_weight, preferred_element_type=jnp.float32
            ).astype(jnp.bfloat16),
            "narrow",
            scatter_dimension=0,
            tiled=True,
        ).astype(jnp.float32)
        first_value, first_pull = jax.vjp(layer_norm, rows_in, gain_one, bias_one)
        rows_norm_grad, gain_one_grad, bias_one_grad = first_pull(normed_one_grad)
        grad_rows.append(resid_grad + rows_norm_grad)
        vector_mb = (
            gain_one_grad,
            bias_one_grad,
            jnp.sum(resid_grad, axis=0),
            gain_two_grad,
            bias_two_grad,
            jnp.sum(top_grad, axis=0),
        )
        vector_acc = vector_mb if vector_acc is None else tree_add(vector_acc, vector_mb)
        matrix_mb = (
            input_grad,
            query_bias_grad,
            value_bias_grad,
            out_grad,
            up_grad,
            up_bias_grad,
            down_grad,
        )
        totals_acc = matrix_mb if totals_acc is None else tree_add(totals_acc, matrix_mb)
    matrix_sums = lax.psum(
        (
            totals_acc[0],
            totals_acc[1],
            totals_acc[2],
            totals_acc[3],
            totals_acc[4],
            totals_acc[5],
            totals_acc[6],
        ),
        "wide",
    )
    vector_sums = lax.psum(
        (vector_acc[0], vector_acc[1], vector_acc[2], vector_acc[3], vector_acc[4], vector_acc[5]),
        ("wide", "narrow"),
    )
    block_out = jnp.stack(out_rows)[:, None]
    tokens_grad = jnp.stack(grad_rows)[:, None]
    return (
        block_out,
        tokens_grad,
        vector_sums[0],
        vector_sums[1],
        matrix_sums[0],
        matrix_sums[1],
        matrix_sums[2],
        matrix_sums[3],
        vector_sums[2],
        vector_sums[3],
        vector_sums[4],
        matrix_sums[4],
        matrix_sums[5],
        matrix_sums[6],
        vector_sums[5],
    )


def solution(mesh):
    in_specs = (
        P(None, "wide", "narrow", None),
        P(None, "wide", "narrow", None),
        P(),
        P(),
        P(),
        P(),
        P(None, None, "narrow"),
        P("narrow"),
        P("narrow"),
        P("narrow", None),
        P(),
        P(),
        P(),
        P(None, "narrow"),
        P("narrow"),
        P("narrow", None),
        P(),
    )
    out_specs = (
        P(None, "wide", "narrow", None),
        P(None, "wide", "narrow", None),
        P(),
        P(),
        P(None, None, "narrow"),
        P("narrow"),
        P("narrow"),
        P("narrow", None),
        P(),
        P(),
        P(),
        P(None, "narrow"),
        P("narrow"),
        P("narrow", None),
        P(),
    )
    return jax.shard_map(local, mesh=mesh, in_specs=in_specs, out_specs=out_specs, check_vma=False)
```

profile of v0, /device:TPU:0, one launch (start us, length us, event | category | flops | bytes accessed | tf_op | source)
XLA Modules:
  0.0 1283.2 jit_solution(8373644285580186725)
XLA Ops:
  14.8 28.2 %all-gather.9.cloned.1.call-done = bf16[1024,1280]{1,0:T(8,128)(2,1)} async-done(((bf16[256,1280]{1,0:T(8,128)(2,1)}), bf16[1024,1280]{1,0:T(8,128)(2,1)}) %all-gather.9.cloned.1.call-update) | async-done | bytes 2621456 | tf_op jit(solution)/shard_map/all_gather | solution.py:150
  43.0 5.2 fusion.105
  50.8 3.2 squeeze.46
  58.5 18.4 %while.58 = (s32[]{:T(128)}, bf16[2,512,5,64]{1,3,2,0:T(8,128)(2,1)}, f32[2,5,512,1]{2,1,3,0:T(8,128)S(1)}, f32[2,5,512,1]{2,1,3,0:T(8,128)S(1)}, bf16[2,512,5,6...) while((s32[]{:T(128)}, ...), condition=%wide.region_5.6_spmd, body=%wide.region_2.5_spmd.sunk | while | flops 694676480 | bytes 41744572 | solution.py:49
  58.5 2.8 multiply_reduce_fusion.10
  63.4 3.4 fusion.268
  67.7 2.8 multiply_reduce_fusion.10
  72.6 3.4 fusion.268
  79.7 3.1 convolution_convert_fusion.5
  83.4 34.2 %reduce-scatter.9.cloned.1.call-done = bf16[256,1280]{1,0:T(8,128)(2,1)} async-done(((bf16[1024,1280]{1,0:T(8,128)(2,1)}), bf16[256,1280]{1,0:T(8,128)(2,1)}) %reduce-scatter.9.cloned.1.call-update) | async-done | bytes 655376 | tf_op jit(solution)/shard_map/reduce_scatter | solution.py:160
  121.9 25.7 %all-gather.13.cloned.1.call-done = bf16[1024,1280]{1,0:T(8,128)(2,1)} async-done(((bf16[256,1280]{1,0:T(8,128)(2,1)}), bf16[1024,1280]{1,0:T(8,128)(2,1)}) %all-gather.13.cloned.1.call-update) | async-done | bytes 2621456 | tf_op jit(solution)/shard_map/all_gather | solution.py:150
  147.6 5.2 fusion.101
  156.0 3.2 squeeze.48
  162.6 18.4 %while.59 = (s32[]{:T(128)}, bf16[2,512,5,64]{1,3,2,0:T(8,128)(2,1)}, f32[2,5,512,1]{2,1,3,0:T(8,128)S(1)}, f32[2,5,512,1]{2,1,3,0:T(8,128)S(1)}, bf16[2,512,5,6...) while((s32[]{:T(128)}, ...), condition=%wide.region_15.16_spmd, body=%wide.region_12.15_spmd.sunk | while | flops 694676480 | bytes 41744572 | solution.py:49
  162.6 2.8 multiply_reduce_fusion.11
  167.5 3.4 fusion.272
  171.8 2.8 multiply_reduce_fusion.11
  176.7 3.4 fusion.272
  183.8 3.1 convolution_convert_fusion.3
  187.5 34.1 %reduce-scatter.13.cloned.1.call-done = bf16[256,1280]{1,0:T(8,128)(2,1)} async-done(((bf16[1024,1280]{1,0:T(8,128)(2,1)}), bf16[256,1280]{1,0:T(8,128)(2,1)}) %reduce-scatter.13.cloned.1.call-update) | async-done | bytes 655376 | tf_op jit(solution)/shard_map/reduce_scatter | solution.py:160
  230.4 3.2 fusion.145
  235.2 16.9 %all-gather.15.cloned.1.call-done = bf16[1024,1280]{1,0:T(8,128)(2,1)} async-done(((bf16[256,1280]{1,0:T(8,128)(2,1)}), bf16[1024,1280]{1,0:T(8,128)(2,1)}) %all-gather.15.cloned.1.call-update) | async-done | bytes 2621456 | tf_op jit(solution)/shard_map/all_gather | solution.py:168
  252.1 7.6 fusion.173
  259.7 19.9 %all-gather.21.cloned.1.call-done = bf16[1024,1280]{1,0:T(8,128)(2,1)} async-done(((bf16[256,1280]{1,0:T(8,128)(2,1)}), bf16[1024,1280]{1,0:T(8,128)(2,1)}) %all-gather.21.cloned.1.call-update) | async-done | bytes 2621456 | tf_op jit(solution)/shard_map/all_gather | solution.py:179
  279.7 9.1 convert_reduce_fusion
  290.3 4.9 convolution_convert_fusion
  295.4 12.0 all-gather.11.cloned.1.call-done
  307.4 27.8 %fusion.70 = (bf16[1024,1280]{1,0:T(8,128)(2,1)}, bf16[1024,1280]{1,0:T(8,128)(2,1)}, f32[1024,1280]{1,0:T(8,128)}) fusion(f32[1280]{0:T(1024)S(1)} %convert_element_type.241, f32[1024,1280]{1,0:T(8,128)} %fusion.173, bf16[1024,1280]{1,0:T(8,128)(2,1)} %all-gather.11.cloned.1.call-done, bf16[1280,1280]{1,0:T(8,128)(2,1)S(1)} %copy-done), kind=kOutput, calls=%fused_computation.92 | convolution fusion | flops 3528458240 | bytes 21632000 | tf_op jit(solution)/shard_map/dot_general | solution.py:169
  335.2 9.0 convert_reduce_fusion.1
  345.8 4.8 convolution_convert_fusion.1
  352.4 6.7 convolution_convert_fusion.4
  360.9 6.9 convolution_convert_fusion.2
  367.8 4.6 reduce-scatter.21.cloned.1.call-done
  372.4 37.8 %reduce-scatter.17.cloned.1.call-done = bf16[256,1280]{1,0:T(8,128)(2,1)} async-done(((bf16[1024,1280]{1,0:T(8,128)(2,1)}), bf16[256,1280]{1,0:T(8,128)(2,1)}) %reduce-scatter.17.cloned.1.call-update) | async-done | bytes 655376 | tf_op jit(solution)/shard_map/reduce_scatter | solution.py:189
  410.2 2.9 fusion.132
  415.3 32.3 %reduce-scatter.11.cloned.1.call-done = bf16[256,1280]{1,0:T(8,128)(2,1)} async-done(((bf16[1024,1280]{1,0:T(8,128)(2,1)}), bf16[256,1280]{1,0:T(8,128)(2,1)}) %reduce-scatter.11.cloned.1.call-update) | async-done | bytes 655376 | tf_op jit(solution)/shard_map/reduce_scatter | solution.py:171
  447.5 3.7 fusion.170
  453.3 31.5 %reduce-scatter.15.cloned.1.call-done = bf16[256,1280]{1,0:T(8,128)(2,1)} async-done(((bf16[1024,1280]{1,0:T(8,128)(2,1)}), bf16[256,1280]{1,0:T(8,128)(2,1)}) %reduce-scatter.15.cloned.1.call-update) | async-done | bytes 655376 | tf_op jit(solution)/shard_map/reduce_scatter | solution.py:171
  484.8 3.7 fusion.169
  489.8 22.7 %all-gather.19.cloned.1.call-done = bf16[1024,1280]{1,0:T(8,128)(2,1)} async-done(((bf16[256,1280]{1,0:T(8,128)(2,1)}), bf16[1024,1280]{1,0:T(8,128)(2,1)}) %all-gather.19.cloned.1.call-update) | async-done | bytes 2621456 | tf_op jit(solution)/shard_map/all_gather | solution.py:200
  512.5 3.8 convolution_convert_fusion.7
  520.0 19.6 %all-gather.23.cloned.1.call-done = bf16[1024,1280]{1,0:T(8,128)(2,1)} async-done(((bf16[256,1280]{1,0:T(8,128)(2,1)}), bf16[1024,1280]{1,0:T(8,128)(2,1)}) %all-gather.23.cloned.1.call-update) | async-done | bytes 2621456 | tf_op jit(solution)/shard_map/all_gather | solution.py:200
  539.5 3.8 convolution_convert_fusion.6
  543.3 3.0 reshape_reshape.5
  549.3 25.4 %while.61 = (s32[]{:T(128)}, f32[1024,5,64]{0,2,1:T(8,128)S(1)}, f32[1024,5,64]{0,2,1:T(8,128)S(1)}, bf16[2,512,5,64]{1,3,2,0:T(8,128)(2,1)}, bf16[2,512,5,64]{1...) while((s32[]{:T(128)}, f32[1024,5,64]{0,2,1:T(8,128)S(1)}, ...), condition=%wide.region_38.39_spmd.clone, body=%wide.region_36.38_spmd.clone.sunk | while | flops 1703114240 | bytes 98398480 | solution.py:92
  549.3 2.8 fusion.295
  552.1 4.4 multiply_reduce_fusion.13
  564.8 4.4 multiply_reduce_fusion.13
  582.0 4.5 bitcast_convert_fusion
  588.7 25.4 %while.60 = (s32[]{:T(128)}, f32[1024,5,64]{0,2,1:T(8,128)S(1)}, f32[1024,5,64]{0,2,1:T(8,128)S(1)}, bf16[2,512,5,64]{1,3,2,0:T(8,128)(2,1)}, bf16[2,512,5,64]{1...) while((s32[]{:T(128)}, f32[1024,5,64]{0,2,1:T(8,128)S(1)}, ...), condition=%wide.region_27.28_spmd.clone, body=%wide.region_25.27_spmd.clone.sunk | while | flops 1703114240 | bytes 98398480 | solution.py:92
  591.5 4.4 multiply_reduce_fusion.12
  604.2 4.4 multiply_reduce_fusion.12
  621.4 4.3 bitcast_convert_fusion.1
  627.5 5.6 fusion.175
  633.1 3.7 fusion.176
  636.8 6.0 convolution_add_fusion.1
  642.8 5.7 convolution_add_fusion
  656.3 4.3 convolution_add_fusion.2
  664.1 38.9 %all-reduce.1 = (f32[320]{0:T(512)}, f32[320]{0:T(512)}, f32[1280]{0:T(1024)}) all-reduce(f32[320]{0:T(512)S(1)} %add.339, f32[320]{0:T(512)S(1)} %add.340, f32[1280]{0:T(1024)S(1)} %add.346), channel_id=1, replica_groups=mesh['wide'=8,'narrow'=4] {'wide'}, use_global_device_ids=true, to_apply=%region_51.52 | all-reduce | flops 1920 | bytes 15360 | tf_op jit(solution)/shard_map/psum | solution.py:249
  706.6 43.6 %all-reduce = (f32[1280]{0:T(1024)}, f32[1280]{0:T(1024)}, f32[1280]{0:T(1024)}, f32[1280]{0:T(1024)}, f32[1280]{0:T(1024)}, /*index=5*/f32[1280]{0:T(1024)}) all-reduce(f32[1280]{0:T(1024)S(1)} %add.336, f32[1280]{0:T(1024)S(1)} %add.337, f32[1280]{0:T(1024)S(1)} %add.342, ...), channel_id=1, replica_groups=mesh['wide'=8,'narrow'=4] {'wide','narrow'}, use_global_device_ids=true, to_apply=%region_44.45 | all-reduce | flops 7680 | bytes 61440 | tf_op jit(solution)/shard_map/psum | solution.py:261
  754.3 506.1 %all-reduce.5.cloned.1.call-done = (f32[1280,3,320]{0,2,1:T(8,128)}, f32[320,1280]{1,0:T(8,128)}, f32[1280,1280]{1,0:T(8,128)}, f32[1280,1280]{1,0:T(8,128)}) async-done(((f32[1280,3,320]{0,2,1:T(8,128)}, f32[320,1280]{1,0:T(8,128)}, f32[1280,1280]{1,0:T(8,128)}, f32[1280,1280]{1,0:T(8,128)}), (f32[1280,3,320]{0,2,1:T(8,128)}, f32[320,1280]{1,0:T(8,128)}, f32[1280,1280]{1,0:T(8,128)}, ...) | async-done | bytes 19660816 | tf_op jit(solution)/shard_map/psum | solution.py:249
  1260.4 5.4 copy.118
  1267.6 3.3 copy.120
  1271.9 3.3 copy.121
  (423 shorter events, 142.2 us)
Async XLA Ops:
  7.2 244.9 %copy-start = (bf16[1280,1280]{1,0:T(8,128)(2,1)S(1)}, bf16[1280,1280]{1,0:T(8,128)(2,1)}, u32[]{:S(2)}) copy-start(bf16[1280,1280]{1,0:T(8,128)(2,1)} %param.38) | copy-start | bytes 9830404
  7.2 7.5 copy-start.91
  7.2 7.5 copy-start.92
  7.2 35.8 %all-gather.9.cloned.1.call-start = ((), (), s32[]{:S(2)}) async-start(), calls=%async_computation.8 | async-start | bytes 3276800 | tf_op jit(solution)/shard_map/all_gather | solution.py:150
  9.0 3.4 copy-start.64
  11.6 107.9 %copy-start.62 = (f32[1280]{0:T(1024)}, f32[1280]{0:T(1024)S(1)}, u32[]{:S(2)}) copy-start(f32[1280]{0:T(1024)S(1)} %convert_element_type.227) | copy-start | bytes 15364
  14.6 103.0 %reduce-scatter.9.cloned.1.call-start = ((), (), s32[]{:S(2)}) async-start(), calls=%async_computation.9 | async-start | bytes 3276800 | tf_op jit(solution)/shard_map/reduce_scatter | solution.py:160
  76.9 5.9 copy-start.58
  76.9 5.9 copy-start.60
  82.8 64.8 %all-gather.13.cloned.1.call-start = ((), (), s32[]{:S(2)}) async-start(), calls=%async_computation.12 | async-start | bytes 3276800 | tf_op jit(solution)/shard_map/all_gather | solution.py:150
  83.4 69.3 %copy-start.66 = (f32[256]{0:T(256)}, f32[256]{0:T(256)S(1)}, u32[]{:S(2)}) copy-start(f32[256]{0:T(256)S(1)} %broadcast_multiply_fusion.1) | copy-start | bytes 3076
  119.5 33.2 %copy-start.82 = (f32[256]{0:T(256)}, f32[256]{0:T(256)S(1)}, u32[]{:S(2)}) copy-start(f32[256]{0:T(256)S(1)} %get-tuple-element.370) | copy-start | bytes 3076
  119.6 33.2 %copy-start.78 = (f32[256]{0:T(256)}, f32[256]{0:T(256)S(1)}, u32[]{:S(2)}) copy-start(f32[256]{0:T(256)S(1)} %fusion.157) | copy-start | bytes 3076
  121.8 99.8 %reduce-scatter.13.cloned.1.call-start = ((), (), s32[]{:S(2)}) async-start(), calls=%async_computation.13 | async-start | bytes 3276800 | tf_op jit(solution)/shard_map/reduce_scatter | solution.py:160
  186.8 65.2 %all-gather.15.cloned.1.call-start = ((), (), s32[]{:S(2)}) async-start(), calls=%async_computation.14 | async-start | bytes 3276800 | tf_op jit(solution)/shard_map/all_gather | solution.py:168
  226.3 8.9 copy-start.89
  226.4 53.3 %all-gather.21.cloned.1.call-start = ((), (), s32[]{:S(2)}) async-start(), calls=%async_computation.20 | async-start | bytes 3276800 | tf_op jit(solution)/shard_map/all_gather | solution.py:179
  233.6 73.8 %all-gather.11.cloned.1.call-start = ((), (), s32[]{:S(2)}) async-start(), calls=%async_computation.10 | async-start | bytes 3276800 | tf_op jit(solution)/shard_map/all_gather | solution.py:168
  234.4 100.8 %all-gather.17.cloned.1.call-start = ((), (), s32[]{:S(2)}) async-start(), calls=%async_computation.16 | async-start | bytes 3276800 | tf_op jit(solution)/shard_map/all_gather | solution.py:179
  235.1 137.2 %reduce-scatter.21.cloned.1.call-start = ((), (), s32[]{:S(2)}) async-start(), calls=%async_computation.21 | async-start | bytes 3276800 | tf_op jit(solution)/shard_map/reduce_scatter | solution.py:189
  295.2 115.0 %reduce-scatter.17.cloned.1.call-start = ((), (), s32[]{:S(2)}) async-start(), calls=%async_computation.17 | async-start | bytes 3276800 | tf_op jit(solution)/shard_map/reduce_scatter | solution.py:189
  350.7 96.9 %reduce-scatter.11.cloned.1.call-start = ((), (), s32[]{:S(2)}) async-start(), calls=%async_computation.11 | async-start | bytes 3276800 | tf_op jit(solution)/shard_map/reduce_scatter | solution.py:171
  359.1 125.6 %reduce-scatter.15.cloned.1.call-start = ((), (), s32[]{:S(2)}) async-start(), calls=%async_computation.15 | async-start | bytes 3276800 | tf_op jit(solution)/shard_map/reduce_scatter | solution.py:171
  360.9 6.9 copy-start.90
  367.7 42.5 %copy-start.3 = (bf16[2,1,256,1280]{3,2,1,0:T(8,128)(2,1)S(1)}, bf16[2,1,256,1280]{3,2,1,0:T(8,128)(2,1)}, u32[]{:S(2)}) copy-start(bf16[2,1,256,1280]{3,2,1,0:T(8,128)(2,1)} %param.25) | copy-start | bytes 3932164
  367.7 42.5 %copy-start.16 = (bf16[256,1280]{1,0:T(8,128)(2,1)S(1)}, bf16[256,1280]{1,0:T(8,128)(2,1)}, u32[]{:S(2)}) copy-start(bf16[256,1280]{1,0:T(8,128)(2,1)} %reduce-scatter.13.cloned.1.call-done) | copy-start | bytes 1966084
  367.7 42.5 %copy-start.18 = (bf16[256,1280]{1,0:T(8,128)(2,1)S(1)}, bf16[256,1280]{1,0:T(8,128)(2,1)}, u32[]{:S(2)}) copy-start(bf16[256,1280]{1,0:T(8,128)(2,1)} %reduce-scatter.9.cloned.1.call-done) | copy-start | bytes 1966084
  367.7 144.8 %all-gather.19.cloned.1.call-start = ((), (), s32[]{:S(2)}) async-start(), calls=%async_computation.18 | async-start | bytes 3276800 | tf_op jit(solution)/shard_map/all_gather | solution.py:200
  372.4 40.8 %copy-start.23 = (bf16[256,1280]{1,0:T(8,128)(2,1)S(1)}, bf16[256,1280]{1,0:T(8,128)(2,1)}, u32[]{:S(2)}) copy-start(bf16[256,1280]{1,0:T(8,128)(2,1)} %reduce-scatter.21.cloned.1.call-done) | copy-start | bytes 1966084
  410.2 3.0 copy-start.24
  453.3 86.3 %all-gather.23.cloned.1.call-start = ((), (), s32[]{:S(2)}) async-start(), calls=%async_computation.22 | async-start | bytes 3276800 | tf_op jit(solution)/shard_map/all_gather | solution.py:200
  489.5 213.4 %reduce-scatter.23.cloned.1.call-start = ((), (), s32[]{:S(2)}) async-start(), calls=%async_computation.23 | async-start | bytes 3276800 | tf_op jit(solution)/shard_map/reduce_scatter | solution.py:219
  543.3 5.9 copy-start.7
  582.0 5.5 copy-start.59
  582.0 5.5 copy-start.61
  586.6 116.4 %reduce-scatter.19.cloned.1.call-start = ((), (), s32[]{:S(2)}) async-start(), calls=%async_computation.19 | async-start | bytes 3276800 | tf_op jit(solution)/shard_map/reduce_scatter | solution.py:219
  619.0 6.7 copy-start.32
  619.3 6.4 copy-start.56
  625.7 634.7 %all-reduce.5.cloned.1.call-start = ((), (), s32[]{:S(2)}) async-start(), calls=%async_computation.24 | async-start | bytes 39321600 | tf_op jit(solution)/shard_map/psum | solution.py:249
  627.4 5.6 copy-start.100
  627.5 5.6 copy-start.112
  633.0 3.8 copy-start.97
  633.1 3.8 copy-start.108
  636.8 6.0 copy-start.98
  636.8 6.0 copy-start.110
  642.8 5.7 copy-start.51
  642.8 5.7 copy-start.101
  650.5 2.9 copy-start.95
  660.8 2.9 copy-start.48
  660.8 3.1 copy-start.45
  662.1 40.9 %copy-start.4 = (bf16[2,1,256,1280]{3,2,1,0:T(8,128)(2,1)S(1)}, bf16[2,1,256,1280]{3,2,1,0:T(8,128)(2,1)}, u32[]{:S(2)}) copy-start(bf16[2,1,256,1280]{3,2,1,0:T(8,128)(2,1)} %param.25) | copy-start | bytes 3932164
  662.1 40.9 %copy-start.63 = (f32[1280]{0:T(1024)S(1)}, f32[1280]{0:T(1024)}, u32[]{:S(2)}) copy-start(f32[1280]{0:T(1024)} %copy-done.62) | copy-start | bytes 15364
  662.1 40.9 %copy-start.65 = (f32[256]{0:T(256)S(1)}, f32[256]{0:T(256)}, u32[]{:S(2)}) copy-start(f32[256]{0:T(256)} %copy-done.64) | copy-start | bytes 3076
  662.1 40.9 %copy-start.67 = (f32[256]{0:T(256)S(1)}, f32[256]{0:T(256)}, u32[]{:S(2)}) copy-start(f32[256]{0:T(256)} %copy-done.66) | copy-start | bytes 3076
  663.3 42.0 %copy-start.81 = (f32[256]{0:T(256)S(1)}, f32[256]{0:T(256)}, u32[]{:S(2)}) copy-start(f32[256]{0:T(256)} %copy-done.80) | copy-start | bytes 3076
  663.3 42.0 %copy-start.83 = (f32[256]{0:T(256)S(1)}, f32[256]{0:T(256)}, u32[]{:S(2)}) copy-start(f32[256]{0:T(256)} %copy-done.82) | copy-start | bytes 3076
  663.3 42.0 %copy-start.77 = (f32[256]{0:T(256)S(1)}, f32[256]{0:T(256)}, u32[]{:S(2)}) copy-start(f32[256]{0:T(256)} %copy-done.76) | copy-start | bytes 3076
  663.3 42.0 %copy-start.79 = (f32[256]{0:T(256)S(1)}, f32[256]{0:T(256)}, u32[]{:S(2)}) copy-start(f32[256]{0:T(256)} %copy-done.78) | copy-start | bytes 3076
  703.0 47.3 %copy-start.20 = (f32[256,1280]{1,0:T(8,128)S(1)}, f32[256,1280]{1,0:T(8,128)}, u32[]{:S(2)}) copy-start(f32[256,1280]{1,0:T(8,128)} %copy-done.19) | copy-start | bytes 3932164
  1260.4 5.4 copy-start.49
  1260.4 7.2 copy-start.22
  1265.8 5.1 slice-start
  1267.6 4.3 slice-start.1
  1271.9 4.3 copy-start.1
  (83 other events, 134.6 us)
Sparse Core Ops, SparseCore 0:
  14.7 28.2 all-gather.8
  82.9 34.6 reduce-scatter.8
  122.0 25.5 all-gather.12
  187.0 34.6 reduce-scatter.12
  226.5 25.5 all-gather.14
  254.1 25.5 all-gather.20
  281.8 25.5 all-gather.10
  309.0 25.5 all-gather.16
  337.7 34.6 reduce-scatter.20
  375.5 34.6 reduce-scatter.16
  412.8 34.6 reduce-scatter.10
  450.1 34.6 reduce-scatter.14
  486.9 25.5 all-gather.18
  513.9 25.5 all-gather.22
  586.7 34.6 reduce-scatter.22
  625.9 34.6 reduce-scatter.18
  666.3 594.0 all-reduce.4
where the time goes:
time: 1290 us; the launch traced here: 1280 us
  waiting for transfers between devices  827 us (64%)
  matrix products  211 us (16%)
  blocking collectives  82.6 us (6%)
  local copies, waits for them, and re-layouts  77.1 us (6%)
  other arithmetic  65.9 us (5%)
  between operations  16.8 us (1%)
    psum x1, waiting for transfers between devices, local(): lax.psum((totals_acc[0], totals_acc[1], totals_acc[2], totals_acc[3], tot...  506 us
    reduce_scatter x2, waiting for transfers between devices, local(): lax.psum_scatter(jnp.dot(attended, out_weight, preferred_element_type=jnp...  68.3 us
    reduce_scatter x2, waiting for transfers between devices, local(): lax.psum_scatter(jnp.dot(activ, down_weight, preferred_element_type=jnp.f...  63.7 us
    all_gather x2, waiting for transfers between devices, local(): normed_all = lax.all_gather(normed_one, 'narrow', axis=0, tiled=True)  53.9 us
    psum x1, blocking collectives, local(): lax.psum((vector_acc[0], vector_acc[1], vector_acc[2], vector_acc[3], vec...  43.6 us
    reduce_scatter x2, waiting for transfers between devices, local(): lax.psum_scatter(jnp.einsum('sf,df->sd', pre_grad, up_weight, preferred_e...  42.4 us
    all_gather x2, waiting for transfers between devices, local(): lax.all_gather(resid_grad.astype(jnp.bfloat16), 'narrow', axis=0, tiled=T...  42.3 us
    unnamed x212, local copies, waits for them, and re-layouts  39.6 us
  transfers between devices with their start and end apart: 17, of which 14 were waited for; matrix products, arithmetic and copies ran while one was open for 14% of the time, Pallas kernels for 0%

commit v1 on v0

v1 whole, which is shorter than its diff:
```python
import jax
import jax.numpy as jnp
from jax import lax
from jax.sharding import PartitionSpec as P

HEAD = 64


norm_eps = 1e-05
score_scale = 0.125


def layer_norm(values, gain_vec, bias_vec):
    average = jnp.mean(values, axis=-1, keepdims=True)
    centred = values - average
    variance = jnp.mean(centred * centred, axis=-1, keepdims=True)
    return centred * lax.rsqrt(variance + norm_eps) * gain_vec + bias_vec


def tree_add(first_tree, second_tree):
    return jax.tree.map(jnp.add, first_tree, second_tree)


def gelu_slope(values):
    cumul = 0.5 * (1.0 + lax.erf(values * 0.7071067811865476))
    density = jnp.exp(-0.5 * values * values) * 0.3989422804014327
    return cumul + values * density


def attend_forward(queries, key_rows, value_rows, block_rows):
    whole_rows, heads_here, head_dim = queries.shape
    blocks = whole_rows // block_rows
    query_blocks = queries.reshape(blocks, block_rows, heads_here, head_dim)

    def one_block(query_block):
        scores = (
            jnp.einsum("qhe,khe->hqk", query_block, key_rows, preferred_element_type=jnp.float32)
            * score_scale
        )
        top_val = jnp.max(scores, axis=-1, keepdims=True)
        exp_scores = jnp.exp(scores - top_val)
        totals = jnp.sum(exp_scores, axis=-1, keepdims=True)
        weights_bf = (exp_scores / totals).astype(jnp.bfloat16)
        mixed_rows = jnp.einsum(
            "hqk,khe->qhe", weights_bf, value_rows, preferred_element_type=jnp.float32
        )
        return (mixed_rows, top_val, totals)

    mixed_rows, top_vals, totals = lax.map(one_block, query_blocks)
    return (mixed_rows.reshape(whole_rows, heads_here * head_dim), top_vals, totals)


def attend_backward(queries, key_rows, value_rows, grad_out, top_vals, totals, block_rows):
    whole_rows, heads_here, head_dim = queries.shape
    blocks = whole_rows // block_rows
    query_blocks = queries.reshape(blocks, block_rows, heads_here, head_dim)
    grad_blocks = grad_out.reshape(blocks, block_rows, heads_here, head_dim)

    def one_block(carried, inputs):
        key_grad, value_grad = carried
        query_block, grad_block, top_block, total_block = inputs
        scores = (
            jnp.einsum("qhe,khe->hqk", query_block, key_rows, preferred_element_type=jnp.float32)
            * score_scale
        )
        weights_f = jnp.exp(scores - top_block) / total_block
        grad_weights = jnp.einsum(
            "qhe,khe->hqk", grad_block, value_rows, preferred_element_type=jnp.float32
        )
        inner_sum = jnp.sum(weights_f * grad_weights, axis=-1, keepdims=True)
        grad_scores = (weights_f * (grad_weights - inner_sum)).astype(jnp.bfloat16)
        query_grad = (
            jnp.einsum("hqk,khe->qhe", grad_scores, key_rows, preferred_element_type=jnp.float32)
            * score_scale
        )
        key_grad = (
            key_grad
            + jnp.einsum(
                "hqk,qhe->khe", grad_scores, query_block, preferred_element_type=jnp.float32
            )
            * score_scale
        )
        value_grad = value_grad + jnp.einsum(
            "hqk,qhe->khe",
            weights_f.astype(jnp.bfloat16),
            grad_block,
            preferred_element_type=jnp.float32,
        )
        return ((key_grad, value_grad), query_grad)

    zero_rows = jnp.zeros((whole_rows, heads_here, head_dim), jnp.float32)
    (key_grad, value_grad), query_grad = lax.scan(
        one_block, (zero_rows, zero_rows), (query_blocks, grad_blocks, top_vals, totals)
    )
    return (
        query_grad.reshape(whole_rows, heads_here * head_dim),
        key_grad.reshape(whole_rows, heads_here * head_dim),
        value_grad.reshape(whole_rows, heads_here * head_dim),
    )


def narrow_swap(values, bit):
    return lax.ppermute(values, "narrow", [(i, i ^ bit) for i in range(lax.axis_size("narrow"))])


def gather_rows(own):
    sibling = narrow_swap(own, 1)
    partner = narrow_swap(own, 2)
    across = narrow_swap(partner, 1)
    return jnp.concatenate([own, sibling, partner, across], axis=0)


def rounded_sum(first, second):
    return (first.astype(jnp.float32) + second.astype(jnp.float32)).astype(jnp.bfloat16)


def scatter_rows(far, near, rows):
    for_partner = rounded_sum(far[:rows], narrow_swap(far[rows:], 1))
    arrived = narrow_swap(for_partner, 2)
    own = near[:rows].astype(jnp.float32) + narrow_swap(near[rows:], 1).astype(jnp.float32)
    return own + arrived.astype(jnp.float32)


def ring_order(count):
    evens = list(range(0, count, 2))
    odds = list(range(1, count, 2))
    return evens + odds[::-1]


def ring_chunks(place, count, direction):
    return [jnp.mod(place - direction * (step + 1), count) for step in range(count)]


def ring_sum(chunk_of, count, direction, place):
    order = ring_order(count)
    perm = [(order[i], order[(i + direction) % count]) for i in range(count)]
    places = ring_chunks(place, count, direction)
    carried = chunk_of(places[0])
    for step in range(1, count):
        arrived = lax.ppermute(carried, "wide", perm)
        carried = rounded_sum(arrived, chunk_of(places[step]))
    pieces = [carried]
    for step in range(1, count):
        carried = lax.ppermute(carried, "wide", perm)
        pieces.append(carried)
    indices = [jnp.mod(place - direction * step, count) for step in range(count)]
    return pieces, indices


def reduce_wide(grad, splits):
    count = lax.axis_size("wide")
    rows, cols = grad.shape
    if count > 8:
        return lax.psum(grad.astype(jnp.bfloat16), "wide").astype(jnp.float32)
    order = ring_order(count)
    inverse = [order.index(i) for i in range(count)]
    place = jnp.take(jnp.array(inverse, jnp.int32), lax.axis_index("wide"))
    parts = grad.reshape(count, splits, rows // (count * splits), cols).astype(jnp.bfloat16)
    total = jnp.zeros(parts.shape, jnp.float32)
    for part in range(splits):
        direction = 1 if part % 2 == 0 else -1

        def chunk_of(index, part=part):
            return lax.dynamic_index_in_dim(parts[:, part], index, 0, keepdims=False)

        pieces, indices = ring_sum(chunk_of, count, direction, place)
        for piece, index in zip(pieces, indices):
            total = lax.dynamic_update_slice(
                total, piece.astype(jnp.float32)[None, None], (index, part, 0, 0)
            )
    return total.reshape(rows, cols)


def butterfly(values, axis):
    count = lax.axis_size(axis)
    bit = 1
    while bit < count:
        values = values + lax.ppermute(values, axis, [(i, i ^ bit) for i in range(count)])
        bit *= 2
    return values


def norm_stats(values):
    average = jnp.mean(values, axis=-1, keepdims=True)
    centred = values - average
    variance = jnp.mean(centred * centred, axis=-1, keepdims=True)
    inverse = lax.rsqrt(variance + norm_eps)
    return centred * inverse, inverse


def norm_back(grad, normed, inverse, gain_vec):
    scaled = grad * gain_vec
    mean_one = jnp.mean(scaled, axis=-1, keepdims=True)
    mean_two = jnp.mean(scaled * normed, axis=-1, keepdims=True)
    return inverse * (scaled - mean_one - normed * mean_two)


def dot32(first, second, first_dim, second_dim):
    return lax.dot_general(
        first, second, (((first_dim,), (second_dim,)), ((), ())), preferred_element_type=jnp.float32
    )


def local(
    tokens,
    cotangent,
    cell_of,
    query_count,
    attn_norm_gain,
    attn_norm_bias,
    input_weight,
    query_bias,
    value_bias,
    out_weight,
    out_bias,
    ffn_norm_gain,
    ffn_norm_bias,
    up_weight,
    up_bias,
    down_weight,
    down_bias,
):
    bf16 = jnp.bfloat16
    micro_count = tokens.shape[0]
    rows = tokens.shape[2]
    model = tokens.shape[3]
    head_local = input_weight.shape[2]
    heads_here = head_local // HEAD
    group_count = lax.axis_size("wide")
    group_index = lax.axis_index("wide")
    whole_rows = rows * lax.axis_size("narrow")
    half = whole_rows // 2
    block_rows = min(512, whole_rows)
    head_shape = (whole_rows, heads_here, HEAD)
    cell_slots = jnp.arange(cell_of.shape[0], dtype=jnp.int32)
    gain_one = attn_norm_gain.astype(jnp.float32)
    bias_one = attn_norm_bias.astype(jnp.float32)
    gain_two = ffn_norm_gain.astype(jnp.float32)
    bias_two = ffn_norm_bias.astype(jnp.float32)
    query_bias_f = query_bias.astype(jnp.float32)
    value_bias_f = value_bias.astype(jnp.float32)
    out_bias_f = out_bias.astype(jnp.float32)
    up_bias_f = up_bias.astype(jnp.float32)
    down_bias_f = down_bias.astype(jnp.float32)
    weight_flat = input_weight.reshape(model, 3 * head_local)
    micros = range(micro_count)

    rows_in, hat_one, inv_one, normed_one_all = [], [], [], []
    for m in micros:
        x = tokens[m, 0].astype(jnp.float32)
        hat, inv = norm_stats(x)
        rows_in.append(x)
        hat_one.append(hat)
        inv_one.append(inv)
        normed_one_all.append(gather_rows((hat * gain_one + bias_one).astype(bf16)))

    top_grad, top_grad_all = [], []
    for m in micros:
        slot_index = m * group_count + group_index
        cell_id = jnp.sum(jnp.where(cell_slots == slot_index, cell_of, 0))
        count_val = jnp.sum(jnp.where(cell_slots == cell_id, query_count, 0))
        loss_scale = jnp.sqrt(count_val.astype(jnp.float32) / 500.0)
        grad = cotangent[m, 0].astype(jnp.float32) * loss_scale
        top_grad.append(grad)
        top_grad_all.append(gather_rows(grad.astype(bf16)))

    queries, keys, values, attended, tops, sums = [], [], [], [], [], []
    resid, hat_two, inv_two, normed_two_all = [], [], [], []
    for m in micros:
        project = dot32(normed_one_all[m], weight_flat, 1, 0)
        queries.append((project[:, :head_local] + query_bias_f).astype(bf16).reshape(head_shape))
        keys.append(project[:, head_local : 2 * head_local].astype(bf16).reshape(head_shape))
        values.append((project[:, 2 * head_local :] + value_bias_f).astype(bf16).reshape(head_shape))
        mixed, top_vals, totals = attend_forward(queries[m], keys[m], values[m], block_rows)
        mixed = mixed.astype(bf16)
        attended.append(mixed)
        tops.append(top_vals)
        sums.append(totals)
        far = dot32(mixed[half:], out_weight, 1, 0).astype(bf16)
        near = dot32(mixed[:half], out_weight, 1, 0).astype(bf16)
        res = rows_in[m] + scatter_rows(far, near, rows) + out_bias_f
        resid.append(res)
        hat, inv = norm_stats(res)
        hat_two.append(hat)
        inv_two.append(inv)
        normed_two_all.append(gather_rows((hat * gain_two + bias_two).astype(bf16)))

    activ, pre_grad = [], []
    out_rows = []
    for m in micros:
        pre_act = dot32(normed_two_all[m], up_weight, 1, 0) + up_bias_f
        cumul = 0.5 * (1.0 + lax.erf(pre_act * 0.7071067811865476))
        density = jnp.exp(-0.5 * pre_act * pre_act) * 0.3989422804014327
        activ.append((pre_act * cumul).astype(bf16))
        act_grad = dot32(top_grad_all[m], down_weight, 1, 1)
        pre_grad.append((act_grad * (cumul + pre_act * density)).astype(bf16))
    normed_two_grad = []
    for m in micros:
        far = dot32(pre_grad[m][half:], up_weight, 1, 1).astype(bf16)
        near = dot32(pre_grad[m][:half], up_weight, 1, 1).astype(bf16)
        normed_two_grad.append(scatter_rows(far, near, rows))
    down_grad = sum(dot32(activ[m], top_grad_all[m], 0, 0) for m in micros)
    down_sum = reduce_wide(down_grad, 4)
    up_grad = sum(dot32(normed_two_all[m], pre_grad[m], 0, 0) for m in micros)
    up_sum = reduce_wide(up_grad, 4)
    up_bias_grad = sum(jnp.sum(pre_grad[m].astype(jnp.float32), axis=0) for m in micros)
    for m in micros:
        far = dot32(activ[m][half:], down_weight, 1, 0).astype(bf16)
        near = dot32(activ[m][:half], down_weight, 1, 0).astype(bf16)
        out_rows.append((resid[m] + scatter_rows(far, near, rows) + down_bias_f).astype(bf16))

    resid_grad, attn_grad_all = [], []
    for m in micros:
        grad = top_grad[m] + norm_back(normed_two_grad[m], hat_two[m], inv_two[m], gain_two)
        resid_grad.append(grad)
        attn_grad_all.append(gather_rows(grad.astype(bf16)))
    stacked, normed_one_grad = [], []
    for m in micros:
        attended_grad = dot32(attn_grad_all[m], out_weight, 1, 1).astype(bf16).reshape(head_shape)
        query_grad, key_grad, value_grad = attend_backward(
            queries[m], keys[m], values[m], attended_grad, tops[m], sums[m], block_rows
        )
        stack = jnp.concatenate([query_grad, key_grad, value_grad], axis=1).astype(bf16)
        stacked.append(stack)
        far = dot32(stack[half:], weight_flat, 1, 1).astype(bf16)
        near = dot32(stack[:half], weight_flat, 1, 1).astype(bf16)
        normed_one_grad.append(scatter_rows(far, near, rows))
    out_grad = sum(dot32(attended[m], attn_grad_all[m], 0, 0) for m in micros)
    out_sum = reduce_wide(out_grad, 2)
    input_grad = sum(dot32(normed_one_all[m], stacked[m], 0, 0) for m in micros)
    input_sum = reduce_wide(input_grad, 4)
    stack_bias = sum(jnp.sum(stacked[m].astype(jnp.float32), axis=0) for m in micros)

    grad_rows = []
    vectors = None
    for m in micros:
        grad_rows.append(
            resid_grad[m] + norm_back(normed_one_grad[m], hat_one[m], inv_one[m], gain_one)
        )
        these = jnp.stack(
            [
                jnp.sum(normed_one_grad[m] * hat_one[m], axis=0),
                jnp.sum(normed_one_grad[m], axis=0),
                jnp.sum(resid_grad[m], axis=0),
                jnp.sum(normed_two_grad[m] * hat_two[m], axis=0),
                jnp.sum(normed_two_grad[m], axis=0),
                jnp.sum(top_grad[m], axis=0),
            ]
        )
        vectors = these if vectors is None else vectors + these
    vectors = butterfly(vectors, "narrow")
    packed = jnp.concatenate(
        [vectors.reshape(-1), stack_bias[:head_local], stack_bias[2 * head_local :], up_bias_grad]
    )
    packed = butterfly(packed, "wide")
    vector_sums = packed[: 6 * model].reshape(6, model)
    tail = packed[6 * model :]
    return (
        jnp.stack(out_rows)[:, None],
        jnp.stack(grad_rows)[:, None],
        vector_sums[0],
        vector_sums[1],
        input_sum.reshape(model, 3, head_local),
        tail[:head_local],
        tail[head_local : 2 * head_local],
        out_sum,
        vector_sums[2],
        vector_sums[3],
        vector_sums[4],
        up_sum,
        tail[2 * head_local :],
        down_sum,
        vector_sums[5],
    )


def solution(mesh):
    in_specs = (
        P(None, "wide", "narrow", None),
        P(None, "wide", "narrow", None),
        P(),
        P(),
        P(),
        P(),
        P(None, None, "narrow"),
        P("narrow"),
        P("narrow"),
        P("narrow", None),
        P(),
        P(),
        P(),
        P(None, "narrow"),
        P("narrow"),
        P("narrow", None),
        P(),
    )
    out_specs = (
        P(None, "wide", "narrow", None),
        P(None, "wide", "narrow", None),
        P(),
        P(),
        P(None, None, "narrow"),
        P("narrow"),
        P("narrow"),
        P("narrow", None),
        P(),
        P(),
        P(),
        P(None, "narrow"),
        P("narrow"),
        P("narrow", None),
        P(),
    )
    return jax.shard_map(local, mesh=mesh, in_specs=in_specs, out_specs=out_specs, check_vma=False)
```

time: 1290 us -> 1400 us (1.085)
  starting transfers between devices: 1.71 us -> 234 us
  waiting for transfers between devices: 827 us -> 667 us
  other arithmetic: 65.9 us -> 161 us
  blocking collectives: 82.6 us -> 0 us
  local copies, waits for them, and re-layouts: 77.1 us -> 111 us
    ppermute x0 -> x249, waiting for transfers between devices: none -> 667 us  [the longest x98 240 us: ring_sum(): carried = lax.ppermute(carried, 'wide', perm)]
    psum x1 -> x0, waiting for transfers between devices: 506 us -> none  [local(): lax.psum((totals_acc[0], totals_acc[1], totals_acc[2], totals_acc[3], tot...]
    ppermute x0 -> x249, starting transfers between devices: none -> 234 us  [the longest x98 108 us: ring_sum(): carried = lax.ppermute(carried, 'wide', perm)]
    reduce_scatter x8 -> x0, waiting for transfers between devices: 174 us -> none  [the longest x2 68.3 us: local(): lax.psum_scatter(jnp.dot(attended, out_weight, preferred_element_type=jnp...]
    all_gather x8 -> x0, waiting for transfers between devices: 145 us -> none  [the longest x2 53.9 us: local(): normed_all = lax.all_gather(normed_one, 'narrow', axis=0, tiled=True)]
    dynamic_update_slice x0 -> x112, other arithmetic: none -> 86.6 us  [reduce_wide(): lax.dynamic_update_slice(total, piece.astype(jnp.float32)[None, None], (i...]
    psum x2 -> x0, blocking collectives: 82.6 us -> none  [the longest x1 43.6 us: local(): lax.psum((vector_acc[0], vector_acc[1], vector_acc[2], vector_acc[3], vec...]
    dot_general x24 -> x32, matrix products: 141 us -> 110 us  [dot32(): lax.dot_general(first, second, (((first_dim,), (second_dim,)), ((), ())),...]
  transfers between devices with their start and end apart: 17 -> 249, of which waited for: 14 -> 183; matrix products, arithmetic and copies ran while one was open for 14% -> 19% of each run, Pallas kernels for 0% -> 0%
where the time goes in v1:
time: 1400 us; the launch traced here: 1390 us
  waiting for transfers between devices  667 us (48%)
  starting transfers between devices  234 us (17%)
  matrix products  215 us (15%)
  other arithmetic  161 us (12%)
  local copies, waits for them, and re-layouts  111 us (8%)
    ppermute x98, waiting for transfers between devices, ring_sum(): carried = lax.ppermute(carried, 'wide', perm)  240 us
    ppermute x98, waiting for transfers between devices, ring_sum(): arrived = lax.ppermute(carried, 'wide', perm)  236 us
    ppermute x48, waiting for transfers between devices, narrow_swap(): lax.ppermute(values, 'narrow', [(i, i ^ bit) for i in range(lax.axis_size...  187 us
    dot_general x32, matrix products, dot32(): lax.dot_general(first, second, (((first_dim,), (second_dim,)), ((), ())),...  110 us
    ppermute x98, starting transfers between devices, ring_sum(): carried = lax.ppermute(carried, 'wide', perm)  108 us
    ppermute x98, starting transfers between devices, ring_sum(): arrived = lax.ppermute(carried, 'wide', perm)  91.7 us
    dynamic_update_slice x112, other arithmetic, reduce_wide(): lax.dynamic_update_slice(total, piece.astype(jnp.float32)[None, None], (i...  86.6 us
    dot_general x8, matrix products, one_block(): jnp.einsum('qhe,khe->hqk', query_block, key_rows, preferred_element_type=...  28.8 us
  transfers between devices with their start and end apart: 249, of which 183 were waited for; matrix products, arithmetic and copies ran while one was open for 19% of the time, Pallas kernels for 0%

profile of v1, /device:TPU:0, one launch (start us, length us, event | category | flops | bytes accessed | tf_op | source)
XLA Modules:
  0.0 1394.8 jit_solution(189124205359286980)
XLA Ops:
  11.0 15.0 %collective-permute-done.1 = bf16[256,1280]{1,0:T(8,128)(2,1)} collective-permute-done((bf16[256,1280]{1,0:T(8,128)(2,1)}, bf16[256,1280]{1,0:T(8,128)(2,1)}, u32[]{:S(2)}, u32[]{:S(2)}) %collective-permute-start.1) | collective-permute-done | bytes 655392 | tf_op jit(solution)/shard_map/ppermute | solution.py:103
  28.4 5.2 fusion.145
  42.0 17.8 %while.60 = (s32[]{:T(128)}, bf16[2,512,5,64]{1,3,2,0:T(8,128)(2,1)}, f32[2,5,512,1]{2,1,3,0:T(8,128)S(1)}, f32[2,5,512,1]{2,1,3,0:T(8,128)S(1)}, bf16[2,512,5,6...) while((s32[]{:T(128)}, ...), condition=%wide.region_5.6_spmd, body=%wide.region_2.5_spmd.sunk | while | flops 694676480 | bytes 36490356 | solution.py:49
  67.3 15.0 %collective-permute-done.5 = bf16[256,1280]{1,0:T(8,128)(2,1)S(1)} collective-permute-done((bf16[256,1280]{1,0:T(8,128)(2,1)S(1)}, bf16[256,1280]{1,0:T(8,128)(2,1)S(1)}, u32[]{:S(2)}, u32[]{:S(2)}) %collective-permute-start.5) | collective-permute-done | bytes 655392 | tf_op jit(solution)/shard_map/ppermute | solution.py:103
  94.0 9.0 collective-permute-done.7
  103.5 11.7 collective-permute-done.25
  115.3 7.1 multiply_convert_fusion.3
  124.8 7.7 convert_reduce_fusion.1
  141.7 15.3 %collective-permute-done.11 = bf16[256,1280]{1,0:T(8,128)(2,1)S(1)} collective-permute-done((bf16[256,1280]{1,0:T(8,128)(2,1)S(1)}, bf16[256,1280]{1,0:T(8,128)(2,1)S(1)}, u32[]{:S(2)}, u32[]{:S(2)}) %collective-permute-start.11) | collective-permute-done | bytes 655392 | tf_op jit(solution)/shard_map/ppermute | solution.py:103
  157.0 13.4 collective-permute-done.29
  177.8 14.7 %collective-permute-done.31 = bf16[256,1280]{1,0:T(8,128)(2,1)} collective-permute-done((bf16[256,1280]{1,0:T(8,128)(2,1)}, bf16[256,1280]{1,0:T(8,128)(2,1)}, u32[]{:S(2)}, u32[]{:S(2)}) %collective-permute-start.31) | collective-permute-done | bytes 655392 | tf_op jit(solution)/shard_map/ppermute | solution.py:103
  204.6 53.9 %while.62 = (s32[]{:T(128)}, f32[1024,5,64]{0,2,1:T(8,128)}, f32[1024,5,64]{0,2,1:T(8,128)}, bf16[2,512,5,64]{1,3,2,0:T(8,128)(2,1)}, bf16[2,512,5,64]{1,3,2,0:T...) while((s32[]{:T(128)}, f32[1024,5,64]{0,2,1:T(8,128)}, ...), condition=%wide.region_22.23_spmd.clone, body=%wide.region_20.22_spmd.clone.sunk | while | flops 1703114240 | bytes 200636240 | solution.py:92
  208.0 4.4 multiply_reduce_fusion.20
  219.6 4.8 fusion.400
  224.4 4.3 fusion.402
  233.8 4.4 multiply_reduce_fusion.20
  245.3 5.2 fusion.400
  250.5 4.3 fusion.402
  269.0 15.0 %collective-permute-done.35 = bf16[256,1280]{1,0:T(8,128)(2,1)S(1)} collective-permute-done((bf16[256,1280]{1,0:T(8,128)(2,1)S(1)}, bf16[256,1280]{1,0:T(8,128)(2,1)S(1)}, u32[]{:S(2)}, u32[]{:S(2)}) %collective-permute-start.35) | collective-permute-done | bytes 655392 | tf_op jit(solution)/shard_map/ppermute | solution.py:103
  289.4 14.5 %collective-permute-done.13 = bf16[256,1280]{1,0:T(8,128)(2,1)} collective-permute-done((bf16[256,1280]{1,0:T(8,128)(2,1)}, bf16[256,1280]{1,0:T(8,128)(2,1)}, u32[]{:S(2)}, u32[]{:S(2)}) %collective-permute-start.13) | collective-permute-done | bytes 655392 | tf_op jit(solution)/shard_map/ppermute | solution.py:103
  306.3 5.2 fusion.143
  319.7 18.1 %while.61 = (s32[]{:T(128)}, bf16[2,512,5,64]{1,3,2,0:T(8,128)(2,1)}, f32[2,5,512,1]{2,1,3,0:T(8,128)S(1)}, f32[2,5,512,1]{2,1,3,0:T(8,128)S(1)}, bf16[2,512,5,6...) while((s32[]{:T(128)}, ...), condition=%wide.region_13.14_spmd, body=%wide.region_10.13_spmd.sunk | while | flops 694676480 | bytes 36490356 | solution.py:49
  345.3 15.0 %collective-permute-done.17 = bf16[256,1280]{1,0:T(8,128)(2,1)S(1)} collective-permute-done((bf16[256,1280]{1,0:T(8,128)(2,1)S(1)}, bf16[256,1280]{1,0:T(8,128)(2,1)S(1)}, u32[]{:S(2)}, u32[]{:S(2)}) %collective-permute-start.17) | collective-permute-done | bytes 655392 | tf_op jit(solution)/shard_map/ppermute | solution.py:103
  365.1 16.0 %collective-permute-done.19 = bf16[256,1280]{1,0:T(8,128)(2,1)} collective-permute-done((bf16[256,1280]{1,0:T(8,128)(2,1)}, bf16[256,1280]{1,0:T(8,128)(2,1)}, u32[]{:S(2)}, u32[]{:S(2)}) %collective-permute-start.19) | collective-permute-done | bytes 655392 | tf_op jit(solution)/shard_map/ppermute | solution.py:103
  383.7 9.6 collective-permute-done.37
  399.6 7.4 multiply_convert_fusion.2
  407.0 7.7 convert_reduce_fusion
  422.4 5.4 fusion.139
  436.3 5.3 fusion.140
  441.6 4.9 fusion.68
  466.7 4.8 collective-permute-done.222
  471.9 4.3 collective-permute-done.194
  481.2 5.3 collective-permute-done.166
  491.6 4.5 collective-permute-done.138
  506.3 4.3 collective-permute-done.223
  521.0 4.6 collective-permute-done.167
  530.3 4.6 collective-permute-done.139
  544.4 4.5 collective-permute-done.224
  549.1 4.5 collective-permute-done.196
  558.4 4.5 collective-permute-done.168
  567.7 4.5 collective-permute-done.140
  581.9 5.3 collective-permute-done.225
  587.4 4.8 collective-permute-done.197
  606.7 5.1 collective-permute-done.141
  621.6 5.0 collective-permute-done.226
  627.5 4.3 collective-permute-done.198
  637.5 4.5 collective-permute-done.170
  683.3 4.8 collective-permute-done.202
  716.9 7.8 collective-permute-done.23
  814.6 6.4 collective-permute-done.43
  875.8 53.5 %while.63 = (s32[]{:T(128)}, f32[1024,5,64]{0,2,1:T(8,128)}, f32[1024,5,64]{0,2,1:T(8,128)}, bf16[2,512,5,64]{1,3,2,0:T(8,128)(2,1)}, bf16[2,512,5,64]{1,3,2,0:T...) while((s32[]{:T(128)}, f32[1024,5,64]{0,2,1:T(8,128)}, ...), condition=%wide.region_31.32_spmd.clone, body=%wide.region_29.31_spmd.clone.sunk | while | flops 1703114240 | bytes 200636240 | solution.py:92
  878.7 4.4 multiply_reduce_fusion.21
  890.2 4.8 fusion.413
  895.0 4.3 fusion.415
  904.5 4.4 multiply_reduce_fusion.21
  916.0 5.2 fusion.413
  921.2 4.3 fusion.415
  947.8 5.1 fusion.142
  952.9 5.9 add_convert_fusion
  958.8 4.4 copy.108
  989.3 4.3 collective-permute-done.233
  1043.7 4.5 collective-permute-done.69
  1376.1 9.6 reshape_reshape.21
  1385.7 9.0 copy.113
  (1163 shorter events, 971.4 us)
Async XLA Ops:
  8.0 18.0 %collective-permute-start.1 = (bf16[256,1280]{1,0:T(8,128)(2,1)}, bf16[256,1280]{1,0:T(8,128)(2,1)}, u32[]{:S(2)}, u32[]{:S(2)}) collective-permute-start(bf16[256,1280]{1,0:T(8,128)(2,1)} %fusion.109), channel_id=1, source_target_pairs={{0,2},{1,3},{2,0},{3,1},{4,6},{5,7},{6,4},{7,5},{8,10},{9,11},{10,... | collective-permute-start | bytes 1966088 | tf_op jit(solution)/shard_map/ppermute | solution.py:103
  11.0 15.1 %collective-permute-start = (bf16[256,1280]{1,0:T(8,128)(2,1)}, bf16[256,1280]{1,0:T(8,128)(2,1)}, u32[]{:S(2)}, u32[]{:S(2)}) collective-permute-start(bf16[256,1280]{1,0:T(8,128)(2,1)} %fusion.109), channel_id=1, source_target_pairs={{0,1},{1,0},{2,3},{3,2},{4,5},{5,4},{6,7},{7,6},{8,9},{9,8},{10,11... | collective-permute-start | bytes 1966088 | tf_op jit(solution)/shard_map/ppermute | solution.py:103
  65.4 16.8 %collective-permute-start.5 = (bf16[256,1280]{1,0:T(8,128)(2,1)S(1)}, bf16[256,1280]{1,0:T(8,128)(2,1)S(1)}, u32[]{:S(2)}, u32[]{:S(2)}) collective-permute-start(bf16[256,1280]{1,0:T(8,128)(2,1)S(1)} %add_convert_fusion.12), channel_id=1, source_target_pairs={{0,2},{1,3},{2,0},{3,1},{4,6},{5,7},{6,4},{7,5},{8,10},{9,11},{10,... | collective-permute-start | bytes 1966088 | tf_op jit(solution)/shard_map/ppermute | solution.py:103
  85.0 18.0 %collective-permute-start.7 = (bf16[256,1280]{1,0:T(8,128)(2,1)}, bf16[256,1280]{1,0:T(8,128)(2,1)}, u32[]{:S(2)}, u32[]{:S(2)}) collective-permute-start(bf16[256,1280]{1,0:T(8,128)(2,1)} %add_convert_fusion.11), channel_id=1, source_target_pairs={{0,2},{1,3},{2,0},{3,1},{4,6},{5,7},{6,4},{7,5},{8,10},{9,11},{10,... | collective-permute-start | bytes 1966088 | tf_op jit(solution)/shard_map/ppermute | solution.py:103
  93.7 21.5 %collective-permute-start.25 = (bf16[256,1280]{1,0:T(8,128)(2,1)S(1)}, bf16[256,1280]{1,0:T(8,128)(2,1)S(1)}, u32[]{:S(2)}, u32[]{:S(2)}) collective-permute-start(bf16[256,1280]{1,0:T(8,128)(2,1)S(1)} %get-tuple-element.564), channel_id=1, source_target_pairs={{0,2},{1,3},{2,0},{3,1},{4,6},{5,7},{6,4},{7,5},{8,10},{9,11},{10,... | collective-permute-start | bytes 1966088 | tf_op jit(solution)/shard_map/ppermute | solution.py:103
  94.0 21.2 %collective-permute-start.6 = (bf16[256,1280]{1,0:T(8,128)(2,1)}, bf16[256,1280]{1,0:T(8,128)(2,1)S(1)}, u32[]{:S(2)}, u32[]{:S(2)}) collective-permute-start(bf16[256,1280]{1,0:T(8,128)(2,1)} %add_convert_fusion.11), channel_id=1, source_target_pairs={{0,1},{1,0},{2,3},{3,2},{4,5},{5,4},{6,7},{7,6},{8,9},{9,8},{10,11... | collective-permute-start | bytes 1966088 | tf_op jit(solution)/shard_map/ppermute | solution.py:103
  103.0 12.2 collective-permute-start.8
  103.0 21.7 %collective-permute-start.24 = (bf16[256,1280]{1,0:T(8,128)(2,1)S(1)}, bf16[256,1280]{1,0:T(8,128)(2,1)S(1)}, u32[]{:S(2)}, u32[]{:S(2)}) collective-permute-start(bf16[256,1280]{1,0:T(8,128)(2,1)S(1)} %get-tuple-element.564), channel_id=1, source_target_pairs={{0,1},{1,0},{2,3},{3,2},{4,5},{5,4},{6,7},{7,6},{8,9},{9,8},{10,11... | collective-permute-start | bytes 1966088 | tf_op jit(solution)/shard_map/ppermute | solution.py:103
  115.2 9.5 collective-permute-start.26
  124.4 14.9 %collective-permute-start.10 = (bf16[256,1280]{1,0:T(8,128)(2,1)S(1)}, bf16[256,1280]{1,0:T(8,128)(2,1)S(1)}, u32[]{:S(2)}, u32[]{:S(2)}) collective-permute-start(bf16[256,1280]{1,0:T(8,128)(2,1)S(1)} %slice.484), channel_id=1, source_target_pairs={{0,1},{1,0},{2,3},{3,2},{4,5},{5,4},{6,7},{7,6},{8,9},{9,8},{10,11... | collective-permute-start | bytes 1966088 | tf_op jit(solution)/shard_map/ppermute | solution.py:103
  139.4 17.6 %collective-permute-start.11 = (bf16[256,1280]{1,0:T(8,128)(2,1)S(1)}, bf16[256,1280]{1,0:T(8,128)(2,1)S(1)}, u32[]{:S(2)}, u32[]{:S(2)}) collective-permute-start(bf16[256,1280]{1,0:T(8,128)(2,1)S(1)} %add_convert_fusion.10), channel_id=1, source_target_pairs={{0,2},{1,3},{2,0},{3,1},{4,6},{5,7},{6,4},{7,5},{8,10},{9,11},{10,... | collective-permute-start | bytes 1966088 | tf_op jit(solution)/shard_map/ppermute | solution.py:103
  141.3 29.1 %collective-permute-start.29 = (bf16[256,1280]{1,0:T(8,128)(2,1)S(1)}, bf16[256,1280]{1,0:T(8,128)(2,1)S(1)}, u32[]{:S(2)}, u32[]{:S(2)}) collective-permute-start(bf16[256,1280]{1,0:T(8,128)(2,1)S(1)} %add_convert_fusion.4), channel_id=1, source_target_pairs={{0,2},{1,3},{2,0},{3,1},{4,6},{5,7},{6,4},{7,5},{8,10},{9,11},{10,... | collective-permute-start | bytes 1966088 | tf_op jit(solution)/shard_map/ppermute | solution.py:103
  176.1 16.4 %collective-permute-start.31 = (bf16[256,1280]{1,0:T(8,128)(2,1)}, bf16[256,1280]{1,0:T(8,128)(2,1)}, u32[]{:S(2)}, u32[]{:S(2)}) collective-permute-start(bf16[256,1280]{1,0:T(8,128)(2,1)} %convert_element_type.1734), channel_id=1, source_target_pairs={{0,2},{1,3},{2,0},{3,1},{4,6},{5,7},{6,4},{7,5},{8,10},{9,11},{10,... | collective-permute-start | bytes 1966088 | tf_op jit(solution)/shard_map/ppermute | solution.py:103
  177.8 14.7 %collective-permute-start.30 = (bf16[256,1280]{1,0:T(8,128)(2,1)}, bf16[256,1280]{1,0:T(8,128)(2,1)}, u32[]{:S(2)}, u32[]{:S(2)}) collective-permute-start(bf16[256,1280]{1,0:T(8,128)(2,1)} %convert_element_type.1734), channel_id=1, source_target_pairs={{0,1},{1,0},{2,3},{3,2},{4,5},{5,4},{6,7},{7,6},{8,9},{9,8},{10,11... | collective-permute-start | bytes 1966088 | tf_op jit(solution)/shard_map/ppermute | solution.py:103
  267.1 16.9 %collective-permute-start.35 = (bf16[256,1280]{1,0:T(8,128)(2,1)S(1)}, bf16[256,1280]{1,0:T(8,128)(2,1)S(1)}, u32[]{:S(2)}, u32[]{:S(2)}) collective-permute-start(bf16[256,1280]{1,0:T(8,128)(2,1)S(1)} %add_convert_fusion.3), channel_id=1, source_target_pairs={{0,2},{1,3},{2,0},{3,1},{4,6},{5,7},{6,4},{7,5},{8,10},{9,11},{10,... | collective-permute-start | bytes 1966088 | tf_op jit(solution)/shard_map/ppermute | solution.py:103
  287.6 16.3 %collective-permute-start.13 = (bf16[256,1280]{1,0:T(8,128)(2,1)}, bf16[256,1280]{1,0:T(8,128)(2,1)}, u32[]{:S(2)}, u32[]{:S(2)}) collective-permute-start(bf16[256,1280]{1,0:T(8,128)(2,1)} %get-tuple-element.563), channel_id=1, source_target_pairs={{0,2},{1,3},{2,0},{3,1},{4,6},{5,7},{6,4},{7,5},{8,10},{9,11},{10,... | collective-permute-start | bytes 1966088 | tf_op jit(solution)/shard_map/ppermute | solution.py:103
  289.4 14.6 %collective-permute-start.12 = (bf16[256,1280]{1,0:T(8,128)(2,1)}, bf16[256,1280]{1,0:T(8,128)(2,1)}, u32[]{:S(2)}, u32[]{:S(2)}) collective-permute-start(bf16[256,1280]{1,0:T(8,128)(2,1)} %get-tuple-element.563), channel_id=1, source_target_pairs={{0,1},{1,0},{2,3},{3,2},{4,5},{5,4},{6,7},{7,6},{8,9},{9,8},{10,11... | collective-permute-start | bytes 1966088 | tf_op jit(solution)/shard_map/ppermute | solution.py:103
  343.5 16.8 %collective-permute-start.17 = (bf16[256,1280]{1,0:T(8,128)(2,1)S(1)}, bf16[256,1280]{1,0:T(8,128)(2,1)S(1)}, u32[]{:S(2)}, u32[]{:S(2)}) collective-permute-start(bf16[256,1280]{1,0:T(8,128)(2,1)S(1)} %add_convert_fusion.8), channel_id=1, source_target_pairs={{0,2},{1,3},{2,0},{3,1},{4,6},{5,7},{6,4},{7,5},{8,10},{9,11},{10,... | collective-permute-start | bytes 1966088 | tf_op jit(solution)/shard_map/ppermute | solution.py:103
  363.1 18.0 %collective-permute-start.19 = (bf16[256,1280]{1,0:T(8,128)(2,1)}, bf16[256,1280]{1,0:T(8,128)(2,1)}, u32[]{:S(2)}, u32[]{:S(2)}) collective-permute-start(bf16[256,1280]{1,0:T(8,128)(2,1)} %add_convert_fusion.7), channel_id=1, source_target_pairs={{0,2},{1,3},{2,0},{3,1},{4,6},{5,7},{6,4},{7,5},{8,10},{9,11},{10,... | collective-permute-start | bytes 1966088 | tf_op jit(solution)/shard_map/ppermute | solution.py:103
  364.8 28.6 %collective-permute-start.37 = (bf16[256,1280]{1,0:T(8,128)(2,1)}, bf16[256,1280]{1,0:T(8,128)(2,1)}, u32[]{:S(2)}, u32[]{:S(2)}) collective-permute-start(bf16[256,1280]{1,0:T(8,128)(2,1)} %get-tuple-element.565), channel_id=1, source_target_pairs={{0,2},{1,3},{2,0},{3,1},{4,6},{5,7},{6,4},{7,5},{8,10},{9,11},{10,... | collective-permute-start | bytes 1966088 | tf_op jit(solution)/shard_map/ppermute | solution.py:103
  365.1 34.5 %collective-permute-start.18 = (bf16[256,1280]{1,0:T(8,128)(2,1)}, bf16[256,1280]{1,0:T(8,128)(2,1)}, u32[]{:S(2)}, u32[]{:S(2)}) collective-permute-start(bf16[256,1280]{1,0:T(8,128)(2,1)} %add_convert_fusion.7), channel_id=1, source_target_pairs={{0,1},{1,0},{2,3},{3,2},{4,5},{5,4},{6,7},{7,6},{8,9},{9,8},{10,11... | collective-permute-start | bytes 1966088 | tf_op jit(solution)/shard_map/ppermute | solution.py:103
  381.0 18.5 %collective-permute-start.20 = (bf16[256,1280]{1,0:T(8,128)(2,1)}, bf16[256,1280]{1,0:T(8,128)(2,1)}, u32[]{:S(2)}, u32[]{:S(2)}) collective-permute-start(bf16[256,1280]{1,0:T(8,128)(2,1)} %collective-permute-done.19), channel_id=1, source_target_pairs={{0,1},{1,0},{2,3},{3,2},{4,5},{5,4},{6,7},{7,6},{8,9},{9,8},{10,11... | collective-permute-start | bytes 1966088 | tf_op jit(solution)/shard_map/ppermute | solution.py:103
  381.0 26.0 %collective-permute-start.36 = (bf16[256,1280]{1,0:T(8,128)(2,1)}, bf16[256,1280]{1,0:T(8,128)(2,1)}, u32[]{:S(2)}, u32[]{:S(2)}) collective-permute-start(bf16[256,1280]{1,0:T(8,128)(2,1)} %get-tuple-element.565), channel_id=1, source_target_pairs={{0,1},{1,0},{2,3},{3,2},{4,5},{5,4},{6,7},{7,6},{8,9},{9,8},{10,11... | collective-permute-start | bytes 1966088 | tf_op jit(solution)/shard_map/ppermute | solution.py:103
  393.4 13.7 collective-permute-start.38
  431.7 18.2 %collective-permute-start.235 = (bf16[40,1280]{1,0:T(8,128)(2,1)S(1)}, bf16[40,1280]{1,0:T(8,128)(2,1)S(1)}, u32[]{:S(2)}, u32[]{:S(2)}) collective-permute-start(bf16[40,1280]{1,0:T(8,128)(2,1)S(1)} %dynamic-slice_bitcast_fusion.4), channel_id=1, source_target_pairs={{0,4},{8,0},{16,8},{24,16},{28,24},{20,28},{12,20},{4,12},{1,5},{9... | collective-permute-start | bytes 307208 | tf_op jit(solution)/shard_map/ppermute | solution.py:140
  433.7 18.4 %collective-permute-start.221 = (bf16[40,1280]{1,0:T(8,128)(2,1)S(1)}, bf16[40,1280]{1,0:T(8,128)(2,1)S(1)}, u32[]{:S(2)}, u32[]{:S(2)}) collective-permute-start(bf16[40,1280]{1,0:T(8,128)(2,1)S(1)} %dynamic-slice_bitcast_fusion.5), channel_id=1, source_target_pairs={{0,8},{8,16},{16,24},{24,28},{28,20},{20,12},{12,4},{4,0},{1,9},{9... | collective-permute-start | bytes 307208 | tf_op jit(solution)/shard_map/ppermute | solution.py:140
  434.1 16.2 %collective-permute-start.207 = (bf16[40,1280]{1,0:T(8,128)(2,1)S(1)}, bf16[40,1280]{1,0:T(8,128)(2,1)S(1)}, u32[]{:S(2)}, u32[]{:S(2)}) collective-permute-start(bf16[40,1280]{1,0:T(8,128)(2,1)S(1)} %dynamic-slice_bitcast_fusion.6), channel_id=1, source_target_pairs={{0,4},{8,0},{16,8},{24,16},{28,24},{20,28},{12,20},{4,12},{1,5},{9... | collective-permute-start | bytes 307208 | tf_op jit(solution)/shard_map/ppermute | solution.py:140
  435.9 16.6 %collective-permute-start.193 = (bf16[40,1280]{1,0:T(8,128)(2,1)S(1)}, bf16[40,1280]{1,0:T(8,128)(2,1)S(1)}, u32[]{:S(2)}, u32[]{:S(2)}) collective-permute-start(bf16[40,1280]{1,0:T(8,128)(2,1)S(1)} %dynamic-slice_bitcast_fusion.7), channel_id=1, source_target_pairs={{0,8},{8,16},{16,24},{24,28},{28,20},{20,12},{12,4},{4,0},{1,9},{9... | collective-permute-start | bytes 307208 | tf_op jit(solution)/shard_map/ppermute | solution.py:140
  452.5 200.1 %collective-permute-start.22 = (bf16[256,1280]{1,0:T(8,128)(2,1)S(1)}, bf16[256,1280]{1,0:T(8,128)(2,1)S(1)}, u32[]{:S(2)}, u32[]{:S(2)}) collective-permute-start(bf16[256,1280]{1,0:T(8,128)(2,1)S(1)} %slice.499), channel_id=1, source_target_pairs={{0,1},{1,0},{2,3},{3,2},{4,5},{5,4},{6,7},{7,6},{8,9},{9,8},{10,11... | collective-permute-start | bytes 1966088 | tf_op jit(solution)/shard_map/ppermute | solution.py:103
  452.6 200.9 %collective-permute-start.40 = (bf16[256,1280]{1,0:T(8,128)(2,1)S(1)}, bf16[256,1280]{1,0:T(8,128)(2,1)S(1)}, u32[]{:S(2)}, u32[]{:S(2)}) collective-permute-start(bf16[256,1280]{1,0:T(8,128)(2,1)S(1)} %slice.517), channel_id=1, source_target_pairs={{0,1},{1,0},{2,3},{3,2},{4,5},{5,4},{6,7},{7,6},{8,9},{9,8},{10,11... | collective-permute-start | bytes 1966088 | tf_op jit(solution)/shard_map/ppermute | solution.py:103
  455.4 256.9 %collective-permute-start.39 = (bf16[256,1280]{1,0:T(8,128)(2,1)S(1)}, bf16[256,1280]{1,0:T(8,128)(2,1)S(1)}, u32[]{:S(2)}, u32[]{:S(2)}) collective-permute-start(bf16[256,1280]{1,0:T(8,128)(2,1)S(1)} %slice.514), channel_id=1, source_target_pairs={{0,1},{1,0},{2,3},{3,2},{4,5},{5,4},{6,7},{7,6},{8,9},{9,8},{10,11... | collective-permute-start | bytes 1966088 | tf_op jit(solution)/shard_map/ppermute | solution.py:103
  455.4 260.2 %collective-permute-start.21 = (bf16[256,1280]{1,0:T(8,128)(2,1)S(1)}, bf16[256,1280]{1,0:T(8,128)(2,1)S(1)}, u32[]{:S(2)}, u32[]{:S(2)}) collective-permute-start(bf16[256,1280]{1,0:T(8,128)(2,1)S(1)} %slice.496), channel_id=1, source_target_pairs={{0,1},{1,0},{2,3},{3,2},{4,5},{5,4},{6,7},{7,6},{8,9},{9,8},{10,11... | collective-permute-start | bytes 1966088 | tf_op jit(solution)/shard_map/ppermute | solution.py:103
  651.3 409.0 %collective-permute-start.241 = (bf16[40,1280]{1,0:T(8,128)(2,1)}, bf16[40,1280]{1,0:T(8,128)(2,1)}, u32[]{:S(2)}, u32[]{:S(2)}) collective-permute-start(bf16[40,1280]{1,0:T(8,128)(2,1)} %fusion.148), channel_id=1, source_target_pairs={{0,4},{8,0},{16,8},{24,16},{28,24},{20,28},{12,20},{4,12},{1,5},{9... | collective-permute-start | bytes 307208 | tf_op jit(solution)/shard_map/ppermute | solution.py:140
  653.6 9.7 collective-permute-start.143
  657.3 56.8 %collective-permute-start.41 = (bf16[256,1280]{1,0:T(8,128)(2,1)S(1)}, bf16[256,1280]{1,0:T(8,128)(2,1)S(1)}, u32[]{:S(2)}, u32[]{:S(2)}) collective-permute-start(bf16[256,1280]{1,0:T(8,128)(2,1)S(1)} %add_convert_fusion.2), channel_id=1, source_target_pairs={{0,2},{1,3},{2,0},{3,1},{4,6},{5,7},{6,4},{7,5},{8,10},{9,11},{10,... | collective-permute-start | bytes 1966088 | tf_op jit(solution)/shard_map/ppermute | solution.py:103
  682.1 6.0 collective-permute-start.202
  711.4 100.8 %collective-permute-start.227 = (bf16[40,1280]{1,0:T(8,128)(2,1)S(1)}, bf16[40,1280]{1,0:T(8,128)(2,1)S(1)}, u32[]{:S(2)}, u32[]{:S(2)}) collective-permute-start(bf16[40,1280]{1,0:T(8,128)(2,1)S(1)} %fusion.155), channel_id=1, source_target_pairs={{0,8},{8,16},{16,24},{24,28},{28,20},{20,12},{12,4},{4,0},{1,9},{9... | collective-permute-start | bytes 307208 | tf_op jit(solution)/shard_map/ppermute | solution.py:140
  712.3 32.7 %collective-permute-start.213 = (bf16[40,1280]{1,0:T(8,128)(2,1)S(1)}, bf16[40,1280]{1,0:T(8,128)(2,1)S(1)}, u32[]{:S(2)}, u32[]{:S(2)}) collective-permute-start(bf16[40,1280]{1,0:T(8,128)(2,1)S(1)} %fusion.162), channel_id=1, source_target_pairs={{0,4},{8,0},{16,8},{24,16},{28,24},{20,28},{12,20},{4,12},{1,5},{9... | collective-permute-start | bytes 307208 | tf_op jit(solution)/shard_map/ppermute | solution.py:140
  714.1 10.6 collective-permute-start.23
  715.7 349.3 %collective-permute-start.185 = (bf16[40,1280]{1,0:T(8,128)(2,1)}, bf16[40,1280]{1,0:T(8,128)(2,1)}, u32[]{:S(2)}, u32[]{:S(2)}) collective-permute-start(bf16[40,1280]{1,0:T(8,128)(2,1)} %fusion.176), channel_id=1, source_target_pairs={{0,4},{8,0},{16,8},{24,16},{28,24},{20,28},{12,20},{4,12},{1,5},{9... | collective-permute-start | bytes 307208 | tf_op jit(solution)/shard_map/ppermute | solution.py:140
  743.4 78.8 %collective-permute-start.171 = (bf16[40,1280]{1,0:T(8,128)(2,1)S(1)}, bf16[40,1280]{1,0:T(8,128)(2,1)S(1)}, u32[]{:S(2)}, u32[]{:S(2)}) collective-permute-start(bf16[40,1280]{1,0:T(8,128)(2,1)S(1)} %fusion.183), channel_id=1, source_target_pairs={{0,8},{8,16},{16,24},{24,28},{28,20},{20,12},{12,4},{4,0},{1,9},{9... | collective-permute-start | bytes 307208 | tf_op jit(solution)/shard_map/ppermute | solution.py:140
  810.4 10.6 collective-permute-start.43
  812.2 8.8 collective-permute-start.164
  821.0 44.0 %collective-permute-start.42 = (bf16[256,1280]{1,0:T(8,128)(2,1)S(1)}, bf16[256,1280]{1,0:T(8,128)(2,1)S(1)}, u32[]{:S(2)}, u32[]{:S(2)}) collective-permute-start(bf16[256,1280]{1,0:T(8,128)(2,1)S(1)} %convert_element_type.1756), channel_id=1, source_target_pairs={{0,1},{1,0},{2,3},{3,2},{4,5},{5,4},{6,7},{7,6},{8,9},{9,8},{10,11... | collective-permute-start | bytes 1966088 | tf_op jit(solution)/shard_map/ppermute | solution.py:103
  821.0 46.1 %collective-permute-start.44 = (bf16[256,1280]{1,0:T(8,128)(2,1)S(1)}, bf16[256,1280]{1,0:T(8,128)(2,1)S(1)}, u32[]{:S(2)}, u32[]{:S(2)}) collective-permute-start(bf16[256,1280]{1,0:T(8,128)(2,1)S(1)} %collective-permute-done.43), channel_id=1, source_target_pairs={{0,1},{1,0},{2,3},{3,2},{4,5},{5,4},{6,7},{7,6},{8,9},{9,8},{10,11... | collective-permute-start | bytes 1966088 | tf_op jit(solution)/shard_map/ppermute | solution.py:103
  861.8 105.1 %collective-permute-start.232 = (bf16[40,1280]{1,0:T(8,128)(2,1)}, bf16[40,1280]{1,0:T(8,128)(2,1)}, u32[]{:S(2)}, u32[]{:S(2)}) collective-permute-start(bf16[40,1280]{1,0:T(8,128)(2,1)} %collective-permute-done.231), channel_id=1, source_target_pairs={{0,8},{8,16},{16,24},{24,28},{28,20},{20,12},{12,4},{4,0},{1,9},{9... | collective-permute-start | bytes 307208 | tf_op jit(solution)/shard_map/ppermute | solution.py:144
  865.0 105.2 %collective-permute-start.176 = (bf16[40,1280]{1,0:T(8,128)(2,1)}, bf16[40,1280]{1,0:T(8,128)(2,1)}, u32[]{:S(2)}, u32[]{:S(2)}) collective-permute-start(bf16[40,1280]{1,0:T(8,128)(2,1)} %collective-permute-done.175), channel_id=1, source_target_pairs={{0,8},{8,16},{16,24},{24,28},{28,20},{20,12},{12,4},{4,0},{1,9},{9... | collective-permute-start | bytes 307208 | tf_op jit(solution)/shard_map/ppermute | solution.py:144
  946.8 25.3 %collective-permute-start.123 = (bf16[20,1280]{1,0:T(8,128)(2,1)S(1)}, bf16[20,1280]{1,0:T(8,128)(2,1)S(1)}, u32[]{:S(2)}, u32[]{:S(2)}) collective-permute-start(bf16[20,1280]{1,0:T(8,128)(2,1)S(1)} %dynamic-slice_bitcast_fusion.16), channel_id=1, source_target_pairs={{0,4},{8,0},{16,8},{24,16},{28,24},{20,28},{12,20},{4,12},{1,5},{9... | collective-permute-start | bytes 153608 | tf_op jit(solution)/shard_map/ppermute | solution.py:140
  966.9 6.9 collective-permute-start.109
  976.6 183.6 %collective-permute-start.46 = (bf16[256,1280]{1,0:T(8,128)(2,1)S(1)}, bf16[256,1280]{1,0:T(8,128)(2,1)S(1)}, u32[]{:S(2)}, u32[]{:S(2)}) collective-permute-start(bf16[256,1280]{1,0:T(8,128)(2,1)S(1)} %slice.523), channel_id=1, source_target_pairs={{0,1},{1,0},{2,3},{3,2},{4,5},{5,4},{6,7},{7,6},{8,9},{9,8},{10,11... | collective-permute-start | bytes 1966088 | tf_op jit(solution)/shard_map/ppermute | solution.py:103
  978.3 296.5 %collective-permute-start.45 = (bf16[256,1280]{1,0:T(8,128)(2,1)}, bf16[256,1280]{1,0:T(8,128)(2,1)}, u32[]{:S(2)}, u32[]{:S(2)}) collective-permute-start(bf16[256,1280]{1,0:T(8,128)(2,1)} %slice.520), channel_id=1, source_target_pairs={{0,1},{1,0},{2,3},{3,2},{4,5},{5,4},{6,7},{7,6},{8,9},{9,8},{10,11... | collective-permute-start | bytes 1966088 | tf_op jit(solution)/shard_map/ppermute | solution.py:103
  1060.3 6.9 collective-permute-start.127
  1064.9 12.9 collective-permute-start.98
  1067.2 12.6 collective-permute-start.84
  1082.9 91.6 %collective-permute-start.129 = (bf16[20,1280]{1,0:T(8,128)(2,1)S(1)}, bf16[20,1280]{1,0:T(8,128)(2,1)S(1)}, u32[]{:S(2)}, u32[]{:S(2)}) collective-permute-start(bf16[20,1280]{1,0:T(8,128)(2,1)S(1)} %fusion.232), channel_id=1, source_target_pairs={{0,4},{8,0},{16,8},{24,16},{28,24},{20,28},{12,20},{4,12},{1,5},{9... | collective-permute-start | bytes 153608 | tf_op jit(solution)/shard_map/ppermute | solution.py:140
  1097.8 6.5 collective-permute-start.243
  1104.3 9.5 collective-permute-start.100
  1118.3 16.3 %collective-permute-start.244 = (bf16[40,1280]{1,0:T(8,128)(2,1)S(1)}, bf16[40,1280]{1,0:T(8,128)(2,1)S(1)}, u32[]{:S(2)}, u32[]{:S(2)}) collective-permute-start(bf16[40,1280]{1,0:T(8,128)(2,1)S(1)} %collective-permute-done.243), channel_id=1, source_target_pairs={{0,4},{8,0},{16,8},{24,16},{28,24},{20,28},{12,20},{4,12},{1,5},{9... | collective-permute-start | bytes 307208 | tf_op jit(solution)/shard_map/ppermute | solution.py:144
  1134.5 207.5 %collective-permute-start.101 = (bf16[40,960]{1,0:T(8,128)(2,1)S(1)}, bf16[40,960]{1,0:T(8,128)(2,1)S(1)}, u32[]{:S(2)}, u32[]{:S(2)}) collective-permute-start(bf16[40,960]{1,0:T(8,128)(2,1)S(1)} %fusion.204), channel_id=1, source_target_pairs={{0,4},{8,0},{16,8},{24,16},{28,24},{20,28},{12,20},{4,12},{1,5},{9... | collective-permute-start | bytes 230408 | tf_op jit(solution)/shard_map/ppermute | solution.py:140
  1157.8 150.2 %collective-permute-start.87 = (bf16[40,960]{1,0:T(8,128)(2,1)}, bf16[40,960]{1,0:T(8,128)(2,1)}, u32[]{:S(2)}, u32[]{:S(2)}) collective-permute-start(bf16[40,960]{1,0:T(8,128)(2,1)} %fusion.211), channel_id=1, source_target_pairs={{0,8},{8,16},{16,24},{24,28},{28,20},{20,12},{12,4},{4,0},{1,9},{9... | collective-permute-start | bytes 230408 | tf_op jit(solution)/shard_map/ppermute | solution.py:140
  1173.8 78.7 %collective-permute-start.73 = (bf16[40,960]{1,0:T(8,128)(2,1)S(1)}, bf16[40,960]{1,0:T(8,128)(2,1)S(1)}, u32[]{:S(2)}, u32[]{:S(2)}) collective-permute-start(bf16[40,960]{1,0:T(8,128)(2,1)S(1)} %fusion.218), channel_id=1, source_target_pairs={{0,4},{8,0},{16,8},{24,16},{28,24},{20,28},{12,20},{4,12},{1,5},{9... | collective-permute-start | bytes 230408 | tf_op jit(solution)/shard_map/ppermute | solution.py:140
  1251.2 23.7 %collective-permute-start.47 = (bf16[256,1280]{1,0:T(8,128)(2,1)}, bf16[256,1280]{1,0:T(8,128)(2,1)}, u32[]{:S(2)}, u32[]{:S(2)}) collective-permute-start(bf16[256,1280]{1,0:T(8,128)(2,1)} %add_convert_fusion.1), channel_id=1, source_target_pairs={{0,2},{1,3},{2,0},{3,1},{4,6},{5,7},{6,4},{7,5},{8,10},{9,11},{10,... | collective-permute-start | bytes 1966088 | tf_op jit(solution)/shard_map/ppermute | solution.py:103
  1271.3 19.7 %collective-permute-start.77 = (bf16[40,960]{1,0:T(8,128)(2,1)}, bf16[40,960]{1,0:T(8,128)(2,1)}, u32[]{:S(2)}, u32[]{:S(2)}) collective-permute-start(bf16[40,960]{1,0:T(8,128)(2,1)} %collective-permute-done.76), channel_id=1, source_target_pairs={{0,4},{8,0},{16,8},{24,16},{28,24},{20,28},{12,20},{4,12},{1,5},{9... | collective-permute-start | bytes 230408 | tf_op jit(solution)/shard_map/ppermute | solution.py:144
  1291.0 7.4 collective-permute-start.78
  (328 other events, 3388.9 us)

commit v2 on v0

v2 whole, which is shorter than its diff:
```python
import functools

import jax
import jax.numpy as jnp
from jax import lax
from jax.experimental import pallas as pl
from jax.experimental.pallas import tpu as pltpu
from jax.sharding import PartitionSpec as P

HEAD = 64
LANES = 128
TILE = 256
norm_eps = 1e-05
score_scale = 0.125
bf16 = jnp.bfloat16
f32 = jnp.float32


class Chain:
    def __init__(self):
        self.last = None

    def run(self, body, outs, *ins, smem=(), scratch=(), alias=None, anywhere=(), out_anywhere=(), limit=32):
        ins = [*smem, *ins]
        count = len(ins)
        specs = []
        for i in range(count):
            if i < len(smem):
                specs.append(pl.BlockSpec(memory_space=pltpu.SMEM))
            elif i - len(smem) in anywhere:
                specs.append(pl.BlockSpec(memory_space=pl.ANY))
            else:
                specs.append(pl.BlockSpec(memory_space=pltpu.VMEM))
        tied = self.last is not None
        if tied:
            specs.append(pl.BlockSpec(memory_space=pl.ANY))
            ins = [*ins, self.last]

        def inner(*refs):
            body(*refs[:count], *refs[count + tied :])

        made = pl.pallas_call(
            inner,
            out_shape=tuple(jax.ShapeDtypeStruct(*o) for o in outs),
            in_specs=specs,
            out_specs=tuple(
                pl.BlockSpec(memory_space=pl.ANY if i in out_anywhere else pltpu.VMEM) for i in range(len(outs))
            ),
            scratch_shapes=scratch,
            input_output_aliases={} if alias is None else {len(smem) + k: v for k, v in alias.items()},
            compiler_params=pltpu.CompilerParams(vmem_limit_bytes=limit << 20),
            cost_estimate=pl.CostEstimate(flops=0, bytes_accessed=0, transcendentals=0),
            name=body.func.__name__ if isinstance(body, functools.partial) else body.__name__,
        )(*ins)
        self.last = made[0]
        return made


def dot32(first, second, first_dim, second_dim):
    return lax.dot_general(
        first, second, (((first_dim,), (second_dim,)), ((), ())), preferred_element_type=f32
    )


def statistics(values):
    average = jnp.mean(values, axis=-1, keepdims=True)
    centred = values - average
    inverse = lax.rsqrt(jnp.mean(centred * centred, axis=-1, keepdims=True) + norm_eps)
    return centred * inverse, inverse


def norm_back(grad, normed, inverse, gain):
    scaled = grad * gain
    mean_one = jnp.mean(scaled, axis=-1, keepdims=True)
    mean_two = jnp.mean(scaled * normed, axis=-1, keepdims=True)
    return inverse * (scaled - mean_one - normed * mean_two)


def of_head(values, j, axis=1):
    if values.shape[axis] <= HEAD:
        return values
    place = lax.broadcasted_iota(jnp.int32, values.shape, axis)
    return jnp.where((place >= HEAD * j) & (place < HEAD * (j + 1)), values, jnp.zeros_like(values))


def head_pairs(width):
    return [(low, min(LANES, width - low)) for low in range(0, width, LANES)]


def norm_one(tok, gain, bias, out, *, m):
    normed, _ = statistics(tok[m, 0].astype(f32))
    out[...] = (normed * gain[...].astype(f32) + bias[...].astype(f32)).astype(bf16)


def scale_cot(scale, cot, out, *, m):
    out[...] = (cot[m, 0].astype(f32) * scale[m]).astype(bf16)


def project(*refs, parts):
    blocks = refs[:parts]
    weight, bias, scale = refs[parts : parts + 3]
    out, whole = refs[parts + 3 :]
    rows = blocks[0].shape[0]
    for b in range(parts):
        values = blocks[b][...]
        at = slice(b * rows, (b + 1) * rows)
        whole[at, :] = values
        out[at, :] = ((dot32(values, weight[...], 1, 0) + bias[...]) * scale[...]).astype(bf16)


def attend(qkv, out_weight, attended, logs, *outs, step):
    whole = qkv.shape[0]
    head = 0
    for low, wide in head_pairs(out_weight.shape[0]):
        heads = wide // HEAD
        key_pair = qkv[:, 3 * low + wide : 3 * low + 2 * wide]
        value_t = qkv[:, 3 * low + 2 * wide : 3 * low + 3 * wide].T
        keys = [of_head(key_pair, j) for j in range(heads)]
        values = [of_head(value_t, j, 0) for j in range(heads)]

        def block(i, carry, low=low, wide=wide, keys=keys, values=values, head=head):
            start = pl.multiple_of(i * step, step)
            query = qkv[pl.ds(start, step), 3 * low : 3 * low + wide]
            total = None
            for j in range(len(keys)):
                scores = dot32(keys[j], query, 1, 1)
                top = jnp.max(scores, axis=0, keepdims=True)
                powers = jnp.exp(scores - top)
                length = jnp.sum(powers, axis=0, keepdims=True)
                mixed = dot32(values[j], powers.astype(bf16), 1, 0) * (1.0 / length)
                total = mixed if total is None else total + mixed
                logs[head + j : head + j + 1, pl.ds(start, step)] = top + jnp.log(length)
            attended[pl.ds(start, step), low : low + wide] = total.T.astype(bf16)
            return carry

        lax.fori_loop(0, whole // step, block, 0)
        head += heads
    rows = whole // len(outs)
    for b in range(len(outs)):
        outs[b][...] = dot32(attended[b * rows : (b + 1) * rows, :], out_weight[...], 1, 0).astype(bf16)


def pair_sum(first, second, out):
    out[...] = (first[...].astype(f32) + second[...].astype(f32)).astype(bf16)


def three(first, second, third):
    return first[...].astype(f32) + second[...].astype(f32) + third[...].astype(f32)


def norm_two(tok, first, second, third, out_bias, gain, bias, resid, normed, *, m):
    value = tok[m, 0].astype(f32) + three(first, second, third) + out_bias[...].astype(f32)
    resid[...] = value
    hat, _ = statistics(value)
    normed[...] = (hat * gain[...].astype(f32) + bias[...].astype(f32)).astype(bf16)


def feed(*refs, parts):
    normed, grads = refs[:parts], refs[parts : 2 * parts]
    up, up_bias, down = refs[2 * parts : 2 * parts + 3]
    activ, pre_grad, bias_grad, normed_all, grads_all = refs[2 * parts + 3 :]
    rows = normed[0].shape[0]
    for b in range(parts):
        normed_all[b * rows : (b + 1) * rows, :] = normed[b][...]
        grads_all[b * rows : (b + 1) * rows, :] = grads[b][...]

    def tile(i, carry):
        cols = pl.ds(pl.multiple_of(i * TILE, TILE), TILE)
        total = None
        for b in range(parts):
            at = slice(b * rows, (b + 1) * rows)
            pre = dot32(normed[b][...], up[:, cols], 1, 0) + up_bias[:, cols].astype(f32)
            cumul = 0.5 + 0.5 * lax.erf(pre * 0.7071067811865476)
            density = jnp.exp(-0.5 * pre * pre) * 0.3989422804014327
            activ[at, cols] = (pre * cumul).astype(bf16)
            back = dot32(grads[b][...], down[cols, :], 1, 1)
            grad = (back * (cumul + pre * density)).astype(bf16)
            pre_grad[at, cols] = grad
            part = jnp.sum(grad.astype(f32), axis=0, keepdims=True)
            total = part if total is None else total + part
        bias_grad[:, cols] = total
        return carry

    lax.fori_loop(0, up.shape[1] // TILE, tile, 0)


def times(value, weight, *outs):
    rows = outs[0].shape[0]

    def tile(i, carry):
        cols = pl.ds(pl.multiple_of(i * TILE, TILE), TILE)
        for b in range(len(outs)):
            outs[b][:, cols] = dot32(value[b * rows : (b + 1) * rows, :], weight[:, cols], 1, 0).astype(bf16)
        return carry

    lax.fori_loop(0, weight.shape[1] // TILE, tile, 0)


def times_back(value, weight, *outs):
    rows = outs[0].shape[0]

    def tile(i, carry):
        cols = pl.ds(pl.multiple_of(i * TILE, TILE), TILE)
        for b in range(len(outs)):
            outs[b][:, cols] = dot32(value[b * rows : (b + 1) * rows, :], weight[cols, :], 1, 1).astype(bf16)
        return carry

    lax.fori_loop(0, weight.shape[0] // TILE, tile, 0)


def weight_grad(place, *refs, count, pairs, ring):
    firsts, seconds = refs[:pairs], refs[pairs : 2 * pairs]
    out, chunk = refs[2 * pairs :]

    def tile(i, carry):
        rows = pl.ds(pl.multiple_of(i * TILE, TILE), TILE)
        total = None
        for first, second in zip(firsts, seconds):
            part = dot32(first[:, rows], second[...], 0, 0)
            total = part if total is None else total + part
        out[rows, :] = total.astype(bf16)
        return carry

    lax.fori_loop(0, out.shape[0] // TILE, tile, 0)
    chunk[...] = out[chunk_rows(place[ring], count, out), :]


def chunk_rows(index, count, ref):
    size = ref.shape[0] // count
    return pl.ds(pl.multiple_of(index * size, size), size)


def norm_two_back(scale, cot, resid, first, second, third, gain, out, rounded, sums, *, m):
    top = cot[m, 0].astype(f32) * scale[m]
    grad = three(first, second, third)
    hat, inverse = statistics(resid[...])
    back = top + norm_back(grad, hat, inverse, gain[...].astype(f32))
    out[...] = back
    rounded[...] = back.astype(bf16)
    sums[0:1, :] = jnp.sum(back, axis=0, keepdims=True)
    sums[1:2, :] = jnp.sum(grad * hat, axis=0, keepdims=True)
    sums[2:3, :] = jnp.sum(grad, axis=0, keepdims=True)
    sums[3:4, :] = jnp.sum(top, axis=0, keepdims=True)
    sums[4:8, :] = jnp.zeros_like(sums[4:8, :])


def attend_back(qkv, logs, out_weight, *refs, parts, step, low, wide):
    grads = refs[:parts]
    out, key_grad, value_grad, given = refs[parts:]
    whole = qkv.shape[0]
    rows = whole // parts
    for b in range(parts):
        given[b * rows : (b + 1) * rows, :] = dot32(
            grads[b][...], out_weight[low : low + wide, :], 1, 1
        ).astype(bf16)
    heads = wide // HEAD
    head = low // HEAD
    key_pair = qkv[:, 3 * low + wide : 3 * low + 2 * wide]
    value_pair = qkv[:, 3 * low + 2 * wide : 3 * low + 3 * wide]
    key_t = key_pair.T
    keys = [of_head(key_pair, j) for j in range(heads)]
    values = [of_head(value_pair, j) for j in range(heads)]
    keys_t = [of_head(key_t, j, 0) for j in range(heads)]
    key_grad[...] = jnp.zeros_like(key_grad)
    value_grad[...] = jnp.zeros_like(value_grad)

    def block(i, carry):
        start = pl.multiple_of(i * step, step)
        query = qkv[pl.ds(start, step), 3 * low : 3 * low + wide]
        grad = given[pl.ds(start, step), :]
        total = None
        for j in range(heads):
            scores = dot32(keys[j], query, 1, 1)
            weights = jnp.exp(scores - logs[head + j : head + j + 1, pl.ds(start, step)])
            back = dot32(values[j], grad, 1, 1)
            inner = jnp.sum(weights * back, axis=0, keepdims=True)
            score_grad = (weights * (back - inner)).astype(bf16)
            value_grad[...] += dot32(weights.astype(bf16), of_head(grad, j), 1, 0)
            key_grad[...] += dot32(score_grad, of_head(query, j), 1, 0)
            part = dot32(keys_t[j], score_grad, 1, 0)
            total = part if total is None else total + part
        out[pl.ds(start, step), :wide] = (total.T * score_scale).astype(bf16)
        return carry

    lax.fori_loop(0, whole // step, block, 0)
    out[:, wide : 2 * wide] = key_grad[...].astype(bf16)
    out[:, 2 * wide :] = value_grad[...].astype(bf16)


def project_back(*refs, pairs):
    grads, weight, sums, outs = refs[:pairs], refs[pairs], refs[pairs + 1], refs[pairs + 2 :]
    rows = outs[0].shape[0]

    def tile(i, carry):
        cols = pl.ds(pl.multiple_of(i * TILE, TILE), TILE)
        for b in range(len(outs)):
            low = 0
            total = None
            for grad in grads:
                wide = grad.shape[1]
                part = dot32(grad[b * rows : (b + 1) * rows, :], weight[cols, low : low + wide], 1, 1)
                total = part if total is None else total + part
                low += wide
            outs[b][:, cols] = total.astype(bf16)
        return carry

    lax.fori_loop(0, weight.shape[0] // TILE, tile, 0)
    low = 0
    for grad in grads:
        wide = grad.shape[1]
        sums[:, low : low + wide] = jnp.sum(grad[...].astype(f32), axis=0, keepdims=True)
        low += wide


def projection_grad(place, *refs, count, micros, pairs):
    normed, refs = refs[:micros], refs[micros:]
    grads, refs = [refs[m * pairs : (m + 1) * pairs] for m in range(micros)], refs[micros * pairs :]
    tops, refs = [refs[4 * m : 4 * m + 4] for m in range(micros)], refs[4 * micros :]
    mixed, refs = refs[:micros], refs[micros:]
    left, right, left_chunk, right_chunk = refs
    cut = left.shape[1]
    rows_b = tops[0][0].shape[0]

    def put(rows, low, values):
        wide = values.shape[1]
        values = values.astype(bf16)
        if low + wide <= cut:
            left[rows, low : low + wide] = values
        elif low >= cut:
            right[rows, low - cut : low - cut + wide] = values
        else:
            left[rows, low:] = values[:, : cut - low]
            right[rows, : low + wide - cut] = values[:, cut - low :]

    def tile(i, carry):
        rows = pl.ds(pl.multiple_of(i * TILE, TILE), TILE)
        low = 0
        for p in range(pairs):
            total = None
            for m in range(micros):
                part = dot32(normed[m][:, rows], grads[m][p][...], 0, 0)
                total = part if total is None else total + part
            put(rows, low, total)
            low += total.shape[1]
        total = None
        for m in range(micros):
            for b in range(4):
                part = dot32(tops[m][b][:, rows], mixed[m][b * rows_b : (b + 1) * rows_b, :], 0, 0)
                total = part if total is None else total + part
        put(rows, low, total)
        return carry

    lax.fori_loop(0, left.shape[0] // TILE, tile, 0)
    left_chunk[...] = left[chunk_rows(place[0], count, left), :]
    right_chunk[...] = right[chunk_rows(place[1], count, right), :]


def ring_add(place, *refs, count, step):
    arrived, whole, outs = refs[:2], refs[2:4], refs[4:]
    for i in range(2):
        local = whole[i][chunk_rows(place[2 * step + i], count, whole[i]), :]
        outs[i][...] = (arrived[i][...].astype(f32) + local.astype(f32)).astype(bf16)


def ring_store(place, *refs, count, step):
    arrived = refs[:2]
    refs = refs[2 if step == 0 else 4 :]
    ahead, outs, buffers, sems = refs[:2], refs[2:4], refs[4:6], refs[6]
    copies = []
    for i in range(2):
        ahead[i][...] = arrived[i][...]
        buffers[i][...] = arrived[i][...].astype(f32)
        rows = chunk_rows(place[2 * step + i], count, outs[i])
        copies.append(pltpu.make_async_copy(buffers[i], outs[i].at[rows, :], sems.at[i]))
        copies[i].start()
    for copy in copies:
        copy.wait()


def norm_one_back(tok, resid_grad, first, second, third, gain, out, sums, *, m):
    grad = three(first, second, third)
    hat, inverse = statistics(tok[m, 0].astype(f32))
    out[...] = resid_grad[...] + norm_back(grad, hat, inverse, gain[...].astype(f32))
    sums[0:4, :] = jnp.zeros_like(sums[0:4, :])
    sums[4:5, :] = jnp.sum(grad * hat, axis=0, keepdims=True)
    sums[5:6, :] = jnp.sum(grad, axis=0, keepdims=True)
    sums[6:8, :] = jnp.zeros_like(sums[6:8, :])


def add_rows(resid, first, second, third, bias, out):
    out[...] = (resid[...] + three(first, second, third) + bias[...].astype(f32)).astype(bf16)


def swap(values, axis, bit):
    return lax.ppermute(values, axis, [(i, i ^ bit) for i in range(lax.axis_size(axis))])


def ring_order(count):
    return list(range(0, count, 2)) + list(range(1, count, 2))[::-1]


def butterfly(values, axis):
    bit = 1
    while bit < lax.axis_size(axis):
        values = values + swap(values, axis, bit)
        bit *= 2
    return values


class Rings:
    def __init__(self, chain, wholes, chunks, sends, keeps):
        self.chain, self.wholes = chain, wholes
        self.sends, self.keeps = sends, keeps
        self.count = lax.axis_size("wide")
        order = ring_order(self.count)
        self.perms = [[(order[i], order[(i + d) % self.count]) for i in range(self.count)] for d in (1, -1)]
        self.moving = [self.pass_on(c, i) for i, c in enumerate(chunks)]
        self.step = 1
        self.outs = None

    def pass_on(self, chunk, i):
        return lax.ppermute(chunk, "wide", self.perms[i])

    def add(self):
        shapes = [(c.shape, bf16) for c in self.moving]
        made = self.chain.run(
            functools.partial(ring_add, count=self.count, step=self.step), shapes, *self.moving, *self.wholes, smem=(self.sends,)
        )
        self.step += 1
        if self.step < self.count:
            self.moving = [self.pass_on(c, i) for i, c in enumerate(made)]
        else:
            self.moving, self.step = list(made), 0
            self.storing = True

    def store(self):
        first = self.outs is None
        shapes = [(c.shape, bf16) for c in self.moving] + [(w.shape, f32) for w in self.wholes]
        kept = () if first else self.outs
        made = self.chain.run(
            functools.partial(ring_store, count=self.count, step=self.step),
            shapes,
            *self.moving,
            *kept,
            smem=(self.keeps,),
            scratch=[pltpu.VMEM(c.shape, f32) for c in self.moving] + [pltpu.SemaphoreType.DMA((2,))],
            alias=None if first else {2: 2, 3: 3},
            anywhere=() if first else (2, 3),
            out_anywhere=(2, 3),
        )
        self.outs = made[2:]
        self.step += 1
        if self.step < self.count:
            self.moving = [self.pass_on(c, i) for i, c in enumerate(made[:2])]


class Whole:
    def __init__(self, wholes):
        self.outs = tuple(lax.psum(tuple(wholes), "wide"))
        self.outs = tuple(w.astype(f32) for w in self.outs)

    def add(self):
        pass

    def store(self):
        pass


def ring_tables(count):
    order = ring_order(count)
    sends = [[0] * (2 * count) for _ in range(count)]
    keeps = [[0] * (2 * count) for _ in range(count)]
    for place, device in enumerate(order):
        for step in range(count):
            for i, d in enumerate((1, -1)):
                sends[device][2 * step + i] = (place - d * (step + 1)) % count
                keeps[device][2 * step + i] = (place - d * step) % count
    return sends, keeps


def local(
    tokens,
    cotangent,
    cell_of,
    query_count,
    attn_norm_gain,
    attn_norm_bias,
    input_weight,
    query_bias,
    value_bias,
    out_weight,
    out_bias,
    ffn_norm_gain,
    ffn_norm_bias,
    up_weight,
    up_bias,
    down_weight,
    down_bias,
):
    micros = range(tokens.shape[0])
    rows, model = tokens.shape[2], tokens.shape[3]
    parts = lax.axis_size("narrow")
    whole = rows * parts
    width = input_weight.shape[2]
    hidden = up_weight.shape[1]
    count = lax.axis_size("wide")
    short = count <= 8
    pairs = head_pairs(width)
    chain = Chain()
    run = chain.run
    index = lax.axis_index("wide")

    block = ((rows, model), bf16)
    blocks = [block] * parts
    wide_rows = ((whole, model), bf16)
    row = lambda v: v.reshape(1, -1)
    gain_one, bias_one, gain_two, bias_two = map(row, (attn_norm_gain, attn_norm_bias, ffn_norm_gain, ffn_norm_bias))
    out_bias, down_bias, up_bias = row(out_bias), row(down_bias), row(up_bias)

    slots = index + count * jnp.arange(len(micros), dtype=jnp.int32)
    counts = jnp.stack([query_count[cell_of[slots[m]]] for m in micros])
    scale = jnp.sqrt(counts.astype(f32) / 500.0)
    sends, keeps = ring_tables(count)
    sends = lax.dynamic_index_in_dim(jnp.array(sends, jnp.int32), index, 0, keepdims=False)
    keeps = lax.dynamic_index_in_dim(jnp.array(keeps, jnp.int32), index, 0, keepdims=False)

    def by_pairs(three_parts):
        return jnp.concatenate([v[..., low : low + wide] for low, wide in pairs for v in three_parts], axis=-1)

    weight = by_pairs([input_weight[:, j] for j in range(3)])
    zero = jnp.zeros((1, width), f32)
    project_bias = by_pairs([row(query_bias).astype(f32), zero, row(value_bias).astype(f32)])
    project_scale = by_pairs([zero + score_scale, zero + 1.0, zero + 1.0])

    def gather(own):
        partner = swap(own, "narrow", 2)
        return [own, swap(own, "narrow", 1), partner, swap(partner, "narrow", 1)]

    def share(shares):
        return [*shares, swap(shares[3], "narrow", 1)]

    def send(shares):
        (both,) = run(pair_sum, [block], shares[2], shares[4])
        return [shares[0], swap(shares[1], "narrow", 1), swap(both, "narrow", 2)]

    nothing = [None, None]
    normed, given, qkv, normed_all, mixed, logs = ([*nothing] for _ in range(6))
    shares, resid, normed_two_b, activ, pre_grad, up_bias_grad, two_all, given_all = ([*nothing] for _ in range(8))
    resid_grad, top, sums_two, sums_one, stack_sums, out_rows, grad_rows = ([*nothing] for _ in range(7))
    pair_grads = [[], []]

    def do_norm_one(m):
        (own,) = run(functools.partial(norm_one, m=m), [block], tokens, gain_one, bias_one)
        normed[m] = gather(own)

    def do_scale(m):
        (own,) = run(functools.partial(scale_cot, m=m), [block], cotangent, smem=(scale,))
        given[m] = gather(own)

    def do_project(m):
        qkv[m], normed_all[m] = run(
            functools.partial(project, parts=parts),
            [((whole, 3 * width), bf16), wide_rows],
            *normed[m],
            weight,
            project_bias,
            project_scale,
        )

    def do_attend(m):
        mixed[m], logs[m], *b = run(
            functools.partial(attend, step=min(512, whole)),
            [((whole, width), bf16), ((8, whole), f32), *blocks],
            qkv[m],
            out_weight,
            limit=40,
        )
        shares[m] = share(b)

    def do_send(m):
        shares[m] = send(shares[m])

    def do_norm_two(m):
        resid[m], own = run(
            functools.partial(norm_two, m=m),
            [((rows, model), f32), block],
            tokens,
            *shares[m],
            out_bias,
            gain_two,
            bias_two,
        )
        normed_two_b[m] = gather(own)

    def do_feed(m):
        activ[m], pre_grad[m], up_bias_grad[m], two_all[m], given_all[m] = run(
            functools.partial(feed, parts=parts),
            [((whole, hidden), bf16), ((whole, hidden), bf16), ((1, hidden), f32), wide_rows, wide_rows],
            *normed_two_b[m],
            *given[m],
            up_weight,
            up_bias,
            down_weight,
            limit=48,
        )

    def do_up_back(m):
        shares[m] = share(run(times_back, blocks, pre_grad[m], up_weight))

    def do_down(m):
        shares_down[m] = share(run(times, blocks, activ[m], down_weight))

    def do_norm_two_back(m):
        resid_grad[m], own, sums_two[m] = run(
            functools.partial(norm_two_back, m=m),
            [((rows, model), f32), block, ((8, model), f32)],
            cotangent,
            resid[m],
            *shares[m],
            gain_two,
            smem=(scale,),
        )
        top[m] = gather(own)

    def do_attend_back(m, p):
        low, wide = pairs[p]
        (made,) = run(
            functools.partial(attend_back, parts=parts, step=min(512, whole), low=low, wide=wide),
            [((whole, 3 * wide), bf16)],
            qkv[m],
            logs[m],
            out_weight,
            *top[m],
            scratch=[pltpu.VMEM((whole, wide), f32)] * 2 + [pltpu.VMEM((whole, wide), bf16)],
            limit=48,
        )
        pair_grads[m].append(made)

    def do_project_back(m):
        stack_sums[m], *b = run(
            functools.partial(project_back, pairs=len(pairs)),
            [((1, 3 * width), f32), *blocks],
            *pair_grads[m],
            weight,
        )
        shares[m] = share(b)

    def do_norm_one_back(m):
        grad_rows[m], sums_one[m] = run(
            functools.partial(norm_one_back, m=m),
            [((rows, model), f32), ((8, model), f32)],
            tokens,
            resid_grad[m],
            *shares[m],
            gain_one,
        )

    def do_add_rows(m):
        (out_rows[m],) = run(add_rows, [block], resid[m], *shares_down[m], down_bias)

    def ffn_grad(firsts, seconds, ring):
        shape = (firsts[0].shape[1], seconds[0].shape[1])
        return run(
            functools.partial(weight_grad, count=count if short else 1, pairs=len(micros), ring=ring),
            [(shape, bf16), ((shape[0] // (count if short else 1), shape[1]), bf16)],
            *firsts,
            *seconds,
            smem=(sends if short else jnp.zeros((2,), jnp.int32),),
            limit=40,
        )

    shares_down = [*nothing]

    do_norm_one(0)
    do_norm_one(1)
    do_scale(0)
    do_project(0)
    do_attend(0)
    do_project(1)
    do_send(0)
    do_attend(1)
    do_norm_two(0)
    do_send(1)
    do_scale(1)
    do_norm_two(1)
    do_feed(0)
    do_up_back(0)
    do_feed(1)
    do_send(0)
    down_grad, down_chunk = ffn_grad(activ, given_all, 0)
    do_up_back(1)
    up_grad, up_chunk = ffn_grad(two_all, pre_grad, 1)
    ffn = Rings(chain, (down_grad, up_grad), (down_chunk, up_chunk), sends, keeps) if short else Whole((down_grad, up_grad))
    do_send(1)
    do_norm_two_back(0)
    ffn.add()
    do_norm_two_back(1)
    do_down(0)
    ffn.add()
    do_attend_back(0, 0)
    ffn.add()
    shares_down[0] = send(shares_down[0])
    do_attend_back(0, 1)
    ffn.add()
    do_attend_back(0, 2)
    do_project_back(0)
    ffn.add()
    do_attend_back(1, 0)
    do_send(0)
    ffn.add()
    do_attend_back(1, 1)
    ffn.add()
    ffn.store()
    do_attend_back(1, 2)
    do_project_back(1)
    ffn.store()
    left, right, left_chunk, right_chunk = run(
        functools.partial(projection_grad, count=count if short else 1, micros=len(micros), pairs=len(pairs)),
        [((model, 2 * width), bf16)] * 2 + [((model // (count if short else 1), 2 * width), bf16)] * 2,
        *normed_all,
        *pair_grads[0],
        *pair_grads[1],
        *top[0],
        *top[1],
        *mixed,
        smem=(sends if short else jnp.zeros((2,), jnp.int32),),
        limit=48,
    )
    attn = Rings(chain, (left, right), (left_chunk, right_chunk), sends, keeps) if short else Whole((left, right))
    do_send(1)
    ffn.store()
    do_norm_one_back(0)
    attn.add()
    do_down(1)
    ffn.store()
    attn.add()
    do_add_rows(0)
    do_norm_one_back(1)
    shares_down[1] = send(shares_down[1])
    ffn.store()
    attn.add()
    ffn.store()
    attn.add()
    do_add_rows(1)
    ffn.store()
    attn.add()
    ffn.store()
    attn.add()
    attn.add()
    for _ in range(count if short else 0):
        attn.store()

    vectors = sums_one[0] + sums_one[1] + sums_two[0] + sums_two[1]
    vectors = butterfly(vectors, "narrow")
    stack_sum = stack_sums[0] + stack_sums[1]
    packed = jnp.concatenate([vectors[:6].reshape(-1), (up_bias_grad[0] + up_bias_grad[1])[0], stack_sum[0]])
    packed = butterfly(packed, "wide")
    vector_sums = packed[: 6 * model].reshape(6, model)
    up_bias_sum = packed[6 * model : 6 * model + hidden]
    stack_sum = packed[6 * model + hidden :]

    def from_pairs(values, j):
        return jnp.concatenate(
            [values[..., 3 * low + j * wide : 3 * low + (j + 1) * wide] for low, wide in pairs], axis=-1
        )

    both = jnp.concatenate(attn.outs, axis=1)
    input_sum = jnp.stack([from_pairs(both[:, : 3 * width], j) for j in range(3)], axis=1)
    return (
        jnp.stack(out_rows)[:, None],
        jnp.stack(grad_rows)[:, None],
        vector_sums[4],
        vector_sums[5],
        input_sum,
        from_pairs(stack_sum, 0),
        from_pairs(stack_sum, 2),
        both[:, 3 * width :].T,
        vector_sums[0],
        vector_sums[1],
        vector_sums[2],
        ffn.outs[1],
        up_bias_sum,
        ffn.outs[0],
        vector_sums[3],
    )


def solution(mesh):
    in_specs = (
        P(None, "wide", "narrow", None),
        P(None, "wide", "narrow", None),
        P(),
        P(),
        P(),
        P(),
        P(None, None, "narrow"),
        P("narrow"),
        P("narrow"),
        P("narrow", None),
        P(),
        P(),
        P(),
        P(None, "narrow"),
        P("narrow"),
        P("narrow", None),
        P(),
    )
    out_specs = (
        P(None, "wide", "narrow", None),
        P(None, "wide", "narrow", None),
        P(),
        P(),
        P(None, None, "narrow"),
        P("narrow"),
        P("narrow"),
        P("narrow", None),
        P(),
        P(),
        P(),
        P(None, "narrow"),
        P("narrow"),
        P("narrow", None),
        P(),
    )
    return jax.shard_map(local, mesh=mesh, in_specs=in_specs, out_specs=out_specs, check_vma=False)
```

time: 1290 us -> 616 us (0.48)
  waiting for transfers between devices: 827 us -> 190 us
  Pallas kernels: 0 us -> 246 us
  matrix products: 211 us -> 0 us
  starting transfers between devices: 1.71 us -> 89 us
  blocking collectives: 82.6 us -> 0 us
  other arithmetic: 65.9 us -> 9.4 us
  local copies, waits for them, and re-layouts: 77.1 us -> 61.2 us
    psum x1 -> x0, waiting for transfers between devices: 506 us -> none  [local(): lax.psum((totals_acc[0], totals_acc[1], totals_acc[2], totals_acc[3], tot...]
    pallas_call x0 -> x71, Pallas kernels: none -> 246 us  [run(): pl.pallas_call(inner, out_shape=tuple((jax.ShapeDtypeStruct(*o) for o in...]
    dot_general x52 -> x0, matrix products: 211 us -> none  [the longest x2 35.5 us: local(): jnp.dot(normed_two_all, up_weight, preferred_element_type=jnp.float32)]
    ppermute x0 -> x109, waiting for transfers between devices: none -> 190 us  [the longest x53 104 us: swap(): lax.ppermute(values, axis, [(i, i ^ bit) for i in range(lax.axis_size(axi...]
    reduce_scatter x8 -> x0, waiting for transfers between devices: 174 us -> none  [the longest x2 68.3 us: local(): lax.psum_scatter(jnp.dot(attended, out_weight, preferred_element_type=jnp...]
    all_gather x8 -> x0, waiting for transfers between devices: 145 us -> none  [the longest x2 53.9 us: local(): normed_all = lax.all_gather(normed_one, 'narrow', axis=0, tiled=True)]
    ppermute x0 -> x109, starting transfers between devices: none -> 89 us  [the longest x56 59.7 us: pass_on(): return lax.ppermute(chunk, 'wide', self.perms[i])]
    psum x2 -> x0, blocking collectives: 82.6 us -> none  [the longest x1 43.6 us: local(): lax.psum((vector_acc[0], vector_acc[1], vector_acc[2], vector_acc[3], vec...]
  transfers between devices with their start and end apart: 17 -> 109, of which waited for: 14 -> 41; matrix products, arithmetic and copies ran while one was open for 14% -> 4% of each run, Pallas kernels for 0% -> 35%
where the time goes in v2:
time: 616 us; the launch traced here: 607 us
  Pallas kernels  246 us (40%)
  waiting for transfers between devices  190 us (31%)
  starting transfers between devices  89 us (14%)
  local copies, waits for them, and re-layouts  61.2 us (10%)
  between operations  10.2 us (2%)
  other arithmetic  9.4 us (2%)
    pallas_call x71, Pallas kernels, run(): pl.pallas_call(inner, out_shape=tuple((jax.ShapeDtypeStruct(*o) for o in...  246 us
    ppermute x53, waiting for transfers between devices, swap(): lax.ppermute(values, axis, [(i, i ^ bit) for i in range(lax.axis_size(axi...  104 us
    ppermute x56, waiting for transfers between devices, pass_on(): return lax.ppermute(chunk, 'wide', self.perms[i])  86.8 us
    ppermute x56, starting transfers between devices, pass_on(): return lax.ppermute(chunk, 'wide', self.perms[i])  59.7 us
    unnamed x231, local copies, waits for them, and re-layouts  43.8 us
    ppermute x53, starting transfers between devices, swap(): lax.ppermute(values, axis, [(i, i ^ bit) for i in range(lax.axis_size(axi...  29.3 us
  transfers between devices with their start and end apart: 109, of which 41 were waited for; matrix products, arithmetic and copies ran while one was open for 4% of the time, Pallas kernels for 35%

profile of v2, /device:TPU:0, one launch (start us, length us, event | category | flops | bytes accessed | tf_op | source)
XLA Modules:
  0.0 606.6 jit_solution(275196398211793951)
XLA Ops:
  6.4 2.5 collective-permute-start.6
  30.6 8.1 %collective-permute-done.1.refs_2_ = bf16[256,1280]{1,0:T(8,128)(2,1)} collective-permute-done((bf16[256,1280]{1,0:T(8,128)(2,1)}, bf16[256,1280]{1,0:T(8,128)(2,1)}, u32[]{:S(2)}, u32[]{:S(2)}) %collective-permute-start.1) | collective-permute-done | bytes 655392 | tf_op jit(solution)/shard_map/ppermute | solution.py:395
  40.0 3.9 concatenate.25.refs_4_.refs_3_
  45.6 4.6 project.2
  51.7 12.6 %attend.2 = (bf16[1024,320]{1,0:T(8,128)(2,1)S(1)}, f32[8,1024]{1,0:T(8,128)S(1)}, bf16[256,1280]{1,0:T(8,128)(2,1)S(1)}, bf16[256,1280]{1,0:T(8,128)(2,1)S(1)},...) custom-call(bf16[1024,960]{1,0:T(8,128)(2,1)S(1)} %get-tuple-element.178.refs_0_.refs_2_, ...), custom_call_target="tpu_custom_call" | custom-call | tf_op jit(solution)/shard_map/attend/pallas_call | solution.py:42
  65.0 4.4 project.3
  73.0 12.8 %attend.3 = (bf16[1024,320]{1,0:T(8,128)(2,1)S(1)}, f32[8,1024]{1,0:T(8,128)S(1)}, bf16[256,1280]{1,0:T(8,128)(2,1)S(1)}, bf16[256,1280]{1,0:T(8,128)(2,1)S(1)},...) custom-call(bf16[1024,960]{1,0:T(8,128)(2,1)S(1)} %get-tuple-element.184.refs_2_.refs_0_, ...), custom_call_target="tpu_custom_call" | custom-call | tf_op jit(solution)/shard_map/attend/pallas_call | solution.py:42
  88.9 2.2 collective-permute-start.17
  91.2 12.3 %collective-permute-done.13.refs_6_ = bf16[256,1280]{1,0:T(8,128)(2,1)S(1)} collective-permute-done((bf16[256,1280]{1,0:T(8,128)(2,1)S(1)}, bf16[256,1280]{1,0:T(8,128)(2,1)S(1)}, u32[]{:S(2)}, u32[]{:S(2)}) %collective-permute-start.13) | collective-permute-done | bytes 655392 | tf_op jit(solution)/shard_map/ppermute | solution.py:395
  105.6 12.0 %collective-permute-done.17.refs_3_ = bf16[256,1280]{1,0:T(8,128)(2,1)S(1)} collective-permute-done((bf16[256,1280]{1,0:T(8,128)(2,1)S(1)}, bf16[256,1280]{1,0:T(8,128)(2,1)S(1)}, u32[]{:S(2)}, u32[]{:S(2)}) %collective-permute-start.17) | collective-permute-done | bytes 655392 | tf_op jit(solution)/shard_map/ppermute | solution.py:395
  122.2 9.4 %collective-permute-done.10.refs_2_ = bf16[256,1280]{1,0:T(8,128)(2,1)S(1)} collective-permute-done((bf16[256,1280]{1,0:T(8,128)(2,1)S(1)}, bf16[256,1280]{1,0:T(8,128)(2,1)S(1)}, u32[]{:S(2)}, u32[]{:S(2)}) %collective-permute-start.10) | collective-permute-done | bytes 655392 | tf_op jit(solution)/shard_map/ppermute | solution.py:395
  132.2 13.6 %collective-permute-done.22.refs_6_ = bf16[256,1280]{1,0:T(8,128)(2,1)} collective-permute-done((bf16[256,1280]{1,0:T(8,128)(2,1)}, bf16[256,1280]{1,0:T(8,128)(2,1)}, u32[]{:S(2)}, u32[]{:S(2)}) %collective-permute-start.22) | collective-permute-done | bytes 655392 | tf_op jit(solution)/shard_map/ppermute | solution.py:395
  146.2 13.1 %collective-permute-done.19.refs_2_ = bf16[256,1280]{1,0:T(8,128)(2,1)} collective-permute-done((bf16[256,1280]{1,0:T(8,128)(2,1)}, bf16[256,1280]{1,0:T(8,128)(2,1)}, u32[]{:S(2)}, u32[]{:S(2)}) %collective-permute-start.19) | collective-permute-done | bytes 655392 | tf_op jit(solution)/shard_map/ppermute | solution.py:395
  159.3 15.4 %feed.2 = (bf16[1024,1280]{1,0:T(8,128)(2,1)}, bf16[1024,1280]{1,0:T(8,128)(2,1)}, f32[1,1280]{1,0:T(1,128)S(1)}, bf16[1024,1280]{1,0:T(8,128)(2,1)}, bf16[1024,1280]{1,0:T(8,128)(2,1)}) custom-call(bf16[256,1280]{1,0:T(8,128)(2,1)S(1)} %get-tuple-element.187.refs_0_, bf16[256,1280]{1,0:T(8,128)(2,1)S(1)} %collective-permute-done.9.refs_1_, ...), custom_call_target="tpu_custom_call" | custom-call | tf_op jit(solution)/shard_map/feed/pallas_call | solution.py:42
  178.2 5.3 times_back.2
  187.5 16.3 %feed.3 = (bf16[1024,1280]{1,0:T(8,128)(2,1)}, bf16[1024,1280]{1,0:T(8,128)(2,1)}, f32[1,1280]{1,0:T(1,128)S(1)}, bf16[1024,1280]{1,0:T(8,128)(2,1)}, bf16[1024,1280]{1,0:T(8,128)(2,1)}) custom-call(bf16[256,1280]{1,0:T(8,128)(2,1)} %get-tuple-element.194.refs_0_, bf16[256,1280]{1,0:T(8,128)(2,1)} %collective-permute-done.18.refs_1_, ...), custom_call_target="tpu_custom_call" | custom-call | tf_op jit(solution)/shard_map/feed/pallas_call | solution.py:42
  203.9 1.9 copy-done.20
  205.8 2.1 pair_sum.10.refs_5_
  211.3 10.1 %weight_grad.2 = (bf16[1280,1280]{1,0:T(8,128)(2,1)}, bf16[160,1280]{1,0:T(8,128)(2,1)S(1)}) custom-call(s32[16]{0:T(128)S(1)} %dynamic-slice_bitcast_fusion.1.refs_0_, bf16[1024,1280]{1,0:T(8,128)(2,1)S(1)} %copy-done.18, bf16[1024,1280]{1,0:T(8,128)(2,1)S(1)} %copy-done.21, bf16[1024,1280]{1,0:T(8,128)(2,1)S(1)} %copy-done.82, ...), custom_call_target="tpu_custom_call" | custom-call | tf_op jit(solution)/shard_map/weight_grad/pallas_call | solution.py:42
  221.4 2.1 copy-done
  223.5 4.9 times_back.3
  229.7 10.3 %weight_grad.3 = (bf16[1280,1280]{1,0:T(8,128)(2,1)}, bf16[160,1280]{1,0:T(8,128)(2,1)S(1)}) custom-call(s32[16]{0:T(128)S(1)} %dynamic-slice_bitcast_fusion.1.refs_0_, bf16[1024,1280]{1,0:T(8,128)(2,1)S(1)} %copy-done.81, bf16[1024,1280]{1,0:T(8,128)(2,1)S(1)} %copy-done.83, bf16[1024,1280]{1,0:T(8,128)(2,1)S(1)} %copy-done.51, ...), custom_call_target="tpu_custom_call" | custom-call | tf_op jit(solution)/shard_map/weight_grad/pallas_call | solution.py:42
  239.9 1.9 copy-done.2
  242.1 3.8 collective-permute-done.31.refs_5_
  245.9 1.9 norm_two_back.2
  251.9 7.0 %collective-permute-done.28.refs_1_ = bf16[160,1280]{1,0:T(8,128)(2,1)S(1)} collective-permute-done((bf16[160,1280]{1,0:T(8,128)(2,1)S(1)}, bf16[160,1280]{1,0:T(8,128)(2,1)S(1)}, u32[]{:S(2)}, u32[]{:S(2)}) %collective-permute-start.28) | collective-permute-done | bytes 409632 | tf_op jit(solution)/shard_map/ppermute | solution.py:422
  265.5 12.2 %collective-permute-done.27.refs_5_ = bf16[256,1280]{1,0:T(8,128)(2,1)S(1)} collective-permute-done((bf16[256,1280]{1,0:T(8,128)(2,1)S(1)}, bf16[256,1280]{1,0:T(8,128)(2,1)S(1)}, u32[]{:S(2)}, u32[]{:S(2)}) %collective-permute-start.27) | collective-permute-done | bytes 655392 | tf_op jit(solution)/shard_map/ppermute | solution.py:395
  278.8 2.7 norm_two_back.3
  281.6 5.1 times.2
  291.1 9.4 %attend_back.6.refs_5_.refs_0_.refs_3_ = bf16[1024,384]{1,0:T(8,128)(2,1)S(1)} custom-call(bf16[1024,960]{1,0:T(8,128)(2,1)} %copy-done.13, f32[8,1024]{1,0:T(8,128)S(1)} %get-tuple-element.224.refs_1_, bf16[320,1280]{1,0:T(8,128)(2,1)S(1)} %copy-done.7, bf16[256,1280]{1,0:T(8,128)(2,1)S(1)} %get-tuple-element.225.refs_3_.refs_9_, ...), custom_call_target="tpu_custom_call" | custom-call | tf_op jit(solution)/shard_map/attend_back/pallas_call | solution.py:42
  300.6 2.4 ring_add.16
  307.1 9.4 %attend_back.7.refs_5_.refs_1_.refs_4_ = bf16[1024,384]{1,0:T(8,128)(2,1)S(1)} custom-call(bf16[1024,960]{1,0:T(8,128)(2,1)} %copy-done.13, f32[8,1024]{1,0:T(8,128)S(1)} %get-tuple-element.224.refs_1_, bf16[320,1280]{1,0:T(8,128)(2,1)S(1)} %copy-done.7, bf16[256,1280]{1,0:T(8,128)(2,1)S(1)} %copy-done.39, bf16[256,1280]{1,0:T(8,128)(2,1)S(1)} %copy-done.45, ...), custom_call_target="tpu_custom_call" | custom-call | tf_op jit(solution)/shard_map/attend_back/pallas_call | solution.py:42
  317.4 2.3 ring_add.17
  322.2 6.2 %attend_back.8.refs_2_.refs_4_.refs_5_ = bf16[1024,192]{1,0:T(8,128)(2,1)S(1)} custom-call(bf16[1024,960]{1,0:T(8,128)(2,1)} %copy-done.13, f32[8,1024]{1,0:T(8,128)S(1)} %get-tuple-element.224.refs_1_, bf16[320,1280]{1,0:T(8,128)(2,1)S(1)} %copy-done.7, bf16[256,1280]{1,0:T(8,128)(2,1)S(1)} %copy-done.39, bf16[256,1280]{1,0:T(8,128)(2,1)S(1)} %copy-done.45, ...), custom_call_target="tpu_custom_call" | custom-call | tf_op jit(solution)/shard_map/attend_back/pallas_call | solution.py:42
  328.5 5.5 project_back.2
  334.2 1.9 ring_add.18
  338.2 9.7 %attend_back.9.refs_2_.refs_0_.refs_6_ = bf16[1024,384]{1,0:T(8,128)(2,1)S(1)} custom-call(bf16[1024,960]{1,0:T(8,128)(2,1)} %copy-done.12, f32[8,1024]{1,0:T(8,128)S(1)} %get-tuple-element.231.refs_1_, bf16[320,1280]{1,0:T(8,128)(2,1)S(1)} %copy-done.7, bf16[256,1280]{1,0:T(8,128)(2,1)} %get-tuple-element.232.refs_3_.refs_13_, ...), custom_call_target="tpu_custom_call" | custom-call | tf_op jit(solution)/shard_map/attend_back/pallas_call | solution.py:42
  353.8 9.7 %attend_back.10.refs_5_.refs_1_.refs_7_ = bf16[1024,384]{1,0:T(8,128)(2,1)S(1)} custom-call(bf16[1024,960]{1,0:T(8,128)(2,1)} %copy-done.12, f32[8,1024]{1,0:T(8,128)S(1)} %get-tuple-element.231.refs_1_, bf16[320,1280]{1,0:T(8,128)(2,1)S(1)} %copy-done.7, bf16[256,1280]{1,0:T(8,128)(2,1)} %get-tuple-element.232.refs_3_.refs_13_, ...), custom_call_target="tpu_custom_call" | custom-call | tf_op jit(solution)/shard_map/attend_back/pallas_call | solution.py:42
  368.2 6.7 %attend_back.11.refs_2_.refs_4_.refs_8_ = bf16[1024,192]{1,0:T(8,128)(2,1)S(1)} custom-call(bf16[1024,960]{1,0:T(8,128)(2,1)} %copy-done.12, f32[8,1024]{1,0:T(8,128)S(1)} %get-tuple-element.231.refs_1_, bf16[320,1280]{1,0:T(8,128)(2,1)S(1)} %copy-done.7, bf16[256,1280]{1,0:T(8,128)(2,1)} %get-tuple-element.232.refs_3_.refs_13_, ...), custom_call_target="tpu_custom_call" | custom-call | tf_op jit(solution)/shard_map/attend_back/pallas_call | solution.py:42
  374.9 4.8 project_back.3
  386.0 8.3 %collective-permute-done.60.refs_1_ = bf16[160,1280]{1,0:T(8,128)(2,1)S(1)} collective-permute-done((bf16[160,1280]{1,0:T(8,128)(2,1)S(1)}, bf16[160,1280]{1,0:T(8,128)(2,1)S(1)}, u32[]{:S(2)}, u32[]{:S(2)}) %collective-permute-start.60) | collective-permute-done | bytes 409632 | tf_op jit(solution)/shard_map/ppermute | solution.py:422
  395.7 17.6 %projection_grad.1 = (bf16[1280,640]{1,0:T(8,128)(2,1)}, bf16[1280,640]{1,0:T(8,128)(2,1)}, bf16[160,640]{1,0:T(8,128)(2,1)}, bf16[160,640]{1,0:T(8,128)(2,1)S(1)}) custom-call(s32[16]{0:T(128)S(1)} %dynamic-slice_bitcast_fusion.1.refs_0_, bf16[1024,1280]{1,0:T(8,128)(2,1)} %copy-done.74, bf16[1024,1280]{1,0:T(8,128)(2,1)} %copy-done.75, ...), custom_call_target="tpu_custom_call" | custom-call | tf_op jit(solution)/shard_map/projection_grad/pallas_call | solution.py:42
  423.0 11.5 %collective-permute-done.57.refs_2_ = bf16[160,640]{1,0:T(8,128)(2,1)S(1)} collective-permute-done((bf16[160,640]{1,0:T(8,128)(2,1)S(1)}, bf16[160,640]{1,0:T(8,128)(2,1)S(1)}, u32[]{:S(2)}, u32[]{:S(2)}) %collective-permute-start.57) | collective-permute-done | bytes 204832 | tf_op jit(solution)/shard_map/ppermute | solution.py:422
  436.3 4.2 times.3
  445.4 3.4 collective-permute-done.63.refs_1_
  451.9 5.8 collective-permute-done.70.refs_4_
  466.8 10.0 %collective-permute-done.72.refs_1_ = bf16[160,640]{1,0:T(8,128)(2,1)S(1)} collective-permute-done((bf16[160,640]{1,0:T(8,128)(2,1)S(1)}, bf16[160,640]{1,0:T(8,128)(2,1)S(1)}, u32[]{:S(2)}, u32[]{:S(2)}) %collective-permute-start.72) | collective-permute-done | bytes 204832 | tf_op jit(solution)/shard_map/ppermute | solution.py:422
  485.8 2.6 collective-permute-done.77.refs_2_
  491.6 5.3 collective-permute-done.71.refs_3_
  498.0 2.7 ring_store.22
  507.6 5.9 collective-permute-done.91.refs_1_
  513.5 4.6 collective-permute-done.92.refs_2_
  518.1 3.1 ring_store.23
  526.0 2.1 collective-permute-done.93.refs_1_
  534.2 4.5 collective-permute-done.83
  538.7 2.3 collective-permute-start.84
  545.9 3.9 collective-permute-done.97.refs_1_
  553.4 4.7 collective-permute-done.99.refs_1_
  562.2 3.8 collective-permute-done.101.refs_1_
  570.6 2.6 collective-permute-done.103.refs_1_
  578.4 3.1 collective-permute-done.105.refs_1_
  587.4 2.4 collective-permute-done.107.refs_1_
  594.5 2.9 pad_maximum_fusion
  597.5 7.3 %copy.67 = f32[1280,3,320]{0,2,1:T(8,128)} copy(f32[1280,3,320]{2,0,1:T(8,128)} %pad_maximum_fusion) | data formatting | bytes 9830400
  (510 shorter events, 189.7 us)
Async XLA Ops:
  6.0 59.0 %collective-permute-start.5 = (bf16[256,1280]{1,0:T(8,128)(2,1)}, bf16[256,1280]{1,0:T(8,128)(2,1)}, u32[]{:S(2)}, u32[]{:S(2)}) collective-permute-start(bf16[256,1280]{1,0:T(8,128)(2,1)} %norm_one.3.refs_2_.refs_0_), channel_id=1, source_target_pairs={{0,1},{1,0},{2,3},{3,2},{4,5},{5,4},{6,7},{7,6},{8,9},{9,8},{10,11... | collective-permute-start | bytes 1966088 | tf_op jit(solution)/shard_map/ppermute | solution.py:395
  6.4 37.5 %collective-permute-start.6 = (bf16[256,1280]{1,0:T(8,128)(2,1)}, bf16[256,1280]{1,0:T(8,128)(2,1)}, u32[]{:S(2)}, u32[]{:S(2)}) collective-permute-start(bf16[256,1280]{1,0:T(8,128)(2,1)} %norm_one.3.refs_2_.refs_0_), channel_id=1, source_target_pairs={{0,2},{1,3},{2,0},{3,1},{4,6},{5,7},{6,4},{7,5},{8,10},{9,11},{10,... | collective-permute-start | bytes 1966088 | tf_op jit(solution)/shard_map/ppermute | solution.py:395
  8.9 35.6 %collective-permute-start = (bf16[256,1280]{1,0:T(8,128)(2,1)}, bf16[256,1280]{1,0:T(8,128)(2,1)}, u32[]{:S(2)}, u32[]{:S(2)}) collective-permute-start(bf16[256,1280]{1,0:T(8,128)(2,1)} %norm_one.2.refs_3_.refs_0_), channel_id=1, source_target_pairs={{0,1},{1,0},{2,3},{3,2},{4,5},{5,4},{6,7},{7,6},{8,9},{9,8},{10,11... | collective-permute-start | bytes 1966088 | tf_op jit(solution)/shard_map/ppermute | solution.py:395
  9.2 29.5 %collective-permute-start.1 = (bf16[256,1280]{1,0:T(8,128)(2,1)}, bf16[256,1280]{1,0:T(8,128)(2,1)}, u32[]{:S(2)}, u32[]{:S(2)}) collective-permute-start(bf16[256,1280]{1,0:T(8,128)(2,1)} %norm_one.2.refs_3_.refs_0_), channel_id=1, source_target_pairs={{0,2},{1,3},{2,0},{3,1},{4,6},{5,7},{6,4},{7,5},{8,10},{9,11},{10,... | collective-permute-start | bytes 1966088 | tf_op jit(solution)/shard_map/ppermute | solution.py:395
  44.0 21.0 %collective-permute-start.7 = (bf16[256,1280]{1,0:T(8,128)(2,1)}, bf16[256,1280]{1,0:T(8,128)(2,1)S(1)}, u32[]{:S(2)}, u32[]{:S(2)}) collective-permute-start(bf16[256,1280]{1,0:T(8,128)(2,1)} %collective-permute-done.6.refs_2_), channel_id=1, source_target_pairs={{0,1},{1,0},{2,3},{3,2},{4,5},{5,4},{6,7},{7,6},{8,9},{9,8},{10,11... | collective-permute-start | bytes 1966088 | tf_op jit(solution)/shard_map/ppermute | solution.py:395
  64.5 22.0 %collective-permute-start.3 = (bf16[256,1280]{1,0:T(8,128)(2,1)S(1)}, bf16[256,1280]{1,0:T(8,128)(2,1)S(1)}, u32[]{:S(2)}, u32[]{:S(2)}) collective-permute-start(bf16[256,1280]{1,0:T(8,128)(2,1)S(1)} %get-tuple-element.180), channel_id=1, source_target_pairs={{0,1},{1,0},{2,3},{3,2},{4,5},{5,4},{6,7},{7,6},{8,9},{9,8},{10,11... | collective-permute-start | bytes 1966088 | tf_op jit(solution)/shard_map/ppermute | solution.py:395
  71.2 16.8 %collective-permute-start.8 = (bf16[256,1280]{1,0:T(8,128)(2,1)S(1)}, bf16[256,1280]{1,0:T(8,128)(2,1)S(1)}, u32[]{:S(2)}, u32[]{:S(2)}) collective-permute-start(bf16[256,1280]{1,0:T(8,128)(2,1)S(1)} %pair_sum.8.refs_2_), channel_id=1, source_target_pairs={{0,2},{1,3},{2,0},{3,1},{4,6},{5,7},{6,4},{7,5},{8,10},{9,11},{10,... | collective-permute-start | bytes 1966088 | tf_op jit(solution)/shard_map/ppermute | solution.py:395
  85.9 17.6 %collective-permute-start.13 = (bf16[256,1280]{1,0:T(8,128)(2,1)S(1)}, bf16[256,1280]{1,0:T(8,128)(2,1)S(1)}, u32[]{:S(2)}, u32[]{:S(2)}) collective-permute-start(bf16[256,1280]{1,0:T(8,128)(2,1)S(1)} %copy-done.59), channel_id=1, source_target_pairs={{0,2},{1,3},{2,0},{3,1},{4,6},{5,7},{6,4},{7,5},{8,10},{9,11},{10,... | collective-permute-start | bytes 1966088 | tf_op jit(solution)/shard_map/ppermute | solution.py:395
  86.3 18.7 %collective-permute-start.15 = (bf16[256,1280]{1,0:T(8,128)(2,1)S(1)}, bf16[256,1280]{1,0:T(8,128)(2,1)S(1)}, u32[]{:S(2)}, u32[]{:S(2)}) collective-permute-start(bf16[256,1280]{1,0:T(8,128)(2,1)S(1)} %get-tuple-element.189), channel_id=1, source_target_pairs={{0,1},{1,0},{2,3},{3,2},{4,5},{5,4},{6,7},{7,6},{8,9},{9,8},{10,11... | collective-permute-start | bytes 1966088 | tf_op jit(solution)/shard_map/ppermute | solution.py:395
  88.9 28.6 %collective-permute-start.17 = (bf16[256,1280]{1,0:T(8,128)(2,1)S(1)}, bf16[256,1280]{1,0:T(8,128)(2,1)S(1)}, u32[]{:S(2)}, u32[]{:S(2)}) collective-permute-start(bf16[256,1280]{1,0:T(8,128)(2,1)S(1)} %pair_sum.9.refs_2_), channel_id=1, source_target_pairs={{0,2},{1,3},{2,0},{3,1},{4,6},{5,7},{6,4},{7,5},{8,10},{9,11},{10,... | collective-permute-start | bytes 1966088 | tf_op jit(solution)/shard_map/ppermute | solution.py:395
  91.1 29.7 %collective-permute-start.12 = (bf16[256,1280]{1,0:T(8,128)(2,1)S(1)}, bf16[256,1280]{1,0:T(8,128)(2,1)S(1)}, u32[]{:S(2)}, u32[]{:S(2)}) collective-permute-start(bf16[256,1280]{1,0:T(8,128)(2,1)S(1)} %copy-done.59), channel_id=1, source_target_pairs={{0,1},{1,0},{2,3},{3,2},{4,5},{5,4},{6,7},{7,6},{8,9},{9,8},{10,11... | collective-permute-start | bytes 1966088 | tf_op jit(solution)/shard_map/ppermute | solution.py:395
  91.1 40.5 %collective-permute-start.10 = (bf16[256,1280]{1,0:T(8,128)(2,1)S(1)}, bf16[256,1280]{1,0:T(8,128)(2,1)S(1)}, u32[]{:S(2)}, u32[]{:S(2)}) collective-permute-start(bf16[256,1280]{1,0:T(8,128)(2,1)S(1)} %get-tuple-element.187.refs_0_), channel_id=1, source_target_pairs={{0,2},{1,3},{2,0},{3,1},{4,6},{5,7},{6,4},{7,5},{8,10},{9,11},{10,... | collective-permute-start | bytes 1966088 | tf_op jit(solution)/shard_map/ppermute | solution.py:395
  103.5 28.1 %collective-permute-start.14 = (bf16[256,1280]{1,0:T(8,128)(2,1)S(1)}, bf16[256,1280]{1,0:T(8,128)(2,1)S(1)}, u32[]{:S(2)}, u32[]{:S(2)}) collective-permute-start(bf16[256,1280]{1,0:T(8,128)(2,1)S(1)} %collective-permute-done.13.refs_6_), channel_id=1, source_target_pairs={{0,1},{1,0},{2,3},{3,2},{4,5},{5,4},{6,7},{7,6},{8,9},{9,8},{10,11... | collective-permute-start | bytes 1966088 | tf_op jit(solution)/shard_map/ppermute | solution.py:395
  105.0 40.7 %collective-permute-start.9 = (bf16[256,1280]{1,0:T(8,128)(2,1)S(1)}, bf16[256,1280]{1,0:T(8,128)(2,1)S(1)}, u32[]{:S(2)}, u32[]{:S(2)}) collective-permute-start(bf16[256,1280]{1,0:T(8,128)(2,1)S(1)} %get-tuple-element.187.refs_0_), channel_id=1, source_target_pairs={{0,1},{1,0},{2,3},{3,2},{4,5},{5,4},{6,7},{7,6},{8,9},{9,8},{10,11... | collective-permute-start | bytes 1966088 | tf_op jit(solution)/shard_map/ppermute | solution.py:395
  117.5 28.2 %collective-permute-start.22 = (bf16[256,1280]{1,0:T(8,128)(2,1)}, bf16[256,1280]{1,0:T(8,128)(2,1)}, u32[]{:S(2)}, u32[]{:S(2)}) collective-permute-start(bf16[256,1280]{1,0:T(8,128)(2,1)} %scale_cot.3.refs_7_.refs_4_), channel_id=1, source_target_pairs={{0,2},{1,3},{2,0},{3,1},{4,6},{5,7},{6,4},{7,5},{8,10},{9,11},{10,... | collective-permute-start | bytes 1966088 | tf_op jit(solution)/shard_map/ppermute | solution.py:395
  120.8 38.5 %collective-permute-start.19 = (bf16[256,1280]{1,0:T(8,128)(2,1)}, bf16[256,1280]{1,0:T(8,128)(2,1)}, u32[]{:S(2)}, u32[]{:S(2)}) collective-permute-start(bf16[256,1280]{1,0:T(8,128)(2,1)} %get-tuple-element.194.refs_0_), channel_id=1, source_target_pairs={{0,2},{1,3},{2,0},{3,1},{4,6},{5,7},{6,4},{7,5},{8,10},{9,11},{10,... | collective-permute-start | bytes 1966088 | tf_op jit(solution)/shard_map/ppermute | solution.py:395
  131.6 27.7 %collective-permute-start.11 = (bf16[256,1280]{1,0:T(8,128)(2,1)S(1)}, bf16[256,1280]{1,0:T(8,128)(2,1)S(1)}, u32[]{:S(2)}, u32[]{:S(2)}) collective-permute-start(bf16[256,1280]{1,0:T(8,128)(2,1)S(1)} %collective-permute-done.10.refs_2_), channel_id=1, source_target_pairs={{0,1},{1,0},{2,3},{3,2},{4,5},{5,4},{6,7},{7,6},{8,9},{9,8},{10,11... | collective-permute-start | bytes 1966088 | tf_op jit(solution)/shard_map/ppermute | solution.py:395
  131.6 54.8 %collective-permute-start.21 = (bf16[256,1280]{1,0:T(8,128)(2,1)}, bf16[256,1280]{1,0:T(8,128)(2,1)}, u32[]{:S(2)}, u32[]{:S(2)}) collective-permute-start(bf16[256,1280]{1,0:T(8,128)(2,1)} %scale_cot.3.refs_7_.refs_4_), channel_id=1, source_target_pairs={{0,1},{1,0},{2,3},{3,2},{4,5},{5,4},{6,7},{7,6},{8,9},{9,8},{10,11... | collective-permute-start | bytes 1966088 | tf_op jit(solution)/shard_map/ppermute | solution.py:395
  145.7 40.7 %collective-permute-start.18 = (bf16[256,1280]{1,0:T(8,128)(2,1)}, bf16[256,1280]{1,0:T(8,128)(2,1)}, u32[]{:S(2)}, u32[]{:S(2)}) collective-permute-start(bf16[256,1280]{1,0:T(8,128)(2,1)} %get-tuple-element.194.refs_0_), channel_id=1, source_target_pairs={{0,1},{1,0},{2,3},{3,2},{4,5},{5,4},{6,7},{7,6},{8,9},{9,8},{10,11... | collective-permute-start | bytes 1966088 | tf_op jit(solution)/shard_map/ppermute | solution.py:395
  145.7 40.7 %collective-permute-start.23 = (bf16[256,1280]{1,0:T(8,128)(2,1)}, bf16[256,1280]{1,0:T(8,128)(2,1)}, u32[]{:S(2)}, u32[]{:S(2)}) collective-permute-start(bf16[256,1280]{1,0:T(8,128)(2,1)} %collective-permute-done.22.refs_6_), channel_id=1, source_target_pairs={{0,1},{1,0},{2,3},{3,2},{4,5},{5,4},{6,7},{7,6},{8,9},{9,8},{10,11... | collective-permute-start | bytes 1966088 | tf_op jit(solution)/shard_map/ppermute | solution.py:395
  159.3 27.1 %collective-permute-start.20 = (bf16[256,1280]{1,0:T(8,128)(2,1)}, bf16[256,1280]{1,0:T(8,128)(2,1)}, u32[]{:S(2)}, u32[]{:S(2)}) collective-permute-start(bf16[256,1280]{1,0:T(8,128)(2,1)} %collective-permute-done.19.refs_2_), channel_id=1, source_target_pairs={{0,1},{1,0},{2,3},{3,2},{4,5},{5,4},{6,7},{7,6},{8,9},{9,8},{10,11... | collective-permute-start | bytes 1966088 | tf_op jit(solution)/shard_map/ppermute | solution.py:395
  185.2 18.7 %collective-permute-start.24 = (bf16[256,1280]{1,0:T(8,128)(2,1)}, bf16[256,1280]{1,0:T(8,128)(2,1)}, u32[]{:S(2)}, u32[]{:S(2)}) collective-permute-start(bf16[256,1280]{1,0:T(8,128)(2,1)} %get-tuple-element.202), channel_id=1, source_target_pairs={{0,1},{1,0},{2,3},{3,2},{4,5},{5,4},{6,7},{7,6},{8,9},{9,8},{10,11... | collective-permute-start | bytes 1966088 | tf_op jit(solution)/shard_map/ppermute | solution.py:395
  228.4 13.6 %collective-permute-start.30 = (bf16[256,1280]{1,0:T(8,128)(2,1)}, bf16[256,1280]{1,0:T(8,128)(2,1)S(1)}, u32[]{:S(2)}, u32[]{:S(2)}) collective-permute-start(bf16[256,1280]{1,0:T(8,128)(2,1)} %get-tuple-element.213), channel_id=1, source_target_pairs={{0,1},{1,0},{2,3},{3,2},{4,5},{5,4},{6,7},{7,6},{8,9},{9,8},{10,11... | collective-permute-start | bytes 1966088 | tf_op jit(solution)/shard_map/ppermute | solution.py:395
  228.9 16.9 %collective-permute-start.31 = (bf16[256,1280]{1,0:T(8,128)(2,1)}, bf16[256,1280]{1,0:T(8,128)(2,1)S(1)}, u32[]{:S(2)}, u32[]{:S(2)}) collective-permute-start(bf16[256,1280]{1,0:T(8,128)(2,1)} %pair_sum.10.refs_5_), channel_id=1, source_target_pairs={{0,2},{1,3},{2,0},{3,1},{4,6},{5,7},{6,4},{7,5},{8,10},{9,11},{10,... | collective-permute-start | bytes 1966088 | tf_op jit(solution)/shard_map/ppermute | solution.py:395
  229.7 33.4 %collective-permute-start.25 = (bf16[256,1280]{1,0:T(8,128)(2,1)}, bf16[256,1280]{1,0:T(8,128)(2,1)S(1)}, u32[]{:S(2)}, u32[]{:S(2)}) collective-permute-start(bf16[256,1280]{1,0:T(8,128)(2,1)} %get-tuple-element.205), channel_id=1, source_target_pairs={{0,1},{1,0},{2,3},{3,2},{4,5},{5,4},{6,7},{7,6},{8,9},{9,8},{10,11... | collective-permute-start | bytes 1966088 | tf_op jit(solution)/shard_map/ppermute | solution.py:395
  247.8 17.7 %collective-permute-start.39 = (bf16[256,1280]{1,0:T(8,128)(2,1)S(1)}, bf16[256,1280]{1,0:T(8,128)(2,1)S(1)}, u32[]{:S(2)}, u32[]{:S(2)}) collective-permute-start(bf16[256,1280]{1,0:T(8,128)(2,1)S(1)} %get-tuple-element.225.refs_3_.refs_9_), channel_id=1, source_target_pairs={{0,2},{1,3},{2,0},{3,1},{4,6},{5,7},{6,4},{7,5},{8,10},{9,11},{10,... | collective-permute-start | bytes 1966088 | tf_op jit(solution)/shard_map/ppermute | solution.py:395
  250.6 27.2 %collective-permute-start.27 = (bf16[256,1280]{1,0:T(8,128)(2,1)S(1)}, bf16[256,1280]{1,0:T(8,128)(2,1)S(1)}, u32[]{:S(2)}, u32[]{:S(2)}) collective-permute-start(bf16[256,1280]{1,0:T(8,128)(2,1)S(1)} %pair_sum.11.refs_7_), channel_id=1, source_target_pairs={{0,2},{1,3},{2,0},{3,1},{4,6},{5,7},{6,4},{7,5},{8,10},{9,11},{10,... | collective-permute-start | bytes 1966088 | tf_op jit(solution)/shard_map/ppermute | solution.py:395
  260.9 25.7 %collective-permute-start.34 = (bf16[160,1280]{1,0:T(8,128)(2,1)S(1)}, bf16[160,1280]{1,0:T(8,128)(2,1)S(1)}, u32[]{:S(2)}, u32[]{:S(2)}) collective-permute-start(bf16[160,1280]{1,0:T(8,128)(2,1)S(1)} %get-tuple-element.215.refs_7_), channel_id=1, source_target_pairs={{0,8},{8,16},{16,24},{24,28},{28,20},{20,12},{12,4},{4,0},{1,9},{9... | collective-permute-start | bytes 1228808 | tf_op jit(solution)/shard_map/ppermute | solution.py:422
  262.6 24.1 %collective-permute-start.35 = (bf16[160,1280]{1,0:T(8,128)(2,1)S(1)}, bf16[160,1280]{1,0:T(8,128)(2,1)S(1)}, u32[]{:S(2)}, u32[]{:S(2)}) collective-permute-start(bf16[160,1280]{1,0:T(8,128)(2,1)S(1)} %get-tuple-element.221), channel_id=1, source_target_pairs={{0,4},{8,0},{16,8},{24,16},{28,24},{20,28},{12,20},{4,12},{1,5},{9... | collective-permute-start | bytes 1228808 | tf_op jit(solution)/shard_map/ppermute | solution.py:422
  263.9 26.5 %collective-permute-start.38 = (bf16[256,1280]{1,0:T(8,128)(2,1)S(1)}, bf16[256,1280]{1,0:T(8,128)(2,1)S(1)}, u32[]{:S(2)}, u32[]{:S(2)}) collective-permute-start(bf16[256,1280]{1,0:T(8,128)(2,1)S(1)} %get-tuple-element.225.refs_3_.refs_9_), channel_id=1, source_target_pairs={{0,1},{1,0},{2,3},{3,2},{4,5},{5,4},{6,7},{7,6},{8,9},{9,8},{10,11... | collective-permute-start | bytes 1966088 | tf_op jit(solution)/shard_map/ppermute | solution.py:395
  265.5 25.6 %collective-permute-start.40 = (bf16[256,1280]{1,0:T(8,128)(2,1)S(1)}, bf16[256,1280]{1,0:T(8,128)(2,1)S(1)}, u32[]{:S(2)}, u32[]{:S(2)}) collective-permute-start(bf16[256,1280]{1,0:T(8,128)(2,1)S(1)} %collective-permute-done.39.refs_5_.refs_11_), channel_id=1, source_target_pairs={{0,1},{1,0},{2,3},{3,2},{4,5},{5,4},{6,7},{7,6},{8,9},{9,8},{10,11... | collective-permute-start | bytes 1966088 | tf_op jit(solution)/shard_map/ppermute | solution.py:395
  290.3 14.7 %collective-permute-start.33 = (bf16[256,1280]{1,0:T(8,128)(2,1)}, bf16[256,1280]{1,0:T(8,128)(2,1)S(1)}, u32[]{:S(2)}, u32[]{:S(2)}) collective-permute-start(bf16[256,1280]{1,0:T(8,128)(2,1)} %get-tuple-element.220), channel_id=1, source_target_pairs={{0,1},{1,0},{2,3},{3,2},{4,5},{5,4},{6,7},{7,6},{8,9},{9,8},{10,11... | collective-permute-start | bytes 1966088 | tf_op jit(solution)/shard_map/ppermute | solution.py:395
  290.3 31.4 %collective-permute-start.45 = (bf16[256,1280]{1,0:T(8,128)(2,1)}, bf16[256,1280]{1,0:T(8,128)(2,1)S(1)}, u32[]{:S(2)}, u32[]{:S(2)}) collective-permute-start(bf16[256,1280]{1,0:T(8,128)(2,1)} %get-tuple-element.232.refs_3_.refs_13_), channel_id=1, source_target_pairs={{0,2},{1,3},{2,0},{3,1},{4,6},{5,7},{6,4},{7,5},{8,10},{9,11},{10,... | collective-permute-start | bytes 1966088 | tf_op jit(solution)/shard_map/ppermute | solution.py:395
  303.0 14.4 %collective-permute-start.42 = (bf16[160,1280]{1,0:T(8,128)(2,1)}, bf16[160,1280]{1,0:T(8,128)(2,1)}, u32[]{:S(2)}, u32[]{:S(2)}) collective-permute-start(bf16[160,1280]{1,0:T(8,128)(2,1)} %get-tuple-element.226.refs_2_), channel_id=1, source_target_pairs={{0,8},{8,16},{16,24},{24,28},{28,20},{20,12},{12,4},{4,0},{1,9},{9... | collective-permute-start | bytes 1228808 | tf_op jit(solution)/shard_map/ppermute | solution.py:422
  304.5 12.8 %collective-permute-start.43 = (bf16[160,1280]{1,0:T(8,128)(2,1)}, bf16[160,1280]{1,0:T(8,128)(2,1)}, u32[]{:S(2)}, u32[]{:S(2)}) collective-permute-start(bf16[160,1280]{1,0:T(8,128)(2,1)} %get-tuple-element.229), channel_id=1, source_target_pairs={{0,4},{8,0},{16,8},{24,16},{28,24},{20,28},{12,20},{4,12},{1,5},{9... | collective-permute-start | bytes 1228808 | tf_op jit(solution)/shard_map/ppermute | solution.py:422
  319.7 14.6 %collective-permute-start.47 = (bf16[160,1280]{1,0:T(8,128)(2,1)S(1)}, bf16[160,1280]{1,0:T(8,128)(2,1)S(1)}, u32[]{:S(2)}, u32[]{:S(2)}) collective-permute-start(bf16[160,1280]{1,0:T(8,128)(2,1)S(1)} %get-tuple-element.230.refs_7_), channel_id=1, source_target_pairs={{0,8},{8,16},{16,24},{24,28},{28,20},{20,12},{12,4},{4,0},{1,9},{9... | collective-permute-start | bytes 1228808 | tf_op jit(solution)/shard_map/ppermute | solution.py:422
  321.2 13.0 %collective-permute-start.48 = (bf16[160,1280]{1,0:T(8,128)(2,1)}, bf16[160,1280]{1,0:T(8,128)(2,1)}, u32[]{:S(2)}, u32[]{:S(2)}) collective-permute-start(bf16[160,1280]{1,0:T(8,128)(2,1)} %get-tuple-element.233), channel_id=1, source_target_pairs={{0,4},{8,0},{16,8},{24,16},{28,24},{20,28},{12,20},{4,12},{1,5},{9... | collective-permute-start | bytes 1228808 | tf_op jit(solution)/shard_map/ppermute | solution.py:422
  321.7 16.5 %collective-permute-start.44 = (bf16[256,1280]{1,0:T(8,128)(2,1)}, bf16[256,1280]{1,0:T(8,128)(2,1)}, u32[]{:S(2)}, u32[]{:S(2)}) collective-permute-start(bf16[256,1280]{1,0:T(8,128)(2,1)} %get-tuple-element.232.refs_3_.refs_13_), channel_id=1, source_target_pairs={{0,1},{1,0},{2,3},{3,2},{4,5},{5,4},{6,7},{7,6},{8,9},{9,8},{10,11... | collective-permute-start | bytes 1966088 | tf_op jit(solution)/shard_map/ppermute | solution.py:395
  321.7 16.5 %collective-permute-start.46 = (bf16[256,1280]{1,0:T(8,128)(2,1)S(1)}, bf16[256,1280]{1,0:T(8,128)(2,1)}, u32[]{:S(2)}, u32[]{:S(2)}) collective-permute-start(bf16[256,1280]{1,0:T(8,128)(2,1)S(1)} %collective-permute-done.45.refs_5_.refs_15_), channel_id=1, source_target_pairs={{0,1},{1,0},{2,3},{3,2},{4,5},{5,4},{6,7},{7,6},{8,9},{9,8},{10,11... | collective-permute-start | bytes 1966088 | tf_op jit(solution)/shard_map/ppermute | solution.py:395
  334.0 13.9 %collective-permute-start.51 = (bf16[256,1280]{1,0:T(8,128)(2,1)}, bf16[256,1280]{1,0:T(8,128)(2,1)S(1)}, u32[]{:S(2)}, u32[]{:S(2)}) collective-permute-start(bf16[256,1280]{1,0:T(8,128)(2,1)} %get-tuple-element.238), channel_id=1, source_target_pairs={{0,1},{1,0},{2,3},{3,2},{4,5},{5,4},{6,7},{7,6},{8,9},{9,8},{10,11... | collective-permute-start | bytes 1966088 | tf_op jit(solution)/shard_map/ppermute | solution.py:395
  336.2 12.9 %collective-permute-start.49 = (bf16[160,1280]{1,0:T(8,128)(2,1)S(1)}, bf16[160,1280]{1,0:T(8,128)(2,1)S(1)}, u32[]{:S(2)}, u32[]{:S(2)}) collective-permute-start(bf16[160,1280]{1,0:T(8,128)(2,1)S(1)} %get-tuple-element.235.refs_7_), channel_id=1, source_target_pairs={{0,8},{8,16},{16,24},{24,28},{28,20},{20,12},{12,4},{4,0},{1,9},{9... | collective-permute-start | bytes 1228808 | tf_op jit(solution)/shard_map/ppermute | solution.py:422
  350.7 12.8 %collective-permute-start.52 = (bf16[160,1280]{1,0:T(8,128)(2,1)S(1)}, bf16[160,1280]{1,0:T(8,128)(2,1)S(1)}, u32[]{:S(2)}, u32[]{:S(2)}) collective-permute-start(bf16[160,1280]{1,0:T(8,128)(2,1)S(1)} %get-tuple-element.239.refs_7_), channel_id=1, source_target_pairs={{0,8},{8,16},{16,24},{24,28},{28,20},{20,12},{12,4},{4,0},{1,9},{9... | collective-permute-start | bytes 1228808 | tf_op jit(solution)/shard_map/ppermute | solution.py:422
  366.1 14.5 %collective-permute-start.54 = (bf16[160,1280]{1,0:T(8,128)(2,1)S(1)}, bf16[160,1280]{1,0:T(8,128)(2,1)S(1)}, u32[]{:S(2)}, u32[]{:S(2)}) collective-permute-start(bf16[160,1280]{1,0:T(8,128)(2,1)S(1)} %get-tuple-element.243.refs_7_), channel_id=1, source_target_pairs={{0,8},{8,16},{16,24},{24,28},{28,20},{20,12},{12,4},{4,0},{1,9},{9... | collective-permute-start | bytes 1228808 | tf_op jit(solution)/shard_map/ppermute | solution.py:422
  367.7 12.8 %collective-permute-start.55 = (bf16[160,1280]{1,0:T(8,128)(2,1)S(1)}, bf16[160,1280]{1,0:T(8,128)(2,1)S(1)}, u32[]{:S(2)}, u32[]{:S(2)}) collective-permute-start(bf16[160,1280]{1,0:T(8,128)(2,1)S(1)} %get-tuple-element.244), channel_id=1, source_target_pairs={{0,4},{8,0},{16,8},{24,16},{28,24},{20,28},{12,20},{4,12},{1,5},{9... | collective-permute-start | bytes 1228808 | tf_op jit(solution)/shard_map/ppermute | solution.py:422
  384.1 34.2 %collective-permute-start.58 = (bf16[256,1280]{1,0:T(8,128)(2,1)}, bf16[256,1280]{1,0:T(8,128)(2,1)S(1)}, u32[]{:S(2)}, u32[]{:S(2)}) collective-permute-start(bf16[256,1280]{1,0:T(8,128)(2,1)} %get-tuple-element.254), channel_id=1, source_target_pairs={{0,1},{1,0},{2,3},{3,2},{4,5},{5,4},{6,7},{7,6},{8,9},{9,8},{10,11... | collective-permute-start | bytes 1966088 | tf_op jit(solution)/shard_map/ppermute | solution.py:395
  384.3 35.6 %collective-permute-start.59 = (bf16[256,1280]{1,0:T(8,128)(2,1)}, bf16[256,1280]{1,0:T(8,128)(2,1)S(1)}, u32[]{:S(2)}, u32[]{:S(2)}) collective-permute-start(bf16[256,1280]{1,0:T(8,128)(2,1)} %pair_sum.13.refs_5_), channel_id=1, source_target_pairs={{0,2},{1,3},{2,0},{3,1},{4,6},{5,7},{6,4},{7,5},{8,10},{9,11},{10,... | collective-permute-start | bytes 1966088 | tf_op jit(solution)/shard_map/ppermute | solution.py:395
  385.6 27.6 %collective-permute-start.61 = (bf16[160,1280]{1,0:T(8,128)(2,1)S(1)}, bf16[160,1280]{1,0:T(8,128)(2,1)S(1)}, u32[]{:S(2)}, u32[]{:S(2)}) collective-permute-start(bf16[160,1280]{1,0:T(8,128)(2,1)S(1)} %get-tuple-element.255), channel_id=1, source_target_pairs={{0,4},{8,0},{16,8},{24,16},{28,24},{20,28},{12,20},{4,12},{1,5},{9... | collective-permute-start | bytes 1228808 | tf_op jit(solution)/shard_map/ppermute | solution.py:422
  386.0 54.5 %collective-permute-start.32 = (bf16[256,1280]{1,0:T(8,128)(2,1)S(1)}, bf16[256,1280]{1,0:T(8,128)(2,1)S(1)}, u32[]{:S(2)}, u32[]{:S(2)}) collective-permute-start(bf16[256,1280]{1,0:T(8,128)(2,1)S(1)} %copy-done.97), channel_id=1, source_target_pairs={{0,1},{1,0},{2,3},{3,2},{4,5},{5,4},{6,7},{7,6},{8,9},{9,8},{10,11... | collective-permute-start | bytes 1966088 | tf_op jit(solution)/shard_map/ppermute | solution.py:395
  394.3 47.0 %collective-permute-start.41 = (bf16[256,1280]{1,0:T(8,128)(2,1)S(1)}, bf16[256,1280]{1,0:T(8,128)(2,1)S(1)}, u32[]{:S(2)}, u32[]{:S(2)}) collective-permute-start(bf16[256,1280]{1,0:T(8,128)(2,1)S(1)} %copy-done.86), channel_id=1, source_target_pairs={{0,2},{1,3},{2,0},{3,1},{4,6},{5,7},{6,4},{7,5},{8,10},{9,11},{10,... | collective-permute-start | bytes 1966088 | tf_op jit(solution)/shard_map/ppermute | solution.py:395
  418.3 23.3 %collective-permute-start.65 = (bf16[160,1280]{1,0:T(8,128)(2,1)S(1)}, bf16[160,1280]{1,0:T(8,128)(2,1)S(1)}, u32[]{:S(2)}, u32[]{:S(2)}) collective-permute-start(bf16[160,1280]{1,0:T(8,128)(2,1)S(1)} %get-tuple-element.260.refs_6_), channel_id=1, source_target_pairs={{0,8},{8,16},{16,24},{24,28},{28,20},{20,12},{12,4},{4,0},{1,9},{9... | collective-permute-start | bytes 1228808 | tf_op jit(solution)/shard_map/ppermute | solution.py:422
  419.9 23.2 %collective-permute-start.66 = (bf16[160,1280]{1,0:T(8,128)(2,1)S(1)}, bf16[160,1280]{1,0:T(8,128)(2,1)S(1)}, u32[]{:S(2)}, u32[]{:S(2)}) collective-permute-start(bf16[160,1280]{1,0:T(8,128)(2,1)S(1)} %get-tuple-element.264), channel_id=1, source_target_pairs={{0,4},{8,0},{16,8},{24,16},{28,24},{20,28},{12,20},{4,12},{1,5},{9... | collective-permute-start | bytes 1228808 | tf_op jit(solution)/shard_map/ppermute | solution.py:422
  420.4 14.2 %collective-permute-start.57 = (bf16[160,640]{1,0:T(8,128)(2,1)S(1)}, bf16[160,640]{1,0:T(8,128)(2,1)S(1)}, u32[]{:S(2)}, u32[]{:S(2)}) collective-permute-start(bf16[160,640]{1,0:T(8,128)(2,1)S(1)} %get-tuple-element.250), channel_id=1, source_target_pairs={{0,4},{8,0},{16,8},{24,16},{28,24},{20,28},{12,20},{4,12},{1,5},{9... | collective-permute-start | bytes 614408 | tf_op jit(solution)/shard_map/ppermute | solution.py:422
  434.6 17.4 %collective-permute-start.69 = (bf16[256,1280]{1,0:T(8,128)(2,1)S(1)}, bf16[256,1280]{1,0:T(8,128)(2,1)S(1)}, u32[]{:S(2)}, u32[]{:S(2)}) collective-permute-start(bf16[256,1280]{1,0:T(8,128)(2,1)S(1)} %copy-done.99), channel_id=1, source_target_pairs={{0,1},{1,0},{2,3},{3,2},{4,5},{5,4},{6,7},{7,6},{8,9},{9,8},{10,11... | collective-permute-start | bytes 1966088 | tf_op jit(solution)/shard_map/ppermute | solution.py:395
  440.5 17.2 %collective-permute-start.70 = (bf16[256,1280]{1,0:T(8,128)(2,1)S(1)}, bf16[256,1280]{1,0:T(8,128)(2,1)S(1)}, u32[]{:S(2)}, u32[]{:S(2)}) collective-permute-start(bf16[256,1280]{1,0:T(8,128)(2,1)S(1)} %pair_sum.14.refs_5_), channel_id=1, source_target_pairs={{0,2},{1,3},{2,0},{3,1},{4,6},{5,7},{6,4},{7,5},{8,10},{9,11},{10,... | collective-permute-start | bytes 1966088 | tf_op jit(solution)/shard_map/ppermute | solution.py:395
  441.3 17.6 %collective-permute-start.68 = (bf16[256,1280]{1,0:T(8,128)(2,1)S(1)}, bf16[256,1280]{1,0:T(8,128)(2,1)S(1)}, u32[]{:S(2)}, u32[]{:S(2)}) collective-permute-start(bf16[256,1280]{1,0:T(8,128)(2,1)S(1)} %get-tuple-element.272), channel_id=1, source_target_pairs={{0,1},{1,0},{2,3},{3,2},{4,5},{5,4},{6,7},{7,6},{8,9},{9,8},{10,11... | collective-permute-start | bytes 1966088 | tf_op jit(solution)/shard_map/ppermute | solution.py:395
  462.7 17.7 %collective-permute-start.78 = (bf16[160,1280]{1,0:T(8,128)(2,1)S(1)}, bf16[160,1280]{1,0:T(8,128)(2,1)S(1)}, u32[]{:S(2)}, u32[]{:S(2)}) collective-permute-start(bf16[160,1280]{1,0:T(8,128)(2,1)S(1)} %get-tuple-element.280.refs_5_), channel_id=1, source_target_pairs={{0,8},{8,16},{16,24},{24,28},{28,20},{20,12},{12,4},{4,0},{1,9},{9... | collective-permute-start | bytes 1228808 | tf_op jit(solution)/shard_map/ppermute | solution.py:422
  464.1 17.8 %collective-permute-start.79 = (bf16[160,1280]{1,0:T(8,128)(2,1)S(1)}, bf16[160,1280]{1,0:T(8,128)(2,1)S(1)}, u32[]{:S(2)}, u32[]{:S(2)}) collective-permute-start(bf16[160,1280]{1,0:T(8,128)(2,1)S(1)} %get-tuple-element.283), channel_id=1, source_target_pairs={{0,4},{8,0},{16,8},{24,16},{28,24},{20,28},{12,20},{4,12},{1,5},{9... | collective-permute-start | bytes 1228808 | tf_op jit(solution)/shard_map/ppermute | solution.py:422
  479.7 17.1 %collective-permute-start.71 = (bf16[256,1280]{1,0:T(8,128)(2,1)S(1)}, bf16[256,1280]{1,0:T(8,128)(2,1)S(1)}, u32[]{:S(2)}, u32[]{:S(2)}) collective-permute-start(bf16[256,1280]{1,0:T(8,128)(2,1)S(1)} %pair_sum.15.refs_5_), channel_id=1, source_target_pairs={{0,2},{1,3},{2,0},{3,1},{4,6},{5,7},{6,4},{7,5},{8,10},{9,11},{10,... | collective-permute-start | bytes 1966088 | tf_op jit(solution)/shard_map/ppermute | solution.py:395
  483.7 14.4 %collective-permute-start.87 = (bf16[160,1280]{1,0:T(8,128)(2,1)S(1)}, bf16[160,1280]{1,0:T(8,128)(2,1)S(1)}, u32[]{:S(2)}, u32[]{:S(2)}) collective-permute-start(bf16[160,1280]{1,0:T(8,128)(2,1)S(1)} %get-tuple-element.286.refs_5_), channel_id=1, source_target_pairs={{0,8},{8,16},{16,24},{24,28},{28,20},{20,12},{12,4},{4,0},{1,9},{9... | collective-permute-start | bytes 1228808 | tf_op jit(solution)/shard_map/ppermute | solution.py:422
  484.3 13.7 %collective-permute-start.88 = (bf16[160,1280]{1,0:T(8,128)(2,1)S(1)}, bf16[160,1280]{1,0:T(8,128)(2,1)S(1)}, u32[]{:S(2)}, u32[]{:S(2)}) collective-permute-start(bf16[160,1280]{1,0:T(8,128)(2,1)S(1)} %get-tuple-element.295), channel_id=1, source_target_pairs={{0,4},{8,0},{16,8},{24,16},{28,24},{20,28},{12,20},{4,12},{1,5},{9... | collective-permute-start | bytes 1228808 | tf_op jit(solution)/shard_map/ppermute | solution.py:422
  500.7 12.8 %collective-permute-start.91 = (bf16[160,1280]{1,0:T(8,128)(2,1)}, bf16[160,1280]{1,0:T(8,128)(2,1)}, u32[]{:S(2)}, u32[]{:S(2)}) collective-permute-start(bf16[160,1280]{1,0:T(8,128)(2,1)} %get-tuple-element.298.refs_5_), channel_id=1, source_target_pairs={{0,8},{8,16},{16,24},{24,28},{28,20},{20,12},{12,4},{4,0},{1,9},{9... | collective-permute-start | bytes 1228808 | tf_op jit(solution)/shard_map/ppermute | solution.py:422
  502.6 18.6 %collective-permute-start.89 = (bf16[160,640]{1,0:T(8,128)(2,1)}, bf16[160,640]{1,0:T(8,128)(2,1)S(1)}, u32[]{:S(2)}, u32[]{:S(2)}) collective-permute-start(bf16[160,640]{1,0:T(8,128)(2,1)} %get-tuple-element.299.refs_5_), channel_id=1, source_target_pairs={{0,8},{8,16},{16,24},{24,28},{28,20},{20,12},{12,4},{4,0},{1,9},{9... | collective-permute-start | bytes 614408 | tf_op jit(solution)/shard_map/ppermute | solution.py:422
  503.1 18.1 %collective-permute-start.90 = (bf16[160,640]{1,0:T(8,128)(2,1)}, bf16[160,640]{1,0:T(8,128)(2,1)}, u32[]{:S(2)}, u32[]{:S(2)}) collective-permute-start(bf16[160,640]{1,0:T(8,128)(2,1)} %get-tuple-element.300), channel_id=1, source_target_pairs={{0,4},{8,0},{16,8},{24,16},{28,24},{20,28},{12,20},{4,12},{1,5},{9... | collective-permute-start | bytes 614408 | tf_op jit(solution)/shard_map/ppermute | solution.py:422
  504.7 13.4 %collective-permute-start.92 = (bf16[160,1280]{1,0:T(8,128)(2,1)}, bf16[160,1280]{1,0:T(8,128)(2,1)}, u32[]{:S(2)}, u32[]{:S(2)}) collective-permute-start(bf16[160,1280]{1,0:T(8,128)(2,1)} %get-tuple-element.301), channel_id=1, source_target_pairs={{0,4},{8,0},{16,8},{24,16},{28,24},{20,28},{12,20},{4,12},{1,5},{9... | collective-permute-start | bytes 1228808 | tf_op jit(solution)/shard_map/ppermute | solution.py:422
  (158 other events, 1379.5 us)

commit v3 on v2

v3 whole, which is shorter than its diff:
```python
import functools

import jax
import jax.numpy as jnp
from jax import lax
from jax.experimental import pallas as pl
from jax.experimental.pallas import tpu as pltpu
from jax.sharding import PartitionSpec as P

HEAD = 64
LANES = 128
TILE = 256
norm_eps = 1e-05
score_scale = 0.125
bf16 = jnp.bfloat16
f32 = jnp.float32


class Chain:
    def __init__(self):
        self.last = []
        self.held = []

    def hold(self, *arrays):
        self.held += arrays

    def run(self, body, outs, *ins, smem=(), scratch=(), alias=None, anywhere=(), out_anywhere=(), limit=12, token=0, cover=False):
        unread = [*self.last, *self.held]
        count = len(smem) + len(ins)
        specs = [pl.BlockSpec(memory_space=pltpu.SMEM)] * len(smem)
        specs += [pl.BlockSpec(memory_space=pl.ANY if i in anywhere else pltpu.VMEM) for i in range(len(ins))]
        specs += [pl.BlockSpec(memory_space=pl.ANY)] * len(unread)

        def inner(*refs):
            body(*refs[:count], *refs[count + len(unread) :])

        made = pl.pallas_call(
            inner,
            out_shape=tuple(jax.ShapeDtypeStruct(*o) for o in outs),
            in_specs=specs,
            out_specs=tuple(
                pl.BlockSpec(memory_space=pl.ANY if i in out_anywhere else pltpu.VMEM) for i in range(len(outs))
            ),
            scratch_shapes=scratch,
            input_output_aliases={} if alias is None else {len(smem) + k: v for k, v in alias.items()},
            compiler_params=pltpu.CompilerParams(vmem_limit_bytes=limit << 20),
            cost_estimate=pl.CostEstimate(flops=10**12 if cover else 1, bytes_accessed=1, transcendentals=0),
            name=body.func.__name__ if isinstance(body, functools.partial) else body.__name__,
        )(*smem, *ins, *unread)
        self.last, self.held = [made[token]], []
        return made


def dot32(first, second, first_dim, second_dim):
    return lax.dot_general(
        first, second, (((first_dim,), (second_dim,)), ((), ())), preferred_element_type=f32
    )


def statistics(values):
    average = jnp.mean(values, axis=-1, keepdims=True)
    centred = values - average
    inverse = lax.rsqrt(jnp.mean(centred * centred, axis=-1, keepdims=True) + norm_eps)
    return centred * inverse, inverse


def norm_back(grad, normed, inverse, gain):
    scaled = grad * gain
    mean_one = jnp.mean(scaled, axis=-1, keepdims=True)
    mean_two = jnp.mean(scaled * normed, axis=-1, keepdims=True)
    return inverse * (scaled - mean_one - normed * mean_two)


def of_head(values, j, axis=1):
    if values.shape[axis] <= HEAD:
        return values
    place = lax.broadcasted_iota(jnp.int32, values.shape, axis)
    return jnp.where((place >= HEAD * j) & (place < HEAD * (j + 1)), values, jnp.zeros_like(values))


def head_pairs(width):
    return [(low, min(LANES, width - low)) for low in range(0, width, LANES)]


def mark(out):
    out[...] = jnp.zeros_like(out)


def by_pairs(weight_t, out):
    width = out.shape[0] // 3
    for low, wide in head_pairs(width):
        for j in range(3):
            out[3 * low + j * wide : 3 * low + (j + 1) * wide, :] = weight_t[
                j * width + low : j * width + low + wide, :
            ]


def norm_one(tok, gain, bias, out, *, m):
    normed, _ = statistics(tok[m, 0].astype(f32))
    out[...] = (normed * gain[...].astype(f32) + bias[...].astype(f32)).astype(bf16)


def scale_cot(scale, cot, out, *, m):
    out[...] = (cot[m, 0].astype(f32) * scale[m]).astype(bf16)


def project(*refs, parts):
    blocks = refs[:parts]
    weight, bias, scale = refs[parts : parts + 3]
    out, whole = refs[parts + 3 :]
    rows = blocks[0].shape[0]
    for b in range(parts):
        values = blocks[b][...]
        at = slice(b * rows, (b + 1) * rows)
        whole[at, :] = values
        out[at, :] = ((dot32(values, weight[...], 1, 1) + bias[...]) * scale[...]).astype(bf16)


def attend(qkv, out_weight, attended, logs, *outs, step):
    whole = qkv.shape[0]
    head = 0
    for low, wide in head_pairs(out_weight.shape[0]):
        heads = wide // HEAD
        key_pair = qkv[:, 3 * low + wide : 3 * low + 2 * wide]
        value_t = qkv[:, 3 * low + 2 * wide : 3 * low + 3 * wide].T
        keys = [of_head(key_pair, j) for j in range(heads)]
        values = [of_head(value_t, j, 0) for j in range(heads)]
        for start in range(0, whole, step):
            at = slice(start, start + step)
            query = qkv[at, 3 * low : 3 * low + wide]
            total = None
            for j in range(heads):
                scores = dot32(keys[j], query, 1, 1)
                top = jnp.max(scores, axis=0, keepdims=True)
                powers = jnp.exp(scores - top)
                length = jnp.sum(powers, axis=0, keepdims=True)
                mixed = dot32(values[j], powers.astype(bf16), 1, 0) * (1.0 / length)
                total = mixed if total is None else total + mixed
                logs[head + j : head + j + 1, at] = top + jnp.log(length)
            attended[at, low : low + wide] = total.T.astype(bf16)
        head += heads
    put_shares(outs, lambda at: dot32(attended[at, :], out_weight[...], 1, 0), whole)


def put_shares(outs, share_of, whole):
    own, partner, crossing = outs
    rows = own.shape[0]
    for b, (out, at) in enumerate(((own, None), (crossing, 0), (partner, None), (crossing, 1))):
        value = share_of(slice(b * rows, (b + 1) * rows)).astype(bf16)
        if at is None:
            out[...] = value
        else:
            out[at] = value


def pair_sum(first, second, out):
    out[...] = (first[...].astype(f32) + second[1].astype(f32)).astype(bf16)


def three(first, second, third):
    return first[...].astype(f32) + second[0].astype(f32) + third[...].astype(f32)


def norm_two(tok, first, second, third, out_bias, gain, bias, resid, normed, *, m):
    value = tok[m, 0].astype(f32) + three(first, second, third) + out_bias[...].astype(f32)
    resid[...] = value
    hat, _ = statistics(value)
    normed[...] = (hat * gain[...].astype(f32) + bias[...].astype(f32)).astype(bf16)


def feed(*refs, parts):
    normed, grads = refs[:parts], refs[parts : 2 * parts]
    up, up_bias, down = refs[2 * parts : 2 * parts + 3]
    activ, pre_grad, bias_grad, normed_all, grads_all = refs[2 * parts + 3 :]
    rows = normed[0].shape[0]
    for b in range(parts):
        normed_all[b * rows : (b + 1) * rows, :] = normed[b][...]
        grads_all[b * rows : (b + 1) * rows, :] = grads[b][...]
    for low in range(0, up.shape[1], TILE):
        cols = slice(low, low + TILE)
        total = None
        for b in range(parts):
            at = slice(b * rows, (b + 1) * rows)
            pre = dot32(normed[b][...], up[:, cols], 1, 0) + up_bias[:, cols].astype(f32)
            cumul = 0.5 + 0.5 * lax.erf(pre * 0.7071067811865476)
            density = jnp.exp(-0.5 * pre * pre) * 0.3989422804014327
            activ[at, cols] = (pre * cumul).astype(bf16)
            back = dot32(grads[b][...], down[cols, :], 1, 1)
            grad = (back * (cumul + pre * density)).astype(bf16)
            pre_grad[at, cols] = grad
            part = jnp.sum(grad.astype(f32), axis=0, keepdims=True)
            total = part if total is None else total + part
        bias_grad[:, cols] = total


def times(value, weight, *outs):
    put_tiles(outs, lambda at, cols: dot32(value[at, :], weight[:, cols], 1, 0), value.shape[0])


def times_back(value, weight, *outs):
    put_tiles(outs, lambda at, cols: dot32(value[at, :], weight[cols, :], 1, 1), value.shape[0])


def put_tiles(outs, share_of, whole):
    own, partner, crossing = outs
    rows, model = own.shape

    def tile(i, carry):
        cols = pl.ds(pl.multiple_of(i * TILE, TILE), TILE)
        own[:, cols] = share_of(slice(0, rows), cols).astype(bf16)
        crossing[0, :, cols] = share_of(slice(rows, 2 * rows), cols).astype(bf16)
        partner[:, cols] = share_of(slice(2 * rows, 3 * rows), cols).astype(bf16)
        crossing[1, :, cols] = share_of(slice(3 * rows, 4 * rows), cols).astype(bf16)
        return carry

    lax.fori_loop(0, model // TILE, tile, 0)


def weight_grad(place, *refs, pairs, ring):
    firsts, seconds = refs[:pairs], refs[pairs : 2 * pairs]
    chunks, whole = refs[2 * pairs : -1], refs[-1]

    def tile(i, carry):
        rows = pl.ds(pl.multiple_of(i * TILE, TILE), TILE)
        total = None
        for first, second in zip(firsts, seconds):
            part = dot32(first[:, rows], second[...], 0, 0)
            total = part if total is None else total + part
        whole[rows, :] = total.astype(bf16)
        return carry

    lax.fori_loop(0, whole.shape[0] // TILE, tile, 0)
    put_chunks(place, chunks, whole, ring)


def put_chunks(place, chunks, whole, ring):
    for s, chunk in enumerate(chunks):
        size = chunk.shape[0]
        chunk[...] = whole[pl.ds(pl.multiple_of(place[2 * s + ring] * size, size), size), :]


def norm_two_back(scale, cot, resid, first, second, third, gain, out, rounded, sums, *, m):
    top = cot[m, 0].astype(f32) * scale[m]
    grad = three(first, second, third)
    hat, inverse = statistics(resid[...])
    back = top + norm_back(grad, hat, inverse, gain[...].astype(f32))
    out[...] = back
    rounded[...] = back.astype(bf16)
    sums[0:1, :] = jnp.sum(back, axis=0, keepdims=True)
    sums[1:2, :] = jnp.sum(grad * hat, axis=0, keepdims=True)
    sums[2:3, :] = jnp.sum(grad, axis=0, keepdims=True)
    sums[3:4, :] = jnp.sum(top, axis=0, keepdims=True)
    sums[4:8, :] = jnp.zeros_like(sums[4:8, :])


def attend_back(qkv, logs, mixed, out_weight, *refs, parts, step, low, wide):
    grads = refs[:parts]
    out, key_grad, value_grad, given, inner = refs[parts:]
    whole = qkv.shape[0]
    rows = whole // parts
    heads = wide // HEAD
    head = low // HEAD
    ones = jnp.concatenate([of_head(jnp.ones((8, wide), bf16), j) for j in range(heads)], axis=0)
    for b in range(parts):
        at = slice(b * rows, (b + 1) * rows)
        value = dot32(grads[b][...], out_weight[low : low + wide, :], 1, 1).astype(bf16)
        given[at, :] = value
        both = value.astype(f32) * mixed[at, low : low + wide].astype(f32)
        high = both.astype(bf16)
        rest = (both - high.astype(f32)).astype(bf16)
        inner[:, at] = dot32(ones, high, 1, 1) + dot32(ones, rest, 1, 1)
    key_pair = qkv[:, 3 * low + wide : 3 * low + 2 * wide]
    value_pair = qkv[:, 3 * low + 2 * wide : 3 * low + 3 * wide]
    key_t = key_pair.T
    keys = [of_head(key_pair, j) for j in range(heads)]
    values = [of_head(value_pair, j) for j in range(heads)]
    keys_t = [of_head(key_t, j, 0) for j in range(heads)]
    key_grad[...] = jnp.zeros_like(key_grad)
    value_grad[...] = jnp.zeros_like(value_grad)

    def block(i, carry):
        start = pl.multiple_of(i * step, step)
        query = qkv[pl.ds(start, step), 3 * low : 3 * low + wide]
        grad = given[pl.ds(start, step), :]
        total = None
        for j in range(heads):
            scores = dot32(keys[j], query, 1, 1)
            weights = jnp.exp(scores - logs[head + j : head + j + 1, pl.ds(start, step)])
            back = dot32(values[j], grad, 1, 1)
            score_grad = (weights * (back - inner[8 * j : 8 * j + 1, pl.ds(start, step)])).astype(bf16)
            value_grad[...] += dot32(weights.astype(bf16), of_head(grad, j), 1, 0)
            key_grad[...] += dot32(score_grad, of_head(query, j), 1, 0)
            part = dot32(keys_t[j], score_grad, 1, 0)
            total = part if total is None else total + part
        out[pl.ds(start, step), :wide] = (total.T * score_scale).astype(bf16)
        return carry

    lax.fori_loop(0, whole // step, block, 0)
    out[:, wide : 2 * wide] = key_grad[...].astype(bf16)
    out[:, 2 * wide :] = value_grad[...].astype(bf16)


def project_back(*refs, pairs):
    grads, weight, own, partner, crossing, sums = refs[:pairs], refs[pairs], *refs[pairs + 1 :]

    def share_of(at, cols):
        total, low = None, 0
        for grad in grads:
            wide = grad.shape[1]
            part = dot32(grad[at, :], weight[low : low + wide, cols], 1, 0)
            total = part if total is None else total + part
            low += wide
        return total

    put_tiles((own, partner, crossing), share_of, grads[0].shape[0])
    low = 0
    for grad in grads:
        wide = grad.shape[1]
        sums[:, low : low + wide] = jnp.sum(grad[...].astype(f32), axis=0, keepdims=True)
        low += wide


def projection_grad(place, *refs, micros, pairs, parts, count):
    normed, refs = refs[:micros], refs[micros:]
    grads, refs = [refs[m * pairs : (m + 1) * pairs] for m in range(micros)], refs[micros * pairs :]
    tops, refs = [refs[m * parts : (m + 1) * parts] for m in range(micros)], refs[micros * parts :]
    mixed, refs = refs[:micros], refs[micros:]
    chunks, (left, right) = refs[:-2], refs[-2:]
    width = mixed[0].shape[1]
    rows = tops[0][0].shape[0]
    for p, (low, wide) in enumerate(head_pairs(width)):
        total = None
        for m in range(micros):
            part = dot32(grads[m][p][...], normed[m][...], 0, 0)
            total = part if total is None else total + part
        left[low : low + wide, :] = total[:wide].astype(bf16)
        left[width + low : width + low + wide, :] = total[wide : 2 * wide].astype(bf16)
        right[low : low + wide, :] = total[2 * wide :].astype(bf16)
        total = None
        for m in range(micros):
            for b in range(parts):
                part = dot32(mixed[m][b * rows : (b + 1) * rows, low : low + wide], tops[m][b][...], 0, 0)
                total = part if total is None else total + part
        right[width + low : width + low + wide, :] = total.astype(bf16)
    put_chunks(place, chunks[:count], left, 0)
    put_chunks(place, chunks[count:], right, 1)


def ring_add(*refs):
    for i in range(2):
        refs[4 + i][...] = (refs[i][...].astype(f32) + refs[2 + i][...].astype(f32)).astype(bf16)


def ring_store(place, *refs, steps, divided):
    number = len(steps)
    moved, refs = refs[: 2 * number], refs[2 * number :]
    done, first, second, buffer, sems = refs[-5:]
    done[...] = jnp.zeros_like(done)
    size = buffer.shape[1]
    copies = []
    for k, step in enumerate(steps):
        for i in range(2):
            slot = 2 * k + i
            buffer[slot] = moved[slot][...].astype(f32)
            row = pl.multiple_of(place[2 * step + i] * size, size)
            if divided and i == 1:
                row = row + divided
                copy_second = pltpu.make_async_copy(
                    buffer.at[slot], second.at[pl.ds(pl.multiple_of(jnp.maximum(row - first.shape[0], 0), 16), size), :], sems.at[slot]
                )
                copy_first = pltpu.make_async_copy(
                    buffer.at[slot], first.at[pl.ds(pl.multiple_of(jnp.minimum(row, first.shape[0] - size), 16), size), :], sems.at[slot]
                )
                pl.when(row < first.shape[0])(copy_first.start)
                pl.when(row >= first.shape[0])(copy_second.start)
                copies.append(copy_first)
            else:
                target = second if i == 1 else first
                copies.append(pltpu.make_async_copy(buffer.at[slot], target.at[pl.ds(row, size), :], sems.at[slot]))
                copies[-1].start()
    for copy in copies:
        copy.wait()


def norm_one_back(tok, resid_grad, first, second, third, gain, out, sums, *, m):
    grad = three(first, second, third)
    hat, inverse = statistics(tok[m, 0].astype(f32))
    out[...] = resid_grad[...] + norm_back(grad, hat, inverse, gain[...].astype(f32))
    sums[0:4, :] = jnp.zeros_like(sums[0:4, :])
    sums[4:5, :] = jnp.sum(grad * hat, axis=0, keepdims=True)
    sums[5:6, :] = jnp.sum(grad, axis=0, keepdims=True)
    sums[6:8, :] = jnp.zeros_like(sums[6:8, :])


def add_rows(resid, first, second, third, bias, out):
    out[...] = (resid[...] + three(first, second, third) + bias[...].astype(f32)).astype(bf16)


def swap(values, axis, bit):
    return lax.ppermute(values, axis, [(i, i ^ bit) for i in range(lax.axis_size(axis))])


def ring_order(count):
    return list(range(0, count, 2)) + list(range(1, count, 2))[::-1]


def ring_tables(count):
    order = ring_order(count)
    sends = [[0] * (2 * count) for _ in range(count)]
    keeps = [[0] * (2 * count) for _ in range(count)]
    for place, device in enumerate(order):
        for step in range(count):
            for i, d in enumerate((1, -1)):
                sends[device][2 * step + i] = (place - d * (step + 1)) % count
                keeps[device][2 * step + i] = (place - d * step) % count
    return sends, keeps


def butterfly(values, axis):
    bit = 1
    while bit < lax.axis_size(axis):
        values = values + swap(values, axis, bit)
        bit *= 2
    return values


class Rings:
    def __init__(self, chain, keeps, shapes, divided=0):
        self.chain, self.keeps, self.shapes, self.divided = chain, keeps, shapes, divided
        self.count = lax.axis_size("wide")
        order = ring_order(self.count)
        self.perms = [[(order[i], order[(i + d) % self.count]) for i in range(self.count)] for d in (1, -1)]
        self.chunks, self.moving, self.have = [None, None], [None, None], []
        self.step = 1
        self.outs = None

    def start(self, i, chunks):
        self.chunks[i] = chunks
        self.moving[i] = lax.ppermute(chunks[0], "wide", self.perms[i])

    def hold(self, i):
        self.chain.hold(self.moving[i])

    def add(self):
        made = self.chain.run(
            ring_add, [(c.shape, bf16) for c in self.moving], *self.moving, self.chunks[0][self.step], self.chunks[1][self.step]
        )
        self.step += 1
        if self.step == self.count:
            self.have.append(made)
        self.moving = [lax.ppermute(c, "wide", self.perms[i]) for i, c in enumerate(made)]

    def forward(self):
        self.have.append(self.moving)
        self.chain.hold(*self.moving)
        if len(self.have) < self.count:
            self.moving = [lax.ppermute(c, "wide", self.perms[i]) for i, c in enumerate(self.moving)]

    def store(self, steps):
        moved = [c for s in steps for c in self.have[s]]
        kept = () if self.outs is None else self.outs
        made = self.chain.run(
            functools.partial(ring_store, steps=tuple(steps), divided=self.divided),
            [((8, LANES), f32)] + [(s, f32) for s in self.shapes],
            *moved,
            *kept,
            smem=(self.keeps,),
            scratch=[
                pltpu.VMEM((len(moved), *moved[0].shape), f32),
                pltpu.SemaphoreType.DMA((len(moved),)),
            ],
            alias={len(moved): 1, len(moved) + 1: 2} if kept else None,
            anywhere=(len(moved), len(moved) + 1) if kept else (),
            out_anywhere=(1, 2),
            limit=4 + (len(moved) * moved[0].size * 4 >> 20) + 1,
        )
        self.outs = made[1:]


class Whole:
    def __init__(self, shapes, divided=0):
        self.shapes, self.divided = shapes, divided
        self.arrays = [None, None]

    def start(self, i, chunks):
        self.arrays[i] = chunks[0]

    def hold(self, i):
        pass

    def add(self):
        pass

    def forward(self):
        pass

    def store(self, steps):
        if isinstance(self.arrays, list):
            self.arrays = lax.psum(tuple(self.arrays), "wide")
            first, second = (a.astype(f32) for a in self.arrays)
            if self.divided:
                cut = self.shapes[0][0] - self.divided
                first, second = jnp.concatenate([first, second[:cut]], axis=0), second[cut:]
            self.outs = (first, second)


def local(
    tokens,
    cotangent,
    cell_of,
    query_count,
    attn_norm_gain,
    attn_norm_bias,
    input_weight,
    query_bias,
    value_bias,
    out_weight,
    out_bias,
    ffn_norm_gain,
    ffn_norm_bias,
    up_weight,
    up_bias,
    down_weight,
    down_bias,
):
    micros = range(tokens.shape[0])
    rows, model = tokens.shape[2], tokens.shape[3]
    parts = lax.axis_size("narrow")
    whole = rows * parts
    width = input_weight.shape[2]
    hidden = up_weight.shape[1]
    count = lax.axis_size("wide")
    rings = count <= 8
    chunks = count if rings else 1
    pairs = head_pairs(width)
    step = min(512, whole)
    chain = Chain()
    run = chain.run
    index = lax.axis_index("wide")

    block = ((rows, model), bf16)
    outgoing = [block, block, ((2, rows, model), bf16)]
    wide_rows = ((whole, model), bf16)
    row = lambda v: v.reshape(1, -1)
    gain_one, bias_one, gain_two, bias_two = map(row, (attn_norm_gain, attn_norm_bias, ffn_norm_gain, ffn_norm_bias))
    out_bias, down_bias, up_bias = row(out_bias), row(down_bias), row(up_bias)

    slots = index + count * jnp.arange(len(micros), dtype=jnp.int32)
    counts = jnp.stack([query_count[cell_of[slots[m]]] for m in micros])
    scale = jnp.sqrt(counts.astype(f32) / 500.0)
    if rings:
        sends, keeps = (
            lax.dynamic_index_in_dim(jnp.array(t, jnp.int32), index, 0, keepdims=False) for t in ring_tables(count)
        )
    else:
        sends = keeps = jnp.zeros((2,), jnp.int32)

    def columns(three_parts):
        return jnp.concatenate([v[:, low : low + wide] for low, wide in pairs for v in three_parts], axis=1)

    weight_t = jnp.transpose(input_weight, (1, 2, 0)).reshape(3 * width, model)
    zero = jnp.zeros((1, width), f32)
    project_bias = columns([row(query_bias).astype(f32), zero, row(value_bias).astype(f32)])
    project_scale = columns([zero + score_scale, zero + 1.0, zero + 1.0])

    def gather(own):
        partner = swap(own, "narrow", 2)
        return [own, swap(own, "narrow", 1), partner, swap(partner, "narrow", 1)]

    def share(made):
        own, partner, crossing = made
        return [own, partner, swap(crossing, "narrow", 1)]

    def send(shares):
        own, partner, crossed = shares
        (both,) = run(pair_sum, [block], partner, crossed)
        return [own, crossed, swap(both, "narrow", 2)]

    def fresh():
        return [None] * len(micros)

    normed, given, qkv, normed_all, mixed, logs, shares, shares_down, resid, normed_two_b = (fresh() for _ in range(10))
    activ, pre_grad, up_bias_grad, two_all, given_all, resid_grad, top = (fresh() for _ in range(7))
    sums_two, sums_one, stack_sums, out_rows, grad_rows = (fresh() for _ in range(5))
    pair_grads = [[] for _ in micros]

    def do_norm_one(m):
        (own,) = run(functools.partial(norm_one, m=m), [block], tokens, gain_one, bias_one)
        normed[m] = gather(own)

    def do_scale(m):
        (own,) = run(functools.partial(scale_cot, m=m), [block], cotangent, smem=(scale,), cover=m == 0)
        given[m] = gather(own)

    def do_project(m):
        qkv[m], normed_all[m] = run(
            functools.partial(project, parts=parts),
            [((whole, 3 * width), bf16), wide_rows],
            *normed[m],
            weight,
            project_bias,
            project_scale,
        )

    def do_attend(m):
        mixed[m], logs[m], *made = run(
            functools.partial(attend, step=whole),
            [((whole, width), bf16), ((8, whole), f32), *outgoing],
            qkv[m],
            out_weight,
            limit=24,
        )
        shares[m] = share(made)

    def do_send(m):
        shares[m] = send(shares[m])

    def do_norm_two(m):
        resid[m], own = run(
            functools.partial(norm_two, m=m),
            [((rows, model), f32), block],
            tokens,
            *shares[m],
            out_bias,
            gain_two,
            bias_two,
            cover=m == 0,
        )
        normed_two_b[m] = gather(own)

    def do_feed(m):
        activ[m], pre_grad[m], up_bias_grad[m], two_all[m], given_all[m] = run(
            functools.partial(feed, parts=parts),
            [((whole, hidden), bf16), ((whole, hidden), bf16), ((1, hidden), f32), wide_rows, wide_rows],
            *normed_two_b[m],
            *given[m],
            up_weight,
            up_bias,
            down_weight,
        )

    def do_up_back(m):
        shares[m] = share(run(times_back, outgoing, pre_grad[m], up_weight))

    def do_down(m):
        shares_down[m] = share(run(times, outgoing, activ[m], down_weight))

    def do_send_down(m):
        shares_down[m] = send(shares_down[m])

    def do_norm_two_back(m):
        resid_grad[m], own, sums_two[m] = run(
            functools.partial(norm_two_back, m=m),
            [((rows, model), f32), block, ((8, model), f32)],
            cotangent,
            resid[m],
            *shares[m],
            gain_two,
            smem=(scale,),
            cover=True,
        )
        top[m] = gather(own)

    def do_attend_back(m, p):
        low, wide = pairs[p]
        (made,) = run(
            functools.partial(attend_back, parts=parts, step=step, low=low, wide=wide),
            [((whole, 3 * wide), bf16)],
            qkv[m],
            logs[m],
            mixed[m],
            out_weight,
            *top[m],
            scratch=[
                pltpu.VMEM((whole, wide), f32),
                pltpu.VMEM((whole, wide), f32),
                pltpu.VMEM((whole, wide), bf16),
                pltpu.VMEM((8 * (wide // HEAD), whole), f32),
            ],
            limit=20,
        )
        pair_grads[m].append(made)

    def do_project_back(m):
        *made, stack_sums[m] = run(
            functools.partial(project_back, pairs=len(pairs)),
            [*outgoing, ((1, 3 * width), f32)],
            *pair_grads[m],
            weight,
        )
        shares[m] = share(made)

    def do_norm_one_back(m):
        grad_rows[m], sums_one[m] = run(
            functools.partial(norm_one_back, m=m),
            [((rows, model), f32), ((8, model), f32)],
            tokens,
            resid_grad[m],
            *shares[m],
            gain_one,
        )

    def wait(*arrays):
        chain.hold(*arrays)
        run(mark, [((8, LANES), f32)], cover=True)

    def do_add_rows(m):
        (out_rows[m],) = run(add_rows, [block], resid[m], *shares_down[m], down_bias)

    def ffn_grad(firsts, seconds, ring):
        shape = (firsts[0].shape[1], seconds[0].shape[1])
        made = run(
            functools.partial(weight_grad, pairs=len(micros), ring=ring),
            [((shape[0] // chunks, shape[1]), bf16)] * chunks,
            *firsts,
            *seconds,
            smem=(sends,),
            scratch=[pltpu.VMEM(shape, bf16)],
            limit=16,
        )
        ffn.start(ring, made)

    def attn_grad():
        made = run(
            functools.partial(projection_grad, micros=len(micros), pairs=len(pairs), parts=parts, count=chunks),
            [((2 * width // chunks, model), bf16)] * (2 * chunks),
            *normed_all,
            *[g for m in micros for g in pair_grads[m]],
            *[t for m in micros for t in top[m]],
            *mixed,
            smem=(sends,),
            scratch=[pltpu.VMEM((2 * width, model), bf16)] * 2,
            limit=20,
        )
        attn.start(0, made[:chunks])
        attn.start(1, made[chunks:])

    ffn_shapes = [(hidden, model), (model, hidden)]
    attn_shapes = [(3 * width, model), (width, model)]
    ffn = Rings(chain, keeps, ffn_shapes) if rings else Whole(ffn_shapes)
    attn = Rings(chain, keeps, attn_shapes, 2 * width) if rings else Whole(attn_shapes, 2 * width)

    do_norm_one(0)
    (weight,) = run(by_pairs, [((3 * width, model), bf16)], weight_t)
    chain.hold(normed[0][1], normed[0][2])
    do_norm_one(1)
    do_project(0)
    do_attend(0)
    chain.hold(normed[1][1], normed[1][2])
    do_scale(0)
    do_send(0)
    chain.hold(given[0][1])
    do_project(1)
    do_attend(1)
    do_norm_two(0)
    do_send(1)
    chain.hold(normed_two_b[0][1])
    do_scale(1)
    do_norm_two(1)
    chain.hold(given[1][1], normed_two_b[1][1])
    do_feed(0)
    do_up_back(0)
    do_down(0)
    wait(given[1][2], normed_two_b[1][2])
    do_send(0)
    do_feed(1)
    do_up_back(1)
    do_norm_two_back(0)
    do_send(1)
    chain.hold(top[0][1])
    ffn_grad(activ, given_all, 0)
    ffn_grad(two_all, pre_grad, 1)
    ffn.hold(0)
    do_norm_two_back(1)
    chain.hold(top[1][1])
    ffn.add()
    do_attend_back(0, 0)
    ffn.add()
    do_attend_back(0, 1)
    ffn.add()
    do_attend_back(0, 2)
    ffn.add()
    do_attend_back(1, 0)
    do_send_down(0)
    ffn.add()
    do_attend_back(1, 1)
    ffn.add()
    do_attend_back(1, 2)
    ffn.add()
    attn_grad()
    ffn.forward()
    do_project_back(0)
    attn.add()
    do_send(0)
    ffn.forward()
    do_project_back(1)
    attn.add()
    do_send(1)
    ffn.forward()
    do_down(1)
    attn.add()
    do_send_down(1)
    ffn.forward()
    do_norm_one_back(0)
    attn.add()
    ffn.forward()
    do_norm_one_back(1)
    attn.add()
    ffn.forward()
    do_add_rows(0)
    attn.add()
    ffn.forward()
    do_add_rows(1)
    attn.add()
    ffn.store(range(0, 4))
    attn.forward()
    ffn.store(range(4, 8))
    attn.forward()
    attn.forward()
    attn.forward()
    attn.store(range(0, 4))
    attn.forward()
    attn.forward()
    attn.store(range(4, 7))
    attn.forward()
    attn.store(range(7, 8))

    vectors = sums_one[0] + sums_one[1] + sums_two[0] + sums_two[1]
    vectors = butterfly(vectors, "narrow")
    stack_sum = stack_sums[0] + stack_sums[1]
    packed = jnp.concatenate([vectors[:6].reshape(-1), (up_bias_grad[0] + up_bias_grad[1])[0], stack_sum[0]])
    packed = butterfly(packed, "wide")
    vector_sums = packed[: 6 * model].reshape(6, model)
    up_bias_sum = packed[6 * model : 6 * model + hidden]
    stack_sum = packed[6 * model + hidden :]

    def plain(j):
        return jnp.concatenate([stack_sum[3 * low + j * wide : 3 * low + (j + 1) * wide] for low, wide in pairs])

    return (
        jnp.stack(out_rows)[:, None],
        jnp.stack(grad_rows)[:, None],
        vector_sums[4],
        vector_sums[5],
        jnp.transpose(attn.outs[0].reshape(3, width, model), (2, 0, 1)),
        plain(0),
        plain(2),
        attn.outs[1],
        vector_sums[0],
        vector_sums[1],
        vector_sums[2],
        ffn.outs[1],
        up_bias_sum,
        ffn.outs[0],
        vector_sums[3],
    )


def solution(mesh):
    in_specs = (
        P(None, "wide", "narrow", None),
        P(None, "wide", "narrow", None),
        P(),
        P(),
        P(),
        P(),
        P(None, None, "narrow"),
        P("narrow"),
        P("narrow"),
        P("narrow", None),
        P(),
        P(),
        P(),
        P(None, "narrow"),
        P("narrow"),
        P("narrow", None),
        P(),
    )
    out_specs = (
        P(None, "wide", "narrow", None),
        P(None, "wide", "narrow", None),
        P(),
        P(),
        P(None, None, "narrow"),
        P("narrow"),
        P("narrow"),
        P("narrow", None),
        P(),
        P(),
        P(),
        P(None, "narrow"),
        P("narrow"),
        P("narrow", None),
        P(),
    )
    return jax.shard_map(local, mesh=mesh, in_specs=in_specs, out_specs=out_specs, check_vma=False)
```

time: 616 us -> 502 us (0.81)
  Pallas kernels: 246 us -> 194 us
  waiting for transfers between devices: 190 us -> 161 us
  local copies, waits for them, and re-layouts: 61.2 us -> 38.8 us
  starting transfers between devices: 89 us -> 81.6 us
    pallas_call x71 -> x62, Pallas kernels: 246 us -> 194 us  [run(): pl.pallas_call(inner, out_shape=tuple((jax.ShapeDtypeStruct(*o) for o in...]
    ppermute x53 -> x45, waiting for transfers between devices: 104 us -> 72.2 us  [swap(): lax.ppermute(values, axis, [(i, i ^ bit) for i in range(lax.axis_size(axi...]
    unnamed x231 -> x266, local copies, waits for them, and re-layouts: 43.8 us -> 32.8 us
    slice x15 -> x6, local copies, waits for them, and re-layouts: 6.92 us -> 0.02 us  [the longest x4 0.01 us: columns(): v[:, low:low + wide]]
    ppermute x53 -> x45, starting transfers between devices: 29.3 us -> 24.1 us  [swap(): lax.ppermute(values, axis, [(i, i ^ bit) for i in range(lax.axis_size(axi...]
  transfers between devices with their start and end apart: 109 -> 101, of which waited for: 41 -> 41; matrix products, arithmetic and copies ran while one was open for 4% -> 2% of each run, Pallas kernels for 35% -> 36%
where the time goes in v3:
time: 502 us; the launch traced here: 492 us
  Pallas kernels  194 us (39%)
  waiting for transfers between devices  161 us (32%)
  starting transfers between devices  81.6 us (16%)
  local copies, waits for them, and re-layouts  38.8 us (8%)
  between operations  10.5 us (2%)
  other arithmetic  6.08 us (1%)
    pallas_call x62, Pallas kernels, run(): pl.pallas_call(inner, out_shape=tuple((jax.ShapeDtypeStruct(*o) for o in...  194 us
    ppermute x45, waiting for transfers between devices, swap(): lax.ppermute(values, axis, [(i, i ^ bit) for i in range(lax.axis_size(axi...  72.2 us
    ppermute x24, waiting for transfers between devices, forward(): lax.ppermute(c, 'wide', self.perms[i])  34.3 us
    ppermute x28, waiting for transfers between devices, add(): lax.ppermute(c, 'wide', self.perms[i])  33.6 us
    unnamed x266, local copies, waits for them, and re-layouts  32.8 us
    ppermute x28, starting transfers between devices, add(): lax.ppermute(c, 'wide', self.perms[i])  29.5 us
    ppermute x45, starting transfers between devices, swap(): lax.ppermute(values, axis, [(i, i ^ bit) for i in range(lax.axis_size(axi...  24.1 us
    ppermute x24, starting transfers between devices, forward(): lax.ppermute(c, 'wide', self.perms[i])  22.6 us
  transfers between devices with their start and end apart: 101, of which 41 were waited for; matrix products, arithmetic and copies ran while one was open for 2% of the time, Pallas kernels for 36%

profile of v3, /device:TPU:0, one launch (start us, length us, event | category | flops | bytes accessed | tf_op | source)
XLA Modules:
  0.0 492.2 jit_solution(9758964419372756970)
XLA Ops:
  3.8 3.0 collective-permute-start.1
  6.9 14.8 %collective-permute-done.1.refs_5_.refs_2_ = bf16[256,1280]{1,0:T(8,128)(2,1)} collective-permute-done((bf16[256,1280]{1,0:T(8,128)(2,1)S(1)}, bf16[256,1280]{1,0:T(8,128)(2,1)}, u32[]{:S(2)}, u32[]{:S(2)}) %collective-permute-start.1) | collective-permute-done | bytes 655392 | tf_op jit(solution)/shard_map/ppermute | solution.py:400
  25.6 1.7 collective-permute-start.5
  40.9 4.2 project.2
  46.6 10.5 %attend.2 = (bf16[1024,320]{1,0:T(8,128)(2,1)S(1)}, f32[8,1024]{1,0:T(8,128)S(1)}, bf16[256,1280]{1,0:T(8,128)(2,1)S(1)}, bf16[256,1280]{1,0:T(8,128)(2,1)S(1)}, bf16[2,256,1280]{2,1,0:T(8,128)(2,1)}) custom-call(bf16[1024,960]{1,0:T(8,128)(2,1)S(1)} %get-tuple-element.147.refs_0_.refs_2_, bf16[320,1280]{1,0:T(8,128)(2,1)S(1)} %copy-done, ...), custom_call_target="tpu_custom_call" | custom-call | flops 1 | bytes 1 | tf_op jit(solution)/shard_map/attend/pallas_call | solution.py:37
  62.4 1.8 collective-permute-start.12
  64.3 4.4 project.3
  70.3 10.7 %attend.3 = (bf16[1024,320]{1,0:T(8,128)(2,1)S(1)}, f32[8,1024]{1,0:T(8,128)S(1)}, bf16[256,1280]{1,0:T(8,128)(2,1)S(1)}, bf16[256,1280]{1,0:T(8,128)(2,1)S(1)}, bf16[2,256,1280]{2,1,0:T(8,128)(2,1)}) custom-call(bf16[1024,960]{1,0:T(8,128)(2,1)S(1)} %get-tuple-element.152.refs_0_.refs_2_, bf16[320,1280]{1,0:T(8,128)(2,1)S(1)} %copy-done.1, ...), custom_call_target="tpu_custom_call" | custom-call | flops 1 | bytes 1 | tf_op jit(solution)/shard_map/attend/pallas_call | solution.py:37
  81.0 2.3 norm_two.2
  87.1 6.7 %collective-permute-done.12.refs_6_ = bf16[256,1280]{1,0:T(8,128)(2,1)} collective-permute-done((bf16[256,1280]{1,0:T(8,128)(2,1)}, bf16[256,1280]{1,0:T(8,128)(2,1)}, u32[]{:S(2)}, u32[]{:S(2)}) %collective-permute-start.12) | collective-permute-done | bytes 655392 | tf_op jit(solution)/shard_map/ppermute | solution.py:400
  93.8 13.9 %collective-permute-done.10.refs_2_ = bf16[256,1280]{1,0:T(8,128)(2,1)S(1)} collective-permute-done((bf16[256,1280]{1,0:T(8,128)(2,1)S(1)}, bf16[256,1280]{1,0:T(8,128)(2,1)S(1)}, u32[]{:S(2)}, u32[]{:S(2)}) %collective-permute-start.10) | collective-permute-done | bytes 655392 | tf_op jit(solution)/shard_map/ppermute | solution.py:400
  109.3 12.5 %collective-permute-done.15.refs_3_ = bf16[256,1280]{1,0:T(8,128)(2,1)S(1)} collective-permute-done((bf16[256,1280]{1,0:T(8,128)(2,1)S(1)}, bf16[256,1280]{1,0:T(8,128)(2,1)S(1)}, u32[]{:S(2)}, u32[]{:S(2)}) %collective-permute-start.15) | collective-permute-done | bytes 655392 | tf_op jit(solution)/shard_map/ppermute | solution.py:400
  121.8 2.2 norm_two.3
  124.5 11.5 %collective-permute-done.21.refs_1_.refs_6_ = bf16[256,1280]{1,0:T(8,128)(2,1)} collective-permute-done((bf16[256,1280]{1,0:T(8,128)(2,1)S(1)}, bf16[256,1280]{1,0:T(8,128)(2,1)}, u32[]{:S(2)}, u32[]{:S(2)}) %collective-permute-start.21) | collective-permute-done | bytes 655392 | tf_op jit(solution)/shard_map/ppermute | solution.py:400
  136.0 9.2 %feed.2 = (bf16[1024,1280]{1,0:T(8,128)(2,1)S(1)}, bf16[1024,1280]{1,0:T(8,128)(2,1)S(1)}, f32[1,1280]{1,0:T(1,128)S(1)}, bf16[1024,1280]{1,0:T(8,128)(2,1)S(1)}, bf16[1024,1280]{1,0:T(8,128)(2,1)S(1)}) custom-call(bf16[256,1280]{1,0:T(8,128)(2,1)S(1)} %get-tuple-element.155.refs_0_, bf16[256,1280]{1,0:T(8,128)(2,1)S(1)} %collective-permute-done.9.refs_3_.refs_1_, ...), custom_call_target="tpu_custom_call" | custom-call | flops 1 | bytes 1 | tf_op jit(solution)/shard_map/feed/pallas_call | solution.py:37
  146.7 5.6 %times_back.2 = (bf16[256,1280]{1,0:T(8,128)(2,1)S(1)}, bf16[256,1280]{1,0:T(8,128)(2,1)S(1)}, bf16[2,256,1280]{2,1,0:T(8,128)(2,1)}) custom-call(bf16[1024,1280]{1,0:T(8,128)(2,1)S(1)} %get-tuple-element.162.refs_0_.refs_3_, bf16[1280,1280]{1,0:T(8,128)(2,1)S(1)} %copy-done.9, bf16[1024,1280]{1,0:T(8,128)(2,1)S(1)} %get-tuple-element.161.refs_2_.refs_0_.refs_1_), custom_call_target="tpu_custom_call" | custom-call | flops 1 | bytes 1 | tf_op jit(solution)/shard_map/times_back/pallas_call | solution.py:37
  152.3 4.2 times.2
  159.4 2.6 collective-permute-done.23.refs_1_.refs_4_
  163.9 9.2 %feed.3 = (bf16[1024,1280]{1,0:T(8,128)(2,1)S(1)}, bf16[1024,1280]{1,0:T(8,128)(2,1)S(1)}, f32[1,1280]{1,0:T(1,128)S(1)}, bf16[1024,1280]{1,0:T(8,128)(2,1)S(1)}, bf16[1024,1280]{1,0:T(8,128)(2,1)S(1)}) custom-call(bf16[256,1280]{1,0:T(8,128)(2,1)S(1)} %copy-done.94, bf16[256,1280]{1,0:T(8,128)(2,1)S(1)} %copy-done.51, ...), custom_call_target="tpu_custom_call" | custom-call | flops 1 | bytes 1 | tf_op jit(solution)/shard_map/feed/pallas_call | solution.py:37
  174.6 5.4 %times_back.3 = (bf16[256,1280]{1,0:T(8,128)(2,1)S(1)}, bf16[256,1280]{1,0:T(8,128)(2,1)S(1)}, bf16[2,256,1280]{2,1,0:T(8,128)(2,1)}) custom-call(bf16[1024,1280]{1,0:T(8,128)(2,1)S(1)} %get-tuple-element.170.refs_0_.refs_4_, bf16[1280,1280]{1,0:T(8,128)(2,1)S(1)} %copy-done.9, bf16[1024,1280]{1,0:T(8,128)(2,1)S(1)} %get-tuple-element.171.refs_2_.refs_0_), custom_call_target="tpu_custom_call" | custom-call | flops 1 | bytes 1 | tf_op jit(solution)/shard_map/times_back/pallas_call | solution.py:37
  180.5 3.5 norm_two_back.2
  184.2 2.6 pair_sum.11.refs_5_
  190.8 1.7 copy-done.18
  192.5 1.7 copy-done.55
  196.0 8.5 %weight_grad.2 = (bf16[160,1280]{1,0:T(8,128)(2,1)S(1)}, bf16[160,1280]{1,0:T(8,128)(2,1)S(1)}, bf16[160,1280]{1,0:T(8,128)(2,1)S(1)}, bf16[160,1280]{1,0:T(8,12...) custom-call(s32[16]{0:T(128)S(1)} %dynamic-slice_bitcast_fusion.1.re, ...), custom_call_target="tpu_custom_call" | custom-call | flops 1 | bytes 1 | tf_op jit(solution)/shard_map/weight_grad/pallas_call | solution.py:37
  206.7 8.8 %weight_grad.3 = (bf16[160,1280]{1,0:T(8,128)(2,1)S(1)}, bf16[160,1280]{1,0:T(8,128)(2,1)S(1)}, bf16[160,1280]{1,0:T(8,128)(2,1)S(1)}, bf16[160,1280]{1,0:T(8,12...) custom-call(s32[16]{0:T(128)S(1)} %dynamic-slice_bitcast_fusion.1.re, ...), custom_call_target="tpu_custom_call" | custom-call | flops 1 | bytes 1 | tf_op jit(solution)/shard_map/weight_grad/pallas_call | solution.py:37
  216.1 2.8 norm_two_back.3
  220.6 2.4 collective-permute-done.35.refs_6_.refs_11_
  223.0 7.9 %collective-permute-done.32.refs_1_ = bf16[160,1280]{1,0:T(8,128)(2,1)S(1)} collective-permute-done((bf16[160,1280]{1,0:T(8,128)(2,1)S(1)}, bf16[160,1280]{1,0:T(8,128)(2,1)S(1)}, u32[]{:S(2)}, u32[]{:S(2)}) %collective-permute-start.32) | collective-permute-done | bytes 409632 | tf_op jit(solution)/shard_map/ppermute | solution.py:439
  235.3 9.1 %attend_back.6.refs_4_.refs_3_.refs_0_ = bf16[1024,384]{1,0:T(8,128)(2,1)S(1)} custom-call(bf16[1024,960]{1,0:T(8,128)(2,1)S(1)} %copy-done.8, f32[8,1024]{1,0:T(8,128)S(1)} %get-tuple-element.191.refs_1_, bf16[1024,320]{1,0:T(8,128)(2,1)S(1)} %copy-done.20, bf16[320,1280]{1,0:T(8,128)(2,1)S(1)} %copy-done.2, ...), custom_call_target="tpu_custom_call" | custom-call | flops 1 | bytes 1 | tf_op jit(solution)/shard_map/attend_back/pallas_call | solution.py:37
  246.8 9.1 %attend_back.7.refs_4_.refs_1_ = bf16[1024,384]{1,0:T(8,128)(2,1)S(1)} custom-call(bf16[1024,960]{1,0:T(8,128)(2,1)S(1)} %copy-done.8, f32[8,1024]{1,0:T(8,128)S(1)} %get-tuple-element.191.refs_1_, bf16[1024,320]{1,0:T(8,128)(2,1)S(1)} %copy-done.20, bf16[320,1280]{1,0:T(8,128)(2,1)S(1)} %copy-done.2, bf16[256,1280]{1,0:T(8,128)(2,1)} %get-tuple-element.180.refs_4_.refs_9_, ...), custom_call_target="tpu_custom_call" | custom-call | flops 1 | bytes 1 | tf_op jit(solution)/shard_map/attend_back/pallas_call | solution.py:37
  260.6 6.9 %attend_back.8.refs_4_.refs_5_.refs_2_ = bf16[1024,192]{1,0:T(8,128)(2,1)S(1)} custom-call(bf16[1024,960]{1,0:T(8,128)(2,1)S(1)} %copy-done.8, f32[8,1024]{1,0:T(8,128)S(1)} %get-tuple-element.191.refs_1_, bf16[1024,320]{1,0:T(8,128)(2,1)S(1)} %copy-done.20, bf16[320,1280]{1,0:T(8,128)(2,1)S(1)} %copy-done.2, ...), custom_call_target="tpu_custom_call" | custom-call | flops 1 | bytes 1 | tf_op jit(solution)/shard_map/attend_back/pallas_call | solution.py:37
  272.9 7.8 %attend_back.9.refs_2_.refs_6_.refs_0_ = bf16[1024,384]{1,0:T(8,128)(2,1)S(1)} custom-call(bf16[1024,960]{1,0:T(8,128)(2,1)S(1)} %copy-done.6, f32[8,1024]{1,0:T(8,128)S(1)} %get-tuple-element.167.refs_1_, bf16[1024,320]{1,0:T(8,128)(2,1)S(1)} %copy-done.23, bf16[320,1280]{1,0:T(8,128)(2,1)S(1)} %copy-done.2, ...), custom_call_target="tpu_custom_call" | custom-call | flops 1 | bytes 1 | tf_op jit(solution)/shard_map/attend_back/pallas_call | solution.py:37
  284.0 7.8 %attend_back.10.refs_4_.refs_7_.refs_1_ = bf16[1024,384]{1,0:T(8,128)(2,1)S(1)} custom-call(bf16[1024,960]{1,0:T(8,128)(2,1)S(1)} %copy-done.6, f32[8,1024]{1,0:T(8,128)S(1)} %get-tuple-element.167.refs_1_, bf16[1024,320]{1,0:T(8,128)(2,1)S(1)} %copy-done.23, bf16[320,1280]{1,0:T(8,128)(2,1)S(1)} %copy-done.2, ...), custom_call_target="tpu_custom_call" | custom-call | flops 1 | bytes 1 | tf_op jit(solution)/shard_map/attend_back/pallas_call | solution.py:37
  294.6 5.5 %attend_back.11.refs_4_.refs_8_.refs_2_ = bf16[1024,192]{1,0:T(8,128)(2,1)S(1)} custom-call(bf16[1024,960]{1,0:T(8,128)(2,1)S(1)} %copy-done.6, f32[8,1024]{1,0:T(8,128)S(1)} %get-tuple-element.167.refs_1_, bf16[1024,320]{1,0:T(8,128)(2,1)S(1)} %copy-done.23, bf16[320,1280]{1,0:T(8,128)(2,1)S(1)} %copy-done.2, ...), custom_call_target="tpu_custom_call" | custom-call | flops 1 | bytes 1 | tf_op jit(solution)/shard_map/attend_back/pallas_call | solution.py:37
  304.5 9.1 %projection_grad.1 = (bf16[80,1280]{1,0:T(8,128)(2,1)S(1)}, bf16[80,1280]{1,0:T(8,128)(2,1)S(1)}, bf16[80,1280]{1,0:T(8,128)(2,1)S(1)}, bf16[80,1280]{1,0:T(8,12...) custom-call(s32[16]{0:T(128)S(1)} %copy-done.117, ...), custom_call_target="tpu_custom_call" | custom-call | flops 1 | bytes 1 | tf_op jit(solution)/shard_map/projection_grad/pallas_call | solution.py:37
  313.7 4.6 project_back.2
  322.8 12.0 %collective-permute-done.48.refs_0_ = bf16[80,1280]{1,0:T(8,128)(2,1)S(1)} collective-permute-done((bf16[80,1280]{1,0:T(8,128)(2,1)S(1)}, bf16[80,1280]{1,0:T(8,128)(2,1)S(1)}, u32[]{:S(2)}, u32[]{:S(2)}) %collective-permute-start.48) | collective-permute-done | bytes 204832 | tf_op jit(solution)/shard_map/ppermute | solution.py:439
  336.0 4.6 project_back.3
  344.8 12.1 %collective-permute-done.52.refs_0_ = bf16[80,1280]{1,0:T(8,128)(2,1)S(1)} collective-permute-done((bf16[80,1280]{1,0:T(8,128)(2,1)S(1)}, bf16[80,1280]{1,0:T(8,128)(2,1)S(1)}, u32[]{:S(2)}, u32[]{:S(2)}) %collective-permute-start.52) | collective-permute-done | bytes 204832 | tf_op jit(solution)/shard_map/ppermute | solution.py:451
  358.2 1.8 copy-done.4
  360.0 4.2 times.3
  368.5 7.8 %collective-permute-done.66.refs_7_.refs_1_ = bf16[160,1280]{1,0:T(8,128)(2,1)S(1)} collective-permute-done((bf16[160,1280]{1,0:T(8,128)(2,1)S(1)}, bf16[160,1280]{1,0:T(8,128)(2,1)S(1)}, u32[]{:S(2)}, u32[]{:S(2)}) %collective-permute-start.66) | collective-permute-done | bytes 409632 | tf_op jit(solution)/shard_map/ppermute | solution.py:457
  378.2 4.6 collective-permute-done.57.refs_0_
  389.6 5.7 %collective-permute-done.71.refs_7_.refs_3_ = bf16[160,1280]{1,0:T(8,128)(2,1)S(1)} collective-permute-done((bf16[160,1280]{1,0:T(8,128)(2,1)S(1)}, bf16[160,1280]{1,0:T(8,128)(2,1)S(1)}, u32[]{:S(2)}, u32[]{:S(2)}) %collective-permute-start.71) | collective-permute-done | bytes 409632 | tf_op jit(solution)/shard_map/ppermute | solution.py:457
  397.2 2.4 collective-permute-done.62.refs_0_
  404.1 3.2 collective-permute-done.73.refs_6_.refs_5_
  409.2 2.3 collective-permute-done.68.refs_0_
  412.4 1.9 collective-permute-start.75
  437.2 4.3 collective-permute-done.83
  442.1 2.0 collective-permute-start.95
  448.7 1.8 collective-permute-start.89
  451.5 3.9 collective-permute-done.89.refs_7_.refs_12_
  457.5 3.7 collective-permute-done.90.refs_14_.refs_1_
  463.3 3.7 collective-permute-done.91.refs_3_.refs_10_
  467.0 1.9 collective-permute-start.92
  468.9 1.8 collective-permute-done.98.refs_4_.refs_11_
  471.9 3.4 ring_store.5
  475.4 2.4 collective-permute-done.99.refs_6_.refs_13_
  477.8 2.0 collective-permute-start.93
  481.0 4.3 ring_store.6
  485.3 2.3 ring_store.7
  487.6 2.1 ring_store.8
  489.7 2.1 ring_store.9
  (505 shorter events, 140.9 us)
Async XLA Ops:
  3.8 17.9 %collective-permute-start.1 = (bf16[256,1280]{1,0:T(8,128)(2,1)S(1)}, bf16[256,1280]{1,0:T(8,128)(2,1)}, u32[]{:S(2)}, u32[]{:S(2)}) collective-permute-start(bf16[256,1280]{1,0:T(8,128)(2,1)S(1)} %norm_one.2.refs_1_.refs_0_), channel_id=1, source_target_pairs={{0,2},{1,3},{2,0},{3,1},{4,6},{5,7},{6,4},{7,5},{8,10},{9,11},{10,... | collective-permute-start | bytes 1966088 | tf_op jit(solution)/shard_map/ppermute | solution.py:400
  6.9 16.8 %collective-permute-start = (bf16[256,1280]{1,0:T(8,128)(2,1)S(1)}, bf16[256,1280]{1,0:T(8,128)(2,1)S(1)}, u32[]{:S(2)}, u32[]{:S(2)}) collective-permute-start(bf16[256,1280]{1,0:T(8,128)(2,1)S(1)} %norm_one.2.refs_1_.refs_0_), channel_id=1, source_target_pairs={{0,1},{1,0},{2,3},{3,2},{4,5},{5,4},{6,7},{7,6},{8,9},{9,8},{10,11... | collective-permute-start | bytes 1966088 | tf_op jit(solution)/shard_map/ppermute | solution.py:400
  21.7 16.9 %collective-permute-start.2 = (bf16[256,1280]{1,0:T(8,128)(2,1)}, bf16[256,1280]{1,0:T(8,128)(2,1)}, u32[]{:S(2)}, u32[]{:S(2)}) collective-permute-start(bf16[256,1280]{1,0:T(8,128)(2,1)} %collective-permute-done.1.refs_5_.refs_2_), channel_id=1, source_target_pairs={{0,1},{1,0},{2,3},{3,2},{4,5},{5,4},{6,7},{7,6},{8,9},{9,8},{10,11... | collective-permute-start | bytes 1966088 | tf_op jit(solution)/shard_map/ppermute | solution.py:400
  25.6 31.8 %collective-permute-start.5 = (bf16[256,1280]{1,0:T(8,128)(2,1)S(1)}, bf16[256,1280]{1,0:T(8,128)(2,1)}, u32[]{:S(2)}, u32[]{:S(2)}) collective-permute-start(bf16[256,1280]{1,0:T(8,128)(2,1)S(1)} %norm_one.3.refs_7_.refs_0_), channel_id=1, source_target_pairs={{0,2},{1,3},{2,0},{3,1},{4,6},{5,7},{6,4},{7,5},{8,10},{9,11},{10,... | collective-permute-start | bytes 1966088 | tf_op jit(solution)/shard_map/ppermute | solution.py:400
  27.3 30.1 %collective-permute-start.4 = (bf16[256,1280]{1,0:T(8,128)(2,1)S(1)}, bf16[256,1280]{1,0:T(8,128)(2,1)}, u32[]{:S(2)}, u32[]{:S(2)}) collective-permute-start(bf16[256,1280]{1,0:T(8,128)(2,1)S(1)} %norm_one.3.refs_7_.refs_0_), channel_id=1, source_target_pairs={{0,1},{1,0},{2,3},{3,2},{4,5},{5,4},{6,7},{7,6},{8,9},{9,8},{10,11... | collective-permute-start | bytes 1966088 | tf_op jit(solution)/shard_map/ppermute | solution.py:400
  62.0 18.9 %collective-permute-start.6 = (bf16[256,1280]{1,0:T(8,128)(2,1)S(1)}, bf16[256,1280]{1,0:T(8,128)(2,1)S(1)}, u32[]{:S(2)}, u32[]{:S(2)}) collective-permute-start(bf16[256,1280]{1,0:T(8,128)(2,1)S(1)} %pair_sum.8.refs_7_), channel_id=1, source_target_pairs={{0,2},{1,3},{2,0},{3,1},{4,6},{5,7},{6,4},{7,5},{8,10},{9,11},{10,... | collective-permute-start | bytes 1966088 | tf_op jit(solution)/shard_map/ppermute | solution.py:400
  62.4 31.3 %collective-permute-start.12 = (bf16[256,1280]{1,0:T(8,128)(2,1)}, bf16[256,1280]{1,0:T(8,128)(2,1)}, u32[]{:S(2)}, u32[]{:S(2)}) collective-permute-start(bf16[256,1280]{1,0:T(8,128)(2,1)} %scale_cot.2.refs_2_.refs_4_), channel_id=1, source_target_pairs={{0,2},{1,3},{2,0},{3,1},{4,6},{5,7},{6,4},{7,5},{8,10},{9,11},{10,... | collective-permute-start | bytes 1966088 | tf_op jit(solution)/shard_map/ppermute | solution.py:400
  83.3 24.4 %collective-permute-start.10 = (bf16[256,1280]{1,0:T(8,128)(2,1)S(1)}, bf16[256,1280]{1,0:T(8,128)(2,1)S(1)}, u32[]{:S(2)}, u32[]{:S(2)}) collective-permute-start(bf16[256,1280]{1,0:T(8,128)(2,1)S(1)} %get-tuple-element.155.refs_0_), channel_id=1, source_target_pairs={{0,2},{1,3},{2,0},{3,1},{4,6},{5,7},{6,4},{7,5},{8,10},{9,11},{10,... | collective-permute-start | bytes 1966088 | tf_op jit(solution)/shard_map/ppermute | solution.py:400
  83.6 24.1 %collective-permute-start.9 = (bf16[256,1280]{1,0:T(8,128)(2,1)S(1)}, bf16[256,1280]{1,0:T(8,128)(2,1)S(1)}, u32[]{:S(2)}, u32[]{:S(2)}) collective-permute-start(bf16[256,1280]{1,0:T(8,128)(2,1)S(1)} %get-tuple-element.155.refs_0_), channel_id=1, source_target_pairs={{0,1},{1,0},{2,3},{3,2},{4,5},{5,4},{6,7},{7,6},{8,9},{9,8},{10,11... | collective-permute-start | bytes 1966088 | tf_op jit(solution)/shard_map/ppermute | solution.py:400
  85.9 35.9 %collective-permute-start.15 = (bf16[256,1280]{1,0:T(8,128)(2,1)S(1)}, bf16[256,1280]{1,0:T(8,128)(2,1)S(1)}, u32[]{:S(2)}, u32[]{:S(2)}) collective-permute-start(bf16[256,1280]{1,0:T(8,128)(2,1)S(1)} %pair_sum.9.refs_2_), channel_id=1, source_target_pairs={{0,2},{1,3},{2,0},{3,1},{4,6},{5,7},{6,4},{7,5},{8,10},{9,11},{10,... | collective-permute-start | bytes 1966088 | tf_op jit(solution)/shard_map/ppermute | solution.py:400
  93.8 30.3 %collective-permute-start.13 = (bf16[256,1280]{1,0:T(8,128)(2,1)}, bf16[256,1280]{1,0:T(8,128)(2,1)S(1)}, u32[]{:S(2)}, u32[]{:S(2)}) collective-permute-start(bf16[256,1280]{1,0:T(8,128)(2,1)} %collective-permute-done.12.refs_6_), channel_id=1, source_target_pairs={{0,1},{1,0},{2,3},{3,2},{4,5},{5,4},{6,7},{7,6},{8,9},{9,8},{10,11... | collective-permute-start | bytes 1966088 | tf_op jit(solution)/shard_map/ppermute | solution.py:400
  107.7 28.2 %collective-permute-start.11 = (bf16[256,1280]{1,0:T(8,128)(2,1)S(1)}, bf16[256,1280]{1,0:T(8,128)(2,1)S(1)}, u32[]{:S(2)}, u32[]{:S(2)}) collective-permute-start(bf16[256,1280]{1,0:T(8,128)(2,1)S(1)} %collective-permute-done.10.refs_2_), channel_id=1, source_target_pairs={{0,1},{1,0},{2,3},{3,2},{4,5},{5,4},{6,7},{7,6},{8,9},{9,8},{10,11... | collective-permute-start | bytes 1966088 | tf_op jit(solution)/shard_map/ppermute | solution.py:400
  108.4 27.5 %collective-permute-start.16 = (bf16[256,1280]{1,0:T(8,128)(2,1)S(1)}, bf16[256,1280]{1,0:T(8,128)(2,1)S(1)}, u32[]{:S(2)}, u32[]{:S(2)}) collective-permute-start(bf16[256,1280]{1,0:T(8,128)(2,1)S(1)} %scale_cot.3.refs_7_.refs_4_), channel_id=1, source_target_pairs={{0,1},{1,0},{2,3},{3,2},{4,5},{5,4},{6,7},{7,6},{8,9},{9,8},{10,11... | collective-permute-start | bytes 1966088 | tf_op jit(solution)/shard_map/ppermute | solution.py:400
  109.0 26.9 %collective-permute-start.21 = (bf16[256,1280]{1,0:T(8,128)(2,1)S(1)}, bf16[256,1280]{1,0:T(8,128)(2,1)}, u32[]{:S(2)}, u32[]{:S(2)}) collective-permute-start(bf16[256,1280]{1,0:T(8,128)(2,1)S(1)} %scale_cot.3.refs_7_.refs_4_), channel_id=1, source_target_pairs={{0,2},{1,3},{2,0},{3,1},{4,6},{5,7},{6,4},{7,5},{8,10},{9,11},{10,... | collective-permute-start | bytes 1966088 | tf_op jit(solution)/shard_map/ppermute | solution.py:400
  124.0 11.9 %collective-permute-start.17 = (bf16[256,1280]{1,0:T(8,128)(2,1)S(1)}, bf16[256,1280]{1,0:T(8,128)(2,1)S(1)}, u32[]{:S(2)}, u32[]{:S(2)}) collective-permute-start(bf16[256,1280]{1,0:T(8,128)(2,1)S(1)} %get-tuple-element.160.refs_0_), channel_id=1, source_target_pairs={{0,1},{1,0},{2,3},{3,2},{4,5},{5,4},{6,7},{7,6},{8,9},{9,8},{10,11... | collective-permute-start | bytes 1966088 | tf_op jit(solution)/shard_map/ppermute | solution.py:400
  124.1 34.9 %collective-permute-start.19 = (bf16[256,1280]{1,0:T(8,128)(2,1)S(1)}, bf16[256,1280]{1,0:T(8,128)(2,1)}, u32[]{:S(2)}, u32[]{:S(2)}) collective-permute-start(bf16[256,1280]{1,0:T(8,128)(2,1)S(1)} %get-tuple-element.160.refs_0_), channel_id=1, source_target_pairs={{0,2},{1,3},{2,0},{3,1},{4,6},{5,7},{6,4},{7,5},{8,10},{9,11},{10,... | collective-permute-start | bytes 1966088 | tf_op jit(solution)/shard_map/ppermute | solution.py:400
  135.9 27.9 %collective-permute-start.22 = (bf16[256,1280]{1,0:T(8,128)(2,1)}, bf16[256,1280]{1,0:T(8,128)(2,1)}, u32[]{:S(2)}, u32[]{:S(2)}) collective-permute-start(bf16[256,1280]{1,0:T(8,128)(2,1)} %collective-permute-done.21.refs_1_.refs_6_), channel_id=1, source_target_pairs={{0,1},{1,0},{2,3},{3,2},{4,5},{5,4},{6,7},{7,6},{8,9},{9,8},{10,11... | collective-permute-start | bytes 1966088 | tf_op jit(solution)/shard_map/ppermute | solution.py:400
  163.4 17.1 %collective-permute-start.25 = (bf16[256,1280]{1,0:T(8,128)(2,1)S(1)}, bf16[256,1280]{1,0:T(8,128)(2,1)S(1)}, u32[]{:S(2)}, u32[]{:S(2)}) collective-permute-start(bf16[256,1280]{1,0:T(8,128)(2,1)S(1)} %pair_sum.10.refs_11_), channel_id=1, source_target_pairs={{0,2},{1,3},{2,0},{3,1},{4,6},{5,7},{6,4},{7,5},{8,10},{9,11},{10,... | collective-permute-start | bytes 1966088 | tf_op jit(solution)/shard_map/ppermute | solution.py:400
  186.8 29.3 %collective-permute-start.26 = (bf16[256,1280]{1,0:T(8,128)(2,1)}, bf16[256,1280]{1,0:T(8,128)(2,1)}, u32[]{:S(2)}, u32[]{:S(2)}) collective-permute-start(bf16[256,1280]{1,0:T(8,128)(2,1)} %pair_sum.11.refs_5_), channel_id=1, source_target_pairs={{0,2},{1,3},{2,0},{3,1},{4,6},{5,7},{6,4},{7,5},{8,10},{9,11},{10,... | collective-permute-start | bytes 1966088 | tf_op jit(solution)/shard_map/ppermute | solution.py:400
  204.5 11.6 %collective-permute-start.28 = (bf16[160,1280]{1,0:T(8,128)(2,1)S(1)}, bf16[160,1280]{1,0:T(8,128)(2,1)S(1)}, u32[]{:S(2)}, u32[]{:S(2)}) collective-permute-start(bf16[160,1280]{1,0:T(8,128)(2,1)S(1)} %get-tuple-element.181.refs_5_), channel_id=1, source_target_pairs={{0,8},{8,16},{16,24},{24,28},{28,20},{20,12},{12,4},{4,0},{1,9},{9... | collective-permute-start | bytes 1228808 | tf_op jit(solution)/shard_map/ppermute | solution.py:439
  206.2 16.8 %collective-permute-start.35 = (bf16[256,1280]{1,0:T(8,128)(2,1)}, bf16[256,1280]{1,0:T(8,128)(2,1)}, u32[]{:S(2)}, u32[]{:S(2)}) collective-permute-start(bf16[256,1280]{1,0:T(8,128)(2,1)} %get-tuple-element.180.refs_4_.refs_9_), channel_id=1, source_target_pairs={{0,2},{1,3},{2,0},{3,1},{4,6},{5,7},{6,4},{7,5},{8,10},{9,11},{10,... | collective-permute-start | bytes 1966088 | tf_op jit(solution)/shard_map/ppermute | solution.py:400
  219.0 11.9 %collective-permute-start.29 = (bf16[256,1280]{1,0:T(8,128)(2,1)S(1)}, bf16[256,1280]{1,0:T(8,128)(2,1)S(1)}, u32[]{:S(2)}, u32[]{:S(2)}) collective-permute-start(bf16[256,1280]{1,0:T(8,128)(2,1)S(1)} %get-tuple-element.183.refs_4_.refs_13_), channel_id=1, source_target_pairs={{0,1},{1,0},{2,3},{3,2},{4,5},{5,4},{6,7},{7,6},{8,9},{9,8},{10,11... | collective-permute-start | bytes 1966088 | tf_op jit(solution)/shard_map/ppermute | solution.py:400
  219.0 11.9 %collective-permute-start.32 = (bf16[160,1280]{1,0:T(8,128)(2,1)S(1)}, bf16[160,1280]{1,0:T(8,128)(2,1)S(1)}, u32[]{:S(2)}, u32[]{:S(2)}) collective-permute-start(bf16[160,1280]{1,0:T(8,128)(2,1)S(1)} %get-tuple-element.182.refs_7_), channel_id=1, source_target_pairs={{0,4},{8,0},{16,8},{24,16},{28,24},{20,28},{12,20},{4,12},{1,5},{9... | collective-permute-start | bytes 1228808 | tf_op jit(solution)/shard_map/ppermute | solution.py:439
  223.0 11.2 %collective-permute-start.36 = (bf16[256,1280]{1,0:T(8,128)(2,1)}, bf16[256,1280]{1,0:T(8,128)(2,1)S(1)}, u32[]{:S(2)}, u32[]{:S(2)}) collective-permute-start(bf16[256,1280]{1,0:T(8,128)(2,1)} %collective-permute-done.35.refs_6_.refs_11_), channel_id=1, source_target_pairs={{0,1},{1,0},{2,3},{3,2},{4,5},{5,4},{6,7},{7,6},{8,9},{9,8},{10,11... | collective-permute-start | bytes 1966088 | tf_op jit(solution)/shard_map/ppermute | solution.py:400
  231.1 13.3 %collective-permute-start.33 = (bf16[160,1280]{1,0:T(8,128)(2,1)S(1)}, bf16[160,1280]{1,0:T(8,128)(2,1)S(1)}, u32[]{:S(2)}, u32[]{:S(2)}) collective-permute-start(bf16[160,1280]{1,0:T(8,128)(2,1)S(1)} %get-tuple-element.187.refs_8_), channel_id=1, source_target_pairs={{0,8},{8,16},{16,24},{24,28},{28,20},{20,12},{12,4},{4,0},{1,9},{9... | collective-permute-start | bytes 1228808 | tf_op jit(solution)/shard_map/ppermute | solution.py:451
  232.7 11.7 %collective-permute-start.34 = (bf16[160,1280]{1,0:T(8,128)(2,1)S(1)}, bf16[160,1280]{1,0:T(8,128)(2,1)S(1)}, u32[]{:S(2)}, u32[]{:S(2)}) collective-permute-start(bf16[160,1280]{1,0:T(8,128)(2,1)S(1)} %get-tuple-element.188), channel_id=1, source_target_pairs={{0,4},{8,0},{16,8},{24,16},{28,24},{20,28},{12,20},{4,12},{1,5},{9... | collective-permute-start | bytes 1228808 | tf_op jit(solution)/shard_map/ppermute | solution.py:451
  233.2 27.4 %collective-permute-start.30 = (bf16[256,1280]{1,0:T(8,128)(2,1)S(1)}, bf16[256,1280]{1,0:T(8,128)(2,1)S(1)}, u32[]{:S(2)}, u32[]{:S(2)}) collective-permute-start(bf16[256,1280]{1,0:T(8,128)(2,1)S(1)} %get-tuple-element.183.refs_4_.refs_13_), channel_id=1, source_target_pairs={{0,2},{1,3},{2,0},{3,1},{4,6},{5,7},{6,4},{7,5},{8,10},{9,11},{10,... | collective-permute-start | bytes 1966088 | tf_op jit(solution)/shard_map/ppermute | solution.py:400
  234.2 46.5 %collective-permute-start.18 = (bf16[2,256,1280]{2,1,0:T(8,128)(2,1)}, bf16[2,256,1280]{2,1,0:T(8,128)(2,1)S(1)}, u32[]{:S(2)}, u32[]{:S(2)}) collective-permute-start(bf16[2,256,1280]{2,1,0:T(8,128)(2,1)} %copy-done.121), channel_id=1, source_target_pairs={{0,1},{1,0},{2,3},{3,2},{4,5},{5,4},{6,7},{7,6},{8,9},{9,8},{10,11... | collective-permute-start | bytes 3932168 | tf_op jit(solution)/shard_map/ppermute | solution.py:400
  244.7 11.9 %collective-permute-start.37 = (bf16[160,1280]{1,0:T(8,128)(2,1)S(1)}, bf16[160,1280]{1,0:T(8,128)(2,1)S(1)}, u32[]{:S(2)}, u32[]{:S(2)}) collective-permute-start(bf16[160,1280]{1,0:T(8,128)(2,1)S(1)} %get-tuple-element.192.refs_8_), channel_id=1, source_target_pairs={{0,8},{8,16},{16,24},{24,28},{28,20},{20,12},{12,4},{4,0},{1,9},{9... | collective-permute-start | bytes 1228808 | tf_op jit(solution)/shard_map/ppermute | solution.py:451
  246.3 11.6 %collective-permute-start.38 = (bf16[160,1280]{1,0:T(8,128)(2,1)S(1)}, bf16[160,1280]{1,0:T(8,128)(2,1)S(1)}, u32[]{:S(2)}, u32[]{:S(2)}) collective-permute-start(bf16[160,1280]{1,0:T(8,128)(2,1)S(1)} %get-tuple-element.193), channel_id=1, source_target_pairs={{0,4},{8,0},{16,8},{24,16},{28,24},{20,28},{12,20},{4,12},{1,5},{9... | collective-permute-start | bytes 1228808 | tf_op jit(solution)/shard_map/ppermute | solution.py:451
  258.1 10.8 %collective-permute-start.39 = (bf16[160,1280]{1,0:T(8,128)(2,1)S(1)}, bf16[160,1280]{1,0:T(8,128)(2,1)S(1)}, u32[]{:S(2)}, u32[]{:S(2)}) collective-permute-start(bf16[160,1280]{1,0:T(8,128)(2,1)S(1)} %get-tuple-element.196.refs_8_), channel_id=1, source_target_pairs={{0,8},{8,16},{16,24},{24,28},{28,20},{20,12},{12,4},{4,0},{1,9},{9... | collective-permute-start | bytes 1228808 | tf_op jit(solution)/shard_map/ppermute | solution.py:451
  259.8 10.9 %collective-permute-start.40 = (bf16[160,1280]{1,0:T(8,128)(2,1)S(1)}, bf16[160,1280]{1,0:T(8,128)(2,1)S(1)}, u32[]{:S(2)}, u32[]{:S(2)}) collective-permute-start(bf16[160,1280]{1,0:T(8,128)(2,1)S(1)} %get-tuple-element.197), channel_id=1, source_target_pairs={{0,4},{8,0},{16,8},{24,16},{28,24},{20,28},{12,20},{4,12},{1,5},{9... | collective-permute-start | bytes 1228808 | tf_op jit(solution)/shard_map/ppermute | solution.py:451
  260.6 12.3 %collective-permute-start.31 = (bf16[256,1280]{1,0:T(8,128)(2,1)S(1)}, bf16[256,1280]{1,0:T(8,128)(2,1)S(1)}, u32[]{:S(2)}, u32[]{:S(2)}) collective-permute-start(bf16[256,1280]{1,0:T(8,128)(2,1)S(1)} %collective-permute-done.30.refs_6_.refs_15_), channel_id=1, source_target_pairs={{0,1},{1,0},{2,3},{3,2},{4,5},{5,4},{6,7},{7,6},{8,9},{9,8},{10,11... | collective-permute-start | bytes 1966088 | tf_op jit(solution)/shard_map/ppermute | solution.py:400
  270.8 10.9 %collective-permute-start.42 = (bf16[160,1280]{1,0:T(8,128)(2,1)S(1)}, bf16[160,1280]{1,0:T(8,128)(2,1)S(1)}, u32[]{:S(2)}, u32[]{:S(2)}) collective-permute-start(bf16[160,1280]{1,0:T(8,128)(2,1)S(1)} %get-tuple-element.200.refs_8_), channel_id=1, source_target_pairs={{0,8},{8,16},{16,24},{24,28},{28,20},{20,12},{12,4},{4,0},{1,9},{9... | collective-permute-start | bytes 1228808 | tf_op jit(solution)/shard_map/ppermute | solution.py:451
  282.0 9.9 %collective-permute-start.44 = (bf16[160,1280]{1,0:T(8,128)(2,1)S(1)}, bf16[160,1280]{1,0:T(8,128)(2,1)S(1)}, u32[]{:S(2)}, u32[]{:S(2)}) collective-permute-start(bf16[160,1280]{1,0:T(8,128)(2,1)S(1)} %get-tuple-element.206.refs_8_), channel_id=1, source_target_pairs={{0,8},{8,16},{16,24},{24,28},{28,20},{20,12},{12,4},{4,0},{1,9},{9... | collective-permute-start | bytes 1228808 | tf_op jit(solution)/shard_map/ppermute | solution.py:451
  302.4 11.3 %collective-permute-start.50 = (bf16[160,1280]{1,0:T(8,128)(2,1)S(1)}, bf16[160,1280]{1,0:T(8,128)(2,1)S(1)}, u32[]{:S(2)}, u32[]{:S(2)}) collective-permute-start(bf16[160,1280]{1,0:T(8,128)(2,1)S(1)} %get-tuple-element.214.refs_19_.refs_1_), channel_id=1, source_target_pairs={{0,8},{8,16},{16,24},{24,28},{28,20},{20,12},{12,4},{4,0},{1,9},{9... | collective-permute-start | bytes 1228808 | tf_op jit(solution)/shard_map/ppermute | solution.py:451
  303.7 10.0 %collective-permute-start.51 = (bf16[160,1280]{1,0:T(8,128)(2,1)S(1)}, bf16[160,1280]{1,0:T(8,128)(2,1)S(1)}, u32[]{:S(2)}, u32[]{:S(2)}) collective-permute-start(bf16[160,1280]{1,0:T(8,128)(2,1)S(1)} %get-tuple-element.219.refs_2_), channel_id=1, source_target_pairs={{0,4},{8,0},{16,8},{24,16},{28,24},{20,28},{12,20},{4,12},{1,5},{9... | collective-permute-start | bytes 1228808 | tf_op jit(solution)/shard_map/ppermute | solution.py:451
  318.4 17.4 %collective-permute-start.54 = (bf16[2,256,1280]{2,1,0:T(8,128)(2,1)S(1)}, bf16[2,256,1280]{2,1,0:T(8,128)(2,1)S(1)}, u32[]{:S(2)}, u32[]{:S(2)}) collective-permute-start(bf16[2,256,1280]{2,1,0:T(8,128)(2,1)S(1)} %get-tuple-element.226), channel_id=1, source_target_pairs={{0,1},{1,0},{2,3},{3,2},{4,5},{5,4},{6,7},{7,6},{8,9},{9,8},{10,11... | collective-permute-start | bytes 3932168 | tf_op jit(solution)/shard_map/ppermute | solution.py:400
  318.5 17.5 %collective-permute-start.55 = (bf16[160,1280]{1,0:T(8,128)(2,1)S(1)}, bf16[160,1280]{1,0:T(8,128)(2,1)S(1)}, u32[]{:S(2)}, u32[]{:S(2)}) collective-permute-start(bf16[160,1280]{1,0:T(8,128)(2,1)S(1)} %collective-permute-done.50.refs_5_.refs_3_), channel_id=1, source_target_pairs={{0,8},{8,16},{16,24},{24,28},{28,20},{20,12},{12,4},{4,0},{1,9},{9... | collective-permute-start | bytes 1228808 | tf_op jit(solution)/shard_map/ppermute | solution.py:457
  319.8 16.2 %collective-permute-start.56 = (bf16[160,1280]{1,0:T(8,128)(2,1)S(1)}, bf16[160,1280]{1,0:T(8,128)(2,1)S(1)}, u32[]{:S(2)}, u32[]{:S(2)}) collective-permute-start(bf16[160,1280]{1,0:T(8,128)(2,1)S(1)} %collective-permute-done.51.refs_6_.refs_4_), channel_id=1, source_target_pairs={{0,4},{8,0},{16,8},{24,16},{28,24},{20,28},{12,20},{4,12},{1,5},{9... | collective-permute-start | bytes 1228808 | tf_op jit(solution)/shard_map/ppermute | solution.py:457
  320.6 14.2 %collective-permute-start.48 = (bf16[80,1280]{1,0:T(8,128)(2,1)S(1)}, bf16[80,1280]{1,0:T(8,128)(2,1)S(1)}, u32[]{:S(2)}, u32[]{:S(2)}) collective-permute-start(bf16[80,1280]{1,0:T(8,128)(2,1)S(1)} %get-tuple-element.215.refs_4_), channel_id=1, source_target_pairs={{0,8},{8,16},{16,24},{24,28},{28,20},{20,12},{12,4},{4,0},{1,9},{9... | collective-permute-start | bytes 614408 | tf_op jit(solution)/shard_map/ppermute | solution.py:439
  321.8 13.9 %collective-permute-start.49 = (bf16[80,1280]{1,0:T(8,128)(2,1)S(1)}, bf16[80,1280]{1,0:T(8,128)(2,1)S(1)}, u32[]{:S(2)}, u32[]{:S(2)}) collective-permute-start(bf16[80,1280]{1,0:T(8,128)(2,1)S(1)} %get-tuple-element.216), channel_id=1, source_target_pairs={{0,4},{8,0},{16,8},{24,16},{28,24},{20,28},{12,20},{4,12},{1,5},{9... | collective-permute-start | bytes 614408 | tf_op jit(solution)/shard_map/ppermute | solution.py:439
  340.7 17.4 %collective-permute-start.59 = (bf16[2,256,1280]{2,1,0:T(8,128)(2,1)S(1)}, bf16[2,256,1280]{2,1,0:T(8,128)(2,1)S(1)}, u32[]{:S(2)}, u32[]{:S(2)}) collective-permute-start(bf16[2,256,1280]{2,1,0:T(8,128)(2,1)S(1)} %get-tuple-element.233), channel_id=1, source_target_pairs={{0,1},{1,0},{2,3},{3,2},{4,5},{5,4},{6,7},{7,6},{8,9},{9,8},{10,11... | collective-permute-start | bytes 3932168 | tf_op jit(solution)/shard_map/ppermute | solution.py:400
  340.7 17.5 %collective-permute-start.60 = (bf16[160,1280]{1,0:T(8,128)(2,1)S(1)}, bf16[160,1280]{1,0:T(8,128)(2,1)S(1)}, u32[]{:S(2)}, u32[]{:S(2)}) collective-permute-start(bf16[160,1280]{1,0:T(8,128)(2,1)S(1)} %collective-permute-done.55.refs_5_), channel_id=1, source_target_pairs={{0,8},{8,16},{16,24},{24,28},{28,20},{20,12},{12,4},{4,0},{1,9},{9... | collective-permute-start | bytes 1228808 | tf_op jit(solution)/shard_map/ppermute | solution.py:457
  342.0 16.2 %collective-permute-start.61 = (bf16[160,1280]{1,0:T(8,128)(2,1)S(1)}, bf16[160,1280]{1,0:T(8,128)(2,1)S(1)}, u32[]{:S(2)}, u32[]{:S(2)}) collective-permute-start(bf16[160,1280]{1,0:T(8,128)(2,1)S(1)} %collective-permute-done.56.refs_6_), channel_id=1, source_target_pairs={{0,4},{8,0},{16,8},{24,16},{28,24},{20,28},{12,20},{4,12},{1,5},{9... | collective-permute-start | bytes 1228808 | tf_op jit(solution)/shard_map/ppermute | solution.py:457
  342.8 14.2 %collective-permute-start.52 = (bf16[80,1280]{1,0:T(8,128)(2,1)S(1)}, bf16[80,1280]{1,0:T(8,128)(2,1)S(1)}, u32[]{:S(2)}, u32[]{:S(2)}) collective-permute-start(bf16[80,1280]{1,0:T(8,128)(2,1)S(1)} %get-tuple-element.221.refs_2_), channel_id=1, source_target_pairs={{0,8},{8,16},{16,24},{24,28},{28,20},{20,12},{12,4},{4,0},{1,9},{9... | collective-permute-start | bytes 614408 | tf_op jit(solution)/shard_map/ppermute | solution.py:451
  344.0 13.9 %collective-permute-start.53 = (bf16[80,1280]{1,0:T(8,128)(2,1)S(1)}, bf16[80,1280]{1,0:T(8,128)(2,1)S(1)}, u32[]{:S(2)}, u32[]{:S(2)}) collective-permute-start(bf16[80,1280]{1,0:T(8,128)(2,1)S(1)} %get-tuple-element.222), channel_id=1, source_target_pairs={{0,4},{8,0},{16,8},{24,16},{28,24},{20,28},{12,20},{4,12},{1,5},{9... | collective-permute-start | bytes 614408 | tf_op jit(solution)/shard_map/ppermute | solution.py:451
  364.3 21.1 %collective-permute-start.65 = (bf16[2,256,1280]{2,1,0:T(8,128)(2,1)S(1)}, bf16[2,256,1280]{2,1,0:T(8,128)(2,1)S(1)}, u32[]{:S(2)}, u32[]{:S(2)}) collective-permute-start(bf16[2,256,1280]{2,1,0:T(8,128)(2,1)S(1)} %get-tuple-element.240), channel_id=1, source_target_pairs={{0,1},{1,0},{2,3},{3,2},{4,5},{5,4},{6,7},{7,6},{8,9},{9,8},{10,11... | collective-permute-start | bytes 3932168 | tf_op jit(solution)/shard_map/ppermute | solution.py:400
  364.4 11.9 %collective-permute-start.66 = (bf16[160,1280]{1,0:T(8,128)(2,1)S(1)}, bf16[160,1280]{1,0:T(8,128)(2,1)S(1)}, u32[]{:S(2)}, u32[]{:S(2)}) collective-permute-start(bf16[160,1280]{1,0:T(8,128)(2,1)S(1)} %collective-permute-done.60.refs_3_.refs_7_), channel_id=1, source_target_pairs={{0,8},{8,16},{16,24},{24,28},{28,20},{20,12},{12,4},{4,0},{1,9},{9... | collective-permute-start | bytes 1228808 | tf_op jit(solution)/shard_map/ppermute | solution.py:457
  364.7 11.8 %collective-permute-start.67 = (bf16[160,1280]{1,0:T(8,128)(2,1)S(1)}, bf16[160,1280]{1,0:T(8,128)(2,1)S(1)}, u32[]{:S(2)}, u32[]{:S(2)}) collective-permute-start(bf16[160,1280]{1,0:T(8,128)(2,1)S(1)} %collective-permute-done.61.refs_4_.refs_8_), channel_id=1, source_target_pairs={{0,4},{8,0},{16,8},{24,16},{28,24},{20,28},{12,20},{4,12},{1,5},{9... | collective-permute-start | bytes 1228808 | tf_op jit(solution)/shard_map/ppermute | solution.py:457
  366.4 18.6 %collective-permute-start.64 = (bf16[256,1280]{1,0:T(8,128)(2,1)S(1)}, bf16[256,1280]{1,0:T(8,128)(2,1)S(1)}, u32[]{:S(2)}, u32[]{:S(2)}) collective-permute-start(bf16[256,1280]{1,0:T(8,128)(2,1)S(1)} %pair_sum.13.refs_4_), channel_id=1, source_target_pairs={{0,2},{1,3},{2,0},{3,1},{4,6},{5,7},{6,4},{7,5},{8,10},{9,11},{10,... | collective-permute-start | bytes 1966088 | tf_op jit(solution)/shard_map/ppermute | solution.py:400
  367.9 32.7 %collective-permute-start.70 = (bf16[256,1280]{1,0:T(8,128)(2,1)S(1)}, bf16[256,1280]{1,0:T(8,128)(2,1)S(1)}, u32[]{:S(2)}, u32[]{:S(2)}) collective-permute-start(bf16[256,1280]{1,0:T(8,128)(2,1)S(1)} %pair_sum.14.refs_2_), channel_id=1, source_target_pairs={{0,2},{1,3},{2,0},{3,1},{4,6},{5,7},{6,4},{7,5},{8,10},{9,11},{10,... | collective-permute-start | bytes 1966088 | tf_op jit(solution)/shard_map/ppermute | solution.py:400
  382.8 12.4 %collective-permute-start.71 = (bf16[160,1280]{1,0:T(8,128)(2,1)S(1)}, bf16[160,1280]{1,0:T(8,128)(2,1)S(1)}, u32[]{:S(2)}, u32[]{:S(2)}) collective-permute-start(bf16[160,1280]{1,0:T(8,128)(2,1)S(1)} %collective-permute-done.66.refs_7_.refs_1_), channel_id=1, source_target_pairs={{0,8},{8,16},{16,24},{24,28},{28,20},{20,12},{12,4},{4,0},{1,9},{9... | collective-permute-start | bytes 1228808 | tf_op jit(solution)/shard_map/ppermute | solution.py:457
  383.2 13.5 %collective-permute-start.72 = (bf16[160,1280]{1,0:T(8,128)(2,1)S(1)}, bf16[160,1280]{1,0:T(8,128)(2,1)S(1)}, u32[]{:S(2)}, u32[]{:S(2)}) collective-permute-start(bf16[160,1280]{1,0:T(8,128)(2,1)S(1)} %collective-permute-done.67.refs_8_.refs_2_), channel_id=1, source_target_pairs={{0,4},{8,0},{16,8},{24,16},{28,24},{20,28},{12,20},{4,12},{1,5},{9... | collective-permute-start | bytes 1228808 | tf_op jit(solution)/shard_map/ppermute | solution.py:457
  385.0 14.6 %collective-permute-start.62 = (bf16[80,1280]{1,0:T(8,128)(2,1)S(1)}, bf16[80,1280]{1,0:T(8,128)(2,1)S(1)}, u32[]{:S(2)}, u32[]{:S(2)}) collective-permute-start(bf16[80,1280]{1,0:T(8,128)(2,1)S(1)} %get-tuple-element.235.refs_2_), channel_id=1, source_target_pairs={{0,8},{8,16},{16,24},{24,28},{28,20},{20,12},{12,4},{4,0},{1,9},{9... | collective-permute-start | bytes 614408 | tf_op jit(solution)/shard_map/ppermute | solution.py:451
  385.4 15.0 %collective-permute-start.63 = (bf16[80,1280]{1,0:T(8,128)(2,1)S(1)}, bf16[80,1280]{1,0:T(8,128)(2,1)S(1)}, u32[]{:S(2)}, u32[]{:S(2)}) collective-permute-start(bf16[80,1280]{1,0:T(8,128)(2,1)S(1)} %get-tuple-element.236), channel_id=1, source_target_pairs={{0,4},{8,0},{16,8},{24,16},{28,24},{20,28},{12,20},{4,12},{1,5},{9... | collective-permute-start | bytes 614408 | tf_op jit(solution)/shard_map/ppermute | solution.py:451
  395.2 19.8 %collective-permute-start.41 = (bf16[256,1280]{1,0:T(8,128)(2,1)S(1)}, bf16[256,1280]{1,0:T(8,128)(2,1)S(1)}, u32[]{:S(2)}, u32[]{:S(2)}) collective-permute-start(bf16[256,1280]{1,0:T(8,128)(2,1)S(1)} %pair_sum.12.refs_4_), channel_id=1, source_target_pairs={{0,2},{1,3},{2,0},{3,1},{4,6},{5,7},{6,4},{7,5},{8,10},{9,11},{10,... | collective-permute-start | bytes 1966088 | tf_op jit(solution)/shard_map/ppermute | solution.py:400
  396.7 10.5 %collective-permute-start.73 = (bf16[160,1280]{1,0:T(8,128)(2,1)S(1)}, bf16[160,1280]{1,0:T(8,128)(2,1)}, u32[]{:S(2)}, u32[]{:S(2)}) collective-permute-start(bf16[160,1280]{1,0:T(8,128)(2,1)S(1)} %collective-permute-done.71.refs_7_.refs_3_), channel_id=1, source_target_pairs={{0,8},{8,16},{16,24},{24,28},{28,20},{20,12},{12,4},{4,0},{1,9},{9... | collective-permute-start | bytes 1228808 | tf_op jit(solution)/shard_map/ppermute | solution.py:457
  409.2 19.7 %collective-permute-start.78 = (bf16[160,1280]{1,0:T(8,128)(2,1)}, bf16[160,1280]{1,0:T(8,128)(2,1)}, u32[]{:S(2)}, u32[]{:S(2)}) collective-permute-start(bf16[160,1280]{1,0:T(8,128)(2,1)} %collective-permute-done.73.refs_6_.refs_5_), channel_id=1, source_target_pairs={{0,8},{8,16},{16,24},{24,28},{28,20},{20,12},{12,4},{4,0},{1,9},{9... | collective-permute-start | bytes 1228808 | tf_op jit(solution)/shard_map/ppermute | solution.py:457
  411.5 18.3 %collective-permute-start.79 = (bf16[160,1280]{1,0:T(8,128)(2,1)}, bf16[160,1280]{1,0:T(8,128)(2,1)}, u32[]{:S(2)}, u32[]{:S(2)}) collective-permute-start(bf16[160,1280]{1,0:T(8,128)(2,1)} %collective-permute-done.74.refs_7_.refs_6_), channel_id=1, source_target_pairs={{0,4},{8,0},{16,8},{24,16},{28,24},{20,28},{12,20},{4,12},{1,5},{9... | collective-permute-start | bytes 1228808 | tf_op jit(solution)/shard_map/ppermute | solution.py:457
  412.4 17.4 %collective-permute-start.75 = (bf16[256,1280]{1,0:T(8,128)(2,1)S(1)}, bf16[256,1280]{1,0:T(8,128)(2,1)}, u32[]{:S(2)}, u32[]{:S(2)}) collective-permute-start(bf16[256,1280]{1,0:T(8,128)(2,1)S(1)} %pair_sum.15.refs_6_), channel_id=1, source_target_pairs={{0,2},{1,3},{2,0},{3,1},{4,6},{5,7},{6,4},{7,5},{8,10},{9,11},{10,... | collective-permute-start | bytes 1966088 | tf_op jit(solution)/shard_map/ppermute | solution.py:400
  467.0 10.8 %collective-permute-start.92 = (bf16[80,1280]{1,0:T(8,128)(2,1)S(1)}, bf16[80,1280]{1,0:T(8,128)(2,1)S(1)}, u32[]{:S(2)}, u32[]{:S(2)}) collective-permute-start(bf16[80,1280]{1,0:T(8,128)(2,1)S(1)} %collective-permute-done.91.refs_3_.refs_10_), channel_id=1, source_target_pairs={{0,8},{8,16},{16,24},{24,28},{28,20},{20,12},{12,4},{4,0},{1,9},{9... | collective-permute-start | bytes 614408 | tf_op jit(solution)/shard_map/ppermute | solution.py:457
  477.8 11.9 %collective-permute-start.100 = (bf16[80,1280]{1,0:T(8,128)(2,1)S(1)}, bf16[80,1280]{1,0:T(8,128)(2,1)S(1)}, u32[]{:S(2)}, u32[]{:S(2)}) collective-permute-start(bf16[80,1280]{1,0:T(8,128)(2,1)S(1)} %collective-permute-done.99.refs_6_.refs_13_), channel_id=1, source_target_pairs={{0,4},{8,0},{16,8},{24,16},{28,24},{20,28},{12,20},{4,12},{1,5},{9... | collective-permute-start | bytes 614408 | tf_op jit(solution)/shard_map/ppermute | solution.py:457
  477.8 11.9 %collective-permute-start.93 = (bf16[80,1280]{1,0:T(8,128)(2,1)S(1)}, bf16[80,1280]{1,0:T(8,128)(2,1)S(1)}, u32[]{:S(2)}, u32[]{:S(2)}) collective-permute-start(bf16[80,1280]{1,0:T(8,128)(2,1)S(1)} %collective-permute-done.92.refs_5_.refs_12_), channel_id=1, source_target_pairs={{0,8},{8,16},{16,24},{24,28},{28,20},{20,12},{12,4},{4,0},{1,9},{9... | collective-permute-start | bytes 614408 | tf_op jit(solution)/shard_map/ppermute | solution.py:457
  (170 other events, 1404.0 us)
